TPU v7x, 32 devices: a whole 2x2x4 slice. The times are simulated.
32 devices in a mesh: dom: 8 (over z, y), rep: 4 (over x, core).
Axes of the slice: x: 2, y: 2, z: 4, core: 2. Of those that a mesh axis runs over, the one named last changes fastest.
Arguments:
- feats: bfloat16 [8192, 256], P('dom'), may hold values from -6 to 6
- history: bfloat16 [8192, 256], P('dom'), may hold values from -6 to 6
- adj_inner: bfloat16 [8192, 1024], P('dom'), may hold values from -0.15625 to 0.15625
- adj_halo: bfloat16 [8192, 256], P('dom'), may hold values from -0.15625 to 0.15625
- halo_rows: int32 [64, 32], P('dom'), may hold values from 0 to 1023
- w_self: bfloat16 [256, 256], replicated, may hold values from -0.375 to 0.375
- w_nbr: bfloat16 [256, 256], replicated, may hold values from -0.375 to 0.375
- b_enc: float32 [256], replicated, may hold values from -3 to 3
- edge_owner: int32 [8192, 2], P(('dom', 'rep')), may hold values from 0 to 7, all different within a row; in each aligned block of 256 rows (0 to 255, 256 to 511, ...) at most 128 rows name the same one
- edge_rows: int32 [8192, 2], P(('dom', 'rep')), may hold values from 0 to 1023
- labels: int32 [8192], P(('dom', 'rep')), may hold values 0 or 1
- w_dec1: bfloat16 [256, 256], replicated, may hold values from -0.375 to 0.375
- b_dec1: float32 [256], replicated, may hold values from -3 to 3
- w_dec2: bfloat16 [256], replicated, may hold values from -0.375 to 0.375
Outputs:
- embed: bfloat16 [8192, 256], P('dom')
- grad_embed: float32 [8192, 256], P(('dom', 'rep'))
- grad_dec1: float32 [256, 256], replicated
- grad_bias1: float32 [256], replicated
- grad_dec2: float32 [256], replicated
Inputs may be any that keep to these rules, and one draw needn't show every extreme that they name: `edge_owner`: among the rows of one device, no owner is named by more than 128 endpoints, a bound that some block reaches; the two endpoints of an edge have different owners.
All inputs are finite; a program needn't handle non-finite values. No bound on the sum of `labels` on one device may be relied on, other than what follows from the above.
Results may differ from a plain program's by a relative error of at most 0.0069.
Values may be sent and summed in bfloat16 or wider, within the bound.
No kernel may reach another device: no remote copies, remote signals or barrier semaphores. Data moves between devices by JAX's collectives and lax.ppermute only.
A program may use at most 64 MiB of HBM per device.

v0:
```python
import jax
import jax.numpy as jnp
from jax import lax
from jax.sharding import PartitionSpec as P


def encode_block(rows_x, a_inner, a_halo, all_x, halo, w_self, w_nbr, b_enc):
    agg = (
        jnp.dot(a_inner, all_x, preferred_element_type=jnp.float32)
        + jnp.dot(a_halo, halo, preferred_element_type=jnp.float32)
    ).astype(jnp.bfloat16)
    pre = (
        jnp.dot(rows_x, w_self, preferred_element_type=jnp.float32)
        + jnp.dot(agg, w_nbr, preferred_element_type=jnp.float32)
        + b_enc
    )
    return jnp.maximum(pre, 0.0).astype(jnp.bfloat16)


def decode(head, tail, target, w_dec1, b_dec1, w_dec2):
    zprod = (head.astype(jnp.float32) * tail.astype(jnp.float32)).astype(jnp.bfloat16)
    pre = jnp.dot(zprod, w_dec1, preferred_element_type=jnp.float32) + b_dec1
    sig = jax.nn.sigmoid(pre)
    hidden = (pre * sig).astype(jnp.bfloat16)
    logit = jnp.dot(hidden, w_dec2, preferred_element_type=jnp.float32)
    dlogit = jax.nn.sigmoid(logit) - target
    d_pre = (
        dlogit[:, None] * w_dec2.astype(jnp.float32) * (sig * (1.0 + pre * (1.0 - sig)))
    ).astype(jnp.bfloat16)
    grad_w1 = jnp.dot(zprod.T, d_pre, preferred_element_type=jnp.float32)
    grad_b1 = jnp.sum(d_pre.astype(jnp.float32), axis=0)
    grad_w2 = jnp.sum(hidden.astype(jnp.float32) * dlogit[:, None], axis=0)
    dzval = jnp.dot(d_pre, w_dec1.T, preferred_element_type=jnp.float32)
    return (
        dzval * tail.astype(jnp.float32),
        dzval * head.astype(jnp.float32),
        grad_w1,
        grad_b1,
        grad_w2,
    )


def per_device(
    feats,
    history,
    adj_inner,
    adj_halo,
    halo_rows,
    w_self,
    w_nbr,
    b_enc,
    edge_owner,
    edge_rows,
    labels,
    w_dec1,
    b_dec1,
    w_dec2,
):
    n_dom = lax.axis_size("dom")
    nodes = feats.shape[0]
    width = feats.shape[1]
    halo = lax.all_to_all(
        history[lax.all_to_all(halo_rows, "dom", split_axis=0, concat_axis=0, tiled=True)],
        "dom",
        split_axis=0,
        concat_axis=0,
        tiled=True,
    ).reshape(-1, width)
    embed = encode_block(feats, adj_inner, adj_halo, feats, halo, w_self, w_nbr, b_enc)
    queries = edge_owner.shape[0]
    cap_edge = max(2, 4 * queries // n_dom)
    owners = edge_owner.reshape(-1)
    local = edge_rows.reshape(-1)
    match = (owners[:, None] == jnp.arange(n_dom, dtype=jnp.int32)[None, :]).astype(jnp.int32)
    slots = jnp.sum(jnp.cumsum(match, axis=0) * match, axis=1) - 1
    place = owners * cap_edge + slots
    send_ids = (
        jnp.zeros((n_dom * cap_edge,), jnp.int32).at[place].set(local).reshape(n_dom, cap_edge)
    )
    wanted = lax.all_to_all(send_ids, "dom", split_axis=0, concat_axis=0, tiled=True)
    fetched = lax.all_to_all(embed[wanted], "dom", split_axis=0, concat_axis=0, tiled=True)
    ends = fetched.reshape(-1, width)[place].reshape(queries, 2, width)
    target = labels.astype(jnp.float32)
    g_head, g_tail, gw1, gb1, gw2 = decode(ends[:, 0], ends[:, 1], target, w_dec1, b_dec1, w_dec2)
    grads = jnp.stack([g_head, g_tail], axis=1).reshape(-1, width)
    send_grads = jnp.zeros((n_dom * cap_edge, width), jnp.float32).at[place].set(grads)
    back = lax.all_to_all(
        send_grads.reshape(n_dom, cap_edge, width), "dom", split_axis=0, concat_axis=0, tiled=True
    )
    local_grad = (
        jnp.zeros((nodes, width), jnp.float32).at[wanted.reshape(-1)].add(back.reshape(-1, width))
    )
    grad_embed = lax.psum_scatter(local_grad, "rep", scatter_dimension=0, tiled=True)
    grad_dec1, grad_bias1, grad_dec2 = lax.psum((gw1, gb1, gw2), ("dom", "rep"))
    return (embed, grad_embed, grad_dec1, grad_bias1, grad_dec2)


def solution(mesh):
    placed = (
        P("dom", None),
        P("dom", None),
        P("dom", None),
        P("dom", None),
        P("dom", None),
        P(),
        P(),
        P(),
        P(("dom", "rep"), None),
        P(("dom", "rep"), None),
        P(("dom", "rep")),
        P(),
        P(),
        P(),
    )
    return jax.shard_map(
        per_device,
        mesh=mesh,
        in_specs=placed,
        out_specs=(P("dom", None), P(("dom", "rep"), None), P(), P(), P()),
        check_vma=False,
    )
```

profile of v0, /device:TPU:0, one launch (start us, length us, event | category | flops | bytes accessed | tf_op | source)
XLA Modules:
  0.0 227.5 jit_solution(4002134847820111080)
XLA Ops:
  8.0 7.4 %all-to-all-start = ((s32[8,1,32]{2,1,0:T(1,128)}), s32[8,1,32]{2,1,0:T(1,128)S(1)}, u32[]{:S(2)}, u32[]{:S(2)}) async-start(s32[8,1,32]{2,1,0:T(1,128)} %bitcast.81), calls=%async_computation | async-start | bytes 8192 | tf_op jit(solution)/shard_map/all_to_all | solution.py:63
  16.1 0.8 copy.29
  17.5 1.1 reduce-window.6
  19.1 2.9 %fusion.20 = f32[1024,256]{1,0:T(8,128)} fusion(bf16[1024,1024]{1,0:T(8,128)(2,1)S(1)} %copy-done, bf16[1024,256]{1,0:T(8,128)(2,1)} %param.14), kind=kOutput, calls=%fused_computation.53 | convolution fusion | flops 536870912 | bytes 3670016 | tf_op jit(solution)/shard_map/dot_general | solution.py:9
  22.2 3.0 %scatter_custom_fusion = s32[1024]{0:T(1024)} fusion(s32[512]{0:T(512)S(1)} %bitcast.76, s32[512]{0:T(512)S(1)} %reshape.223, s32[]{:T(128)} %constant.6.clone.1), kind=kCustom, calls=%fused_computation.46 | custom fusion | bytes 4100 | tf_op jit(solution)/shard_map/scatter | solution.py:78
  25.3 6.0 %all-to-all-start.2 = ((s32[8,1,128]{2,1,0:T(1,128)}), s32[8,1,128]{2,1,0:T(1,128)S(1)}, u32[]{:S(2)}, u32[]{:S(2)}) async-start(s32[8,1,128]{2,1,0:T(1,128)} %bitcast.9), calls=%async_computation.2 | async-start | bytes 8192 | tf_op jit(solution)/shard_map/all_to_all | solution.py:80
  31.4 1.8 gather_fusion
  33.2 4.5 %all-to-all-done.2 = s32[8,1,128]{2,1,0:T(1,128)S(1)} async-done(((s32[8,1,128]{2,1,0:T(1,128)}), s32[8,1,128]{2,1,0:T(1,128)S(1)}, u32[]{:S(2)}, u32[]{:S(2)}) %all-to-all-start.2) | async-done | bytes 4128 | tf_op jit(solution)/shard_map/all_to_all | solution.py:80
  37.6 3.4 %all-to-all-start.1 = ((bf16[8,32,256]{2,1,0:T(8,128)(2,1)}), bf16[8,32,256]{2,1,0:T(8,128)(2,1)S(1)}, u32[]{:S(2)}, u32[]{:S(2)}) async-start(bf16[8,32,256]{2,1,0:T(8,128)(2,1)} %bitcast.2), calls=%async_computation.1 | async-start | bytes 262144 | tf_op jit(solution)/shard_map/all_to_all | solution.py:62
  41.0 2.3 %fusion.19 = f32[1024,256]{1,0:T(8,128)} fusion(bf16[1024,256]{1,0:T(8,128)(2,1)} %param.14, bf16[256,256]{1,0:T(8,128)(2,1)S(1)} %copy-done.5), kind=kOutput, calls=%fused_computation.52 | convolution fusion | flops 134217728 | bytes 1703936 | tf_op jit(solution)/shard_map/dot_general | solution.py:13
  43.4 4.9 %all-to-all-done.1 = bf16[8,32,256]{2,1,0:T(8,128)(2,1)S(1)} async-done(((bf16[8,32,256]{2,1,0:T(8,128)(2,1)}), bf16[8,32,256]{2,1,0:T(8,128)(2,1)S(1)}, u32[]{:S(2)}, u32[]{:S(2)}) %all-to-all-start.1) | async-done | bytes 131104 | tf_op jit(solution)/shard_map/all_to_all | solution.py:62
  48.3 2.1 fusion.3
  50.4 4.9 %gather_fusion.1 = bf16[1024,256]{1,0:T(8,128)(2,1)} fusion(bf16[1024,256]{1,0:T(8,128)(2,1)S(1)} %fusion.3, s32[1024]{0:T(1024)S(1)} %fusion.15), kind=kCustom, calls=%fused_computation.1 | custom fusion | bytes 1052672 | tf_op jit(solution)/shard_map/gather | solution.py:81
  55.4 3.5 %all-to-all-start.3 = ((bf16[8,128,256]{2,1,0:T(8,128)(2,1)}), bf16[8,128,256]{2,1,0:T(8,128)(2,1)S(1)}, u32[]{:S(2)}, u32[]{:S(2)}) async-start(bf16[8,128,256]{2,1,0:T(8,128)(2,1)} %bitcast.14), calls=%async_computation.3 | async-start | bytes 1048576 | tf_op jit(solution)/shard_map/all_to_all | solution.py:81
  58.9 11.5 %all-to-all-done.3 = bf16[8,128,256]{2,1,0:T(8,128)(2,1)S(1)} async-done(((bf16[8,128,256]{2,1,0:T(8,128)(2,1)}), bf16[8,128,256]{2,1,0:T(8,128)(2,1)S(1)}, u32[]{:S(2)}, u32[]{:S(2)}) %all-to-all-start.3) | async-done | bytes 524320 | tf_op jit(solution)/shard_map/all_to_all | solution.py:81
  70.4 1.9 gather_fusion.2
  74.6 3.3 %scatter_custom_fusion.1 = f32[1024,256]{1,0:T(8,128)} fusion(s32[512]{0:T(512)S(1)} %bitcast.78, f32[512,256]{1,0:T(8,128)S(1)} %reshape.231, f32[]{:T(128)} %constant.8.clone.1), kind=kCustom, calls=%fused_computation.17 | custom fusion | bytes 1048580 | tf_op jit(solution)/shard_map/scatter | solution.py:86
  77.9 3.7 %all-to-all-start.4 = ((f32[8,128,256]{2,1,0:T(8,128)}), f32[8,128,256]{2,1,0:T(8,128)S(1)}, u32[]{:S(2)}, u32[]{:S(2)}) async-start(f32[8,128,256]{2,1,0:T(8,128)} %bitcast.22), calls=%async_computation.4 | async-start | bytes 2097152 | tf_op jit(solution)/shard_map/all_to_all | solution.py:87
  81.6 0.9 fusion.22
  82.8 23.9 %all-to-all-done.4 = f32[8,128,256]{2,1,0:T(8,128)S(1)} async-done(((f32[8,128,256]{2,1,0:T(8,128)}), f32[8,128,256]{2,1,0:T(8,128)S(1)}, u32[]{:S(2)}, u32[]{:S(2)}) %all-to-all-start.4) | async-done | bytes 1048608 | tf_op jit(solution)/shard_map/all_to_all | solution.py:87
  106.7 7.7 %scatter_custom_fusion.2 = f32[1024,256]{1,0:T(8,128)} fusion(s32[1024]{0:T(1024)S(1)} %bitcast.82, f32[1024,256]{1,0:T(8,128)S(1)} %bitcast.72, f32[]{:T(128)} %constant.8.clone.1), kind=kCustom, calls=%fused_computation.15 | custom fusion | flops 262144 | bytes 1048580 | tf_op jit(solution)/shard_map/scatter-add | solution.py:91
  114.5 37.7 %all-reduce = (f32[256]{0:T(256)}, f32[256]{0:T(256)}) all-reduce(f32[256]{0:T(256)S(1)} %get-tuple-element.7, f32[256]{0:T(256)S(1)} %get-tuple-element.13), channel_id=1, replica_groups=mesh['dom'=8,'rep'=4] {'dom','rep'}, use_global_device_ids=true, to_apply=%region_9.10 | all-reduce | flops 512 | bytes 4096 | tf_op jit(solution)/shard_map/psum | solution.py:94
  152.2 66.2 %all-reduce.3.cloned.1.call-done = f32[256,256]{1,0:T(8,128)} async-done(((f32[256,256]{1,0:T(8,128)}), f32[256,256]{1,0:T(8,128)}) %all-reduce.3.cloned.1.call-update) | async-done | bytes 262160 | tf_op jit(solution)/shard_map/psum | solution.py:94
  218.4 1.7 copy.49
  (61 shorter events, 4.5 us)
Async XLA Ops:
  8.0 11.0 %copy-start = (bf16[1024,1024]{1,0:T(8,128)(2,1)S(1)}, bf16[1024,1024]{1,0:T(8,128)(2,1)}, u32[]{:S(2)}) copy-start(bf16[1024,1024]{1,0:T(8,128)(2,1)} %param.16) | copy-start | bytes 6291460
  8.0 17.2 %all-to-all-start = ((s32[8,1,32]{2,1,0:T(1,128)}), s32[8,1,32]{2,1,0:T(1,128)S(1)}, u32[]{:S(2)}, u32[]{:S(2)}) async-start(s32[8,1,32]{2,1,0:T(1,128)} %bitcast.81), calls=%async_computation | async-start | bytes 8192 | tf_op jit(solution)/shard_map/all_to_all | solution.py:63
  19.0 2.9 %copy-start.7 = (s32[256,2]{0,1:T(2,128)S(1)}, s32[256,2]{0,1:T(2,128)}, u32[]{:S(2)}) copy-start(s32[256,2]{0,1:T(2,128)} %param.23) | copy-start | bytes 6148
  19.1 12.3 %copy-start.2 = (bf16[1024,256]{1,0:T(8,128)(2,1)S(1)}, bf16[1024,256]{1,0:T(8,128)(2,1)}, u32[]{:S(2)}) copy-start(bf16[1024,256]{1,0:T(8,128)(2,1)} %param.15) | copy-start | bytes 1572868
  19.1 22.0 %copy-start.5 = (bf16[256,256]{1,0:T(8,128)(2,1)S(1)}, bf16[256,256]{1,0:T(8,128)(2,1)}, u32[]{:S(2)}) copy-start(bf16[256,256]{1,0:T(8,128)(2,1)} %param.19) | copy-start | bytes 393220
  21.9 26.4 %copy-start.3 = (bf16[1024,256]{1,0:T(8,128)(2,1)S(1)}, bf16[1024,256]{1,0:T(8,128)(2,1)}, u32[]{:S(2)}) copy-start(bf16[1024,256]{1,0:T(8,128)(2,1)} %param.17) | copy-start | bytes 1572868
  21.9 26.4 %copy-start.4 = (bf16[256,256]{1,0:T(8,128)(2,1)S(1)}, bf16[256,256]{1,0:T(8,128)(2,1)}, u32[]{:S(2)}) copy-start(bf16[256,256]{1,0:T(8,128)(2,1)} %param.20) | copy-start | bytes 393220
  25.3 12.4 %all-to-all-start.2 = ((s32[8,1,128]{2,1,0:T(1,128)}), s32[8,1,128]{2,1,0:T(1,128)S(1)}, u32[]{:S(2)}, u32[]{:S(2)}) async-start(s32[8,1,128]{2,1,0:T(1,128)} %bitcast.9), calls=%async_computation.2 | async-start | bytes 8192 | tf_op jit(solution)/shard_map/all_to_all | solution.py:80
  37.6 10.7 %all-to-all-start.1 = ((bf16[8,32,256]{2,1,0:T(8,128)(2,1)}), bf16[8,32,256]{2,1,0:T(8,128)(2,1)S(1)}, u32[]{:S(2)}, u32[]{:S(2)}) async-start(bf16[8,32,256]{2,1,0:T(8,128)(2,1)} %bitcast.2), calls=%async_computation.1 | async-start | bytes 262144 | tf_op jit(solution)/shard_map/all_to_all | solution.py:62
  50.4 5.0 %copy-start.1 = (bf16[1024,256]{1,0:T(8,128)(2,1)}, bf16[1024,256]{1,0:T(8,128)(2,1)S(1)}, u32[]{:S(2)}) copy-start(bf16[1024,256]{1,0:T(8,128)(2,1)S(1)} %fusion.3) | copy-start | bytes 1572868
  50.4 8.5 %copy-start.10 = (bf16[256]{0:T(256)(128)(2,1)S(1)}, bf16[256]{0:T(256)(128)(2,1)}, u32[]{:S(2)}) copy-start(bf16[256]{0:T(256)(128)(2,1)} %param.27) | copy-start | bytes 1540
  55.4 15.0 %all-to-all-start.3 = ((bf16[8,128,256]{2,1,0:T(8,128)(2,1)}), bf16[8,128,256]{2,1,0:T(8,128)(2,1)S(1)}, u32[]{:S(2)}, u32[]{:S(2)}) async-start(bf16[8,128,256]{2,1,0:T(8,128)(2,1)} %bitcast.14), calls=%async_computation.3 | async-start | bytes 1048576 | tf_op jit(solution)/shard_map/all_to_all | solution.py:81
  70.4 2.5 %copy-start.6 = (bf16[256,256]{1,0:T(8,128)(2,1)S(1)}, bf16[256,256]{1,0:T(8,128)(2,1)}, u32[]{:S(2)}) copy-start(bf16[256,256]{1,0:T(8,128)(2,1)} %param.25) | copy-start | bytes 393220
  70.4 2.5 %copy-start.9 = (f32[256]{0:T(256)S(1)}, f32[256]{0:T(256)}, u32[]{:S(2)}) copy-start(f32[256]{0:T(256)} %param.26) | copy-start | bytes 3076
  72.4 1.0 copy-start.8
  77.9 28.8 %all-to-all-start.4 = ((f32[8,128,256]{2,1,0:T(8,128)}), f32[8,128,256]{2,1,0:T(8,128)S(1)}, u32[]{:S(2)}, u32[]{:S(2)}) async-start(f32[8,128,256]{2,1,0:T(8,128)} %bitcast.22), calls=%async_computation.4 | async-start | bytes 2097152 | tf_op jit(solution)/shard_map/all_to_all | solution.py:87
  81.5 136.8 %all-reduce.3.cloned.1.call-start = ((), (), s32[]{:S(2)}) async-start(), calls=%async_computation.7 | async-start | bytes 524288 | tf_op jit(solution)/shard_map/psum | solution.py:94
  82.5 135.8 %reduce-scatter.2.cloned.1.call-start = ((), (), s32[]{:S(2)}) async-start(), calls=%async_computation.6 | async-start | bytes 1310720 | tf_op jit(solution)/shard_map/reduce_scatter | solution.py:93
Sparse Core Ops, SparseCore 0:
  89.3 128.9 all-reduce.2
Sparse Core Ops, SparseCore 1:
  114.5 23.7 reduce-scatter.1
where the time goes:
time: 228 us; the launch traced here: 227 us
  waiting for transfers between devices  111 us (49%)
  blocking collectives  37.7 us (17%)
  starting transfers between devices  24.2 us (11%)
  local copies, waits for them, and re-layouts  19.9 us (9%)
  between operations  15.8 us (7%)
  other arithmetic  10 us (4%)
  matrix products  8.82 us (4%)
    psum x1, waiting for transfers between devices, per_device(): grad_dec1, grad_bias1, grad_dec2 = lax.psum((gw1, gb1, gw2), ('dom', 'rep'))  66.2 us
    psum x1, blocking collectives, per_device(): grad_dec1, grad_bias1, grad_dec2 = lax.psum((gw1, gb1, gw2), ('dom', 'rep'))  37.7 us
    all_to_all x1, waiting for transfers between devices, per_device(): lax.all_to_all(send_grads.reshape(n_dom, cap_edge, width), 'dom', split_a...  23.9 us
    all_to_all x1, waiting for transfers between devices, per_device(): lax.all_to_all(embed[wanted], 'dom', split_axis=0, concat_axis=0, tiled=T...  11.5 us
    scatter-add x1, other arithmetic, per_device(): jnp.zeros((nodes, width), jnp.float32).at[wanted.reshape(-1)]  7.72 us
    all_to_all x1, starting transfers between devices, per_device(): lax.all_to_all(halo_rows, 'dom', split_axis=0, concat_axis=0, tiled=True)  7.42 us
    all_to_all x1, starting transfers between devices, per_device(): lax.all_to_all(send_ids, 'dom', split_axis=0, concat_axis=0, tiled=True)  6 us
    gather x1, local copies, waits for them, and re-layouts, per_device(): embed[wanted]  4.95 us
  transfers between devices with their start and end apart: 7, of which 5 were waited for; matrix products, arithmetic and copies ran while one was open for 10% of the time, Pallas kernels for 0%

commit v1 on v0

v1 whole, which is shorter than its diff:
```python
import functools

import jax
import jax.numpy as jnp
from jax import lax
from jax.experimental import pallas as pl
from jax.experimental.pallas import tpu as pltpu
from jax.sharding import PartitionSpec as P

F32 = jnp.float32
BF16 = jnp.bfloat16
I32 = jnp.int32
VMEM_BYTES = 24 * 1024 * 1024


def iota(shape, dim):
    return lax.broadcasted_iota(I32, shape, dim)


def split_index(index, size):
    if size & (size - 1) == 0:
        return lax.shift_right_logical(index, size.bit_length() - 1), index & (size - 1)
    return lax.div(index, size), lax.rem(index, size)


def dot(a, b, dims=((1,), (0,))):
    return lax.dot_general(a, b, (dims, ((), ())), preferred_element_type=F32)


def exact_dot(a, ids, dims, ids_first):
    high = lax.shift_right_logical(ids, 8).astype(F32).astype(BF16)
    low = (ids & 255).astype(F32).astype(BF16)
    if ids_first:
        return dot(high, a, dims) * 256.0 + dot(low, a, dims)
    return dot(a, high, dims) * 256.0 + dot(a, low, dims)


def ones_where(mask):
    return jnp.where(mask, 1.0, 0.0).astype(BF16)


def as_column(ids, count):
    n, w = ids.shape
    rows = n * count
    source, _ = split_index(iota((rows, n), 0), count)
    picked = exact_dot(ones_where(source == iota((rows, n), 1)), ids, ((1,), (0,)), False)
    _, lane = split_index(iota((rows, w), 0), count)
    return jnp.sum(jnp.where(lane == iota((rows, w), 1), picked, 0.0), axis=1, keepdims=True).astype(I32)


def as_row(ids, count):
    n, w = ids.shape
    rows = n * count
    _, lane = split_index(iota((w, rows), 1), count)
    picked = exact_dot(ones_where(lane == iota((w, rows), 0)), ids, ((1,), (0,)), True)
    source, _ = split_index(iota((n, rows), 1), count)
    return jnp.sum(jnp.where(source == iota((n, rows), 0), picked, 0.0), axis=0, keepdims=True).astype(I32)


def row_to_column(row):
    size = row.shape[1]
    same = iota((size, size), 0) == iota((size, size), 1)
    return jnp.sum(jnp.where(same, row, 0.0), axis=1, keepdims=True)


def request_kernel(cap, owner_ref, local_ref, halo_ref, word_ref, place_ref):
    n = word_ref.shape[0]
    owner = jnp.concatenate([owner_ref[0:1, :], owner_ref[1:2, :]], axis=1)
    local = jnp.concatenate([local_ref[0:1, :], local_ref[1:2, :]], axis=1)
    ends = owner.shape[1]
    match = iota((n, ends), 0) == owner
    upto = ones_where(iota((ends, ends), 0) <= iota((ends, ends), 1))
    count = dot(ones_where(match), upto)
    slot = jnp.sum(jnp.where(match, count, 0.0), axis=0, keepdims=True).astype(I32) - 1
    place_ref[...] = owner * cap + slot
    at_slot = ones_where(iota((cap, ends), 0) == slot)
    wanted = jnp.where(match, local, 0)
    ids = exact_dot(at_slot, wanted, ((1,), (1,)), True).astype(I32)
    word_ref[...] = ids
    halo = halo_ref.shape[1]
    word_ref[:, :halo] = ids[:, :halo] + lax.shift_left(halo_ref[...], 16)


def inner_kernel(feats_ref, adj_ref, w_ref, b_ref, place_ref, label_ref, agg_ref, base_ref, place_col_ref, target_ref):
    feats = feats_ref[...]
    agg_ref[...] = dot(adj_ref[...], feats)
    base_ref[...] = dot(feats, w_ref[...]) + b_ref[...]
    place_col_ref[...] = row_to_column(place_ref[...].astype(F32)).astype(I32)
    target_ref[...] = row_to_column(label_ref[...].astype(F32))


def halo_kernel(cap, word_ref, history_ref, out_ref):
    ids = as_column(lax.shift_right_logical(word_ref[...], 16), cap)
    nodes = history_ref.shape[0]
    out_ref[...] = dot(ones_where(ids == iota((ids.shape[0], nodes), 1)), history_ref[...]).astype(BF16)


def embed_kernel(cap, word_ref, agg_ref, base_ref, halo_ref, adj_ref, w_ref, embed_ref, out_ref):
    agg = (agg_ref[...] + dot(adj_ref[...], halo_ref[...])).astype(BF16)
    embed = jnp.maximum(base_ref[...] + dot(agg, w_ref[...]), 0.0).astype(BF16)
    embed_ref[...] = embed
    ids = as_column(word_ref[...] & 65535, cap)
    out_ref[...] = dot(ones_where(ids == iota((ids.shape[0], embed.shape[0]), 1)), embed).astype(BF16)


def decode_kernel(
    ends_ref, place_ref, place_col_ref, target_ref, w1_ref, b1_ref, w2_ref,
    grads_ref, z_ref, d_pre_ref, aux_ref,
):
    slots = ends_ref.shape[0]
    ends = place_ref.shape[1]
    queries = ends // 2
    rows = dot(ones_where(place_col_ref[...] == iota((ends, slots), 1)), ends_ref[...])
    head, tail = rows[:queries], rows[queries:]
    z = (head * tail).astype(BF16)
    w1 = w1_ref[...]
    pre = dot(z, w1) + b1_ref[...]
    sig = jax.nn.sigmoid(pre)
    hidden = (pre * sig).astype(BF16).astype(F32)
    w2 = w2_ref[...].astype(F32)
    logit = jnp.sum(hidden * w2, axis=1, keepdims=True)
    dlogit = jax.nn.sigmoid(logit) - target_ref[...]
    d_pre = (dlogit * w2 * (sig * (1.0 + pre * (1.0 - sig)))).astype(BF16)
    dz = dot(d_pre, w1, ((1,), (1,)))
    grads = jnp.concatenate([dz * tail, dz * head], axis=0).astype(BF16)
    grads_ref[...] = dot(ones_where(iota((slots, ends), 0) == place_ref[...]), grads).astype(BF16)
    z_ref[...] = z
    d_pre_ref[...] = d_pre
    first = iota(aux_ref.shape, 0)
    bias = jnp.sum(d_pre.astype(F32), axis=0, keepdims=True)
    outer = jnp.sum(hidden * dlogit, axis=0, keepdims=True)
    aux_ref[...] = jnp.where(first == 0, bias, jnp.where(first == 1, outer, 0.0))


def weight_kernel(rep_ref, z_ref, d_pre_ref, aux_ref, keep_ref, send_ref):
    grad = dot(z_ref[...], d_pre_ref[...], ((0,), (0,)))
    half = grad.shape[0] // 2
    odd = (rep_ref[0] & 1) == 1
    low, high = grad[:half], grad[half:]
    keep_ref[:half] = jnp.where(odd, high, low)
    send_ref[:half] = jnp.where(odd, low, high)
    keep_ref[half:] = aux_ref[...]
    send_ref[half:] = aux_ref[...]


def scatter_kernel(cap, blocks, rep_ref, word_ref, grads_ref, keep_ref, send_ref):
    ids = as_row(word_ref[...] & 65535, cap)
    grads = grads_ref[...]
    size = keep_ref.shape[0] // (blocks // 2)
    for j in range(blocks):
        first = (rep_ref[0] ^ j) * size
        sums = dot(ones_where(iota((size, ids.shape[1]), 0) + first == ids), grads)
        out = send_ref if j % 2 else keep_ref
        out[(j // 2) * size:(j // 2 + 1) * size, :] = sums


def call(kernel, outs, *args, scalar=False):
    in_specs = [pl.BlockSpec(memory_space=pltpu.VMEM)] * len(args)
    if scalar:
        in_specs[0] = pl.BlockSpec(memory_space=pltpu.SMEM)
    return pl.pallas_call(
        kernel,
        out_shape=[jax.ShapeDtypeStruct(s, t) for s, t in outs],
        in_specs=in_specs,
        out_specs=[pl.BlockSpec(memory_space=pltpu.VMEM)] * len(outs),
        compiler_params=pltpu.CompilerParams(vmem_limit_bytes=VMEM_BYTES),
    )(*args)


def swap(x, axis, mask):
    return lax.ppermute(x, axis, [(i, i ^ mask) for i in range(lax.axis_size(axis))])


def exchange(x, axis):
    return lax.all_to_all(x, axis, split_axis=0, concat_axis=0, tiled=True)


def per_device(
    feats, history, adj_inner, adj_halo, halo_rows, w_self, w_nbr, b_enc,
    edge_owner, edge_rows, labels, w_dec1, b_dec1, w_dec2,
):
    n_dom = lax.axis_size("dom")
    n_rep = lax.axis_size("rep")
    nodes, width = feats.shape
    queries = edge_owner.shape[0]
    cap_halo = halo_rows.shape[1]
    cap = max(2, 4 * queries // n_dom)
    slots = n_dom * cap
    rep = lax.axis_index("rep").astype(I32).reshape(1)

    word, place = call(
        functools.partial(request_kernel, cap),
        [((n_dom, cap), I32), ((1, 2 * queries), I32)],
        edge_owner.T, edge_rows.T, halo_rows,
    )
    word = exchange(word, "dom")
    agg, base, place_col, target = call(
        inner_kernel,
        [((nodes, width), F32), ((nodes, width), F32), ((2 * queries, 1), I32), ((queries, 1), F32)],
        feats, adj_inner, w_self, b_enc.reshape(1, -1), place, labels.reshape(1, -1),
    )
    (halo,) = call(functools.partial(halo_kernel, cap_halo), [((n_dom * cap_halo, width), BF16)], word, history)
    halo = exchange(halo.reshape(n_dom, cap_halo, width), "dom").reshape(-1, width)
    embed, fetched = call(
        functools.partial(embed_kernel, cap),
        [((nodes, width), BF16), ((slots, width), BF16)],
        word, agg, base, halo, adj_halo, w_nbr,
    )
    fetched = exchange(fetched.reshape(n_dom, cap, width), "dom").reshape(-1, width)
    grads, z, d_pre, aux = call(
        decode_kernel,
        [((slots, width), BF16), ((queries, width), BF16), ((queries, width), BF16), ((8, width), F32)],
        fetched, place, place_col, target, w_dec1, b_dec1.reshape(1, -1), w_dec2.reshape(1, -1),
    )
    back = exchange(grads.reshape(n_dom, cap, width), "dom").reshape(-1, width)

    half = width // 2
    keep, send = call(
        weight_kernel, [((half + 8, width), F32), ((half + 8, width), F32)], rep, z, d_pre, aux, scalar=True
    )
    weights = keep + swap(send, "rep", 1)
    step = 2
    while step < n_rep:
        weights = weights + swap(weights, "rep", step)
        step *= 2
    step = 1
    while step < n_dom:
        weights = weights + swap(weights, "dom", step)
        step *= 2
    others = swap(weights, "rep", 1)

    size = nodes // n_rep
    keep, send = call(
        functools.partial(scatter_kernel, cap, n_rep),
        [((nodes // 2, width), F32), ((nodes // 2, width), F32)],
        rep, word, back, scalar=True,
    )
    sums = keep + swap(send, "rep", 1)
    step = 2
    while step < n_rep:
        blocks = sums.reshape(-1, 2, size, width)
        sums = blocks[:, 0] + swap(blocks[:, 1].astype(BF16), "rep", step).astype(F32)
        step *= 2
    grad_embed = sums.reshape(size, width)

    odd = (rep[0] & 1) == 1
    low = jnp.where(odd, others, weights)
    high = jnp.where(odd, weights, others)
    grad_dec1 = jnp.concatenate([low[:half], high[:half]], axis=0)
    return embed, grad_embed, grad_dec1, low[half], low[half + 1]


def solution(mesh):
    placed = (
        P("dom", None), P("dom", None), P("dom", None), P("dom", None), P("dom", None),
        P(), P(), P(),
        P(("dom", "rep"), None), P(("dom", "rep"), None), P(("dom", "rep")),
        P(), P(), P(),
    )
    return jax.shard_map(
        per_device,
        mesh=mesh,
        in_specs=placed,
        out_specs=(P("dom", None), P(("dom", "rep"), None), P(), P(), P()),
        check_vma=False,
    )
```

time: 228 us -> 93 us (0.41)
  waiting for transfers between devices: 111 us -> 35.8 us
  blocking collectives: 37.7 us -> 13.6 us
  between operations: 15.8 us -> 0.8 us
  local copies, waits for them, and re-layouts: 19.9 us -> 8.6 us
  matrix products: 8.82 us -> 0 us
  Pallas kernels: 0 us -> 8.63 us
  other arithmetic: 10 us -> 1.66 us
    psum x1 -> x0, waiting for transfers between devices: 66.2 us -> none  [per_device(): grad_dec1, grad_bias1, grad_dec2 = lax.psum((gw1, gb1, gw2), ('dom', 'rep'))]
    psum x1 -> x0, blocking collectives: 37.7 us -> none  [per_device(): grad_dec1, grad_bias1, grad_dec2 = lax.psum((gw1, gb1, gw2), ('dom', 'rep'))]
    all_to_all x5 -> x3, waiting for transfers between devices: 44.8 us -> 14.3 us  [exchange(): return lax.all_to_all(x, axis, split_axis=0, concat_axis=0, tiled=True)]
    ppermute x0 -> x8, waiting for transfers between devices: none -> 21.6 us  [swap(): lax.ppermute(x, axis, [(i, i ^ mask) for i in range(lax.axis_size(axis))])]
    all_to_all x0 -> x1, blocking collectives: none -> 13.6 us  [exchange(): return lax.all_to_all(x, axis, split_axis=0, concat_axis=0, tiled=True)]
    all_to_all x5 -> x3, starting transfers between devices: 23.9 us -> 11.5 us  [exchange(): return lax.all_to_all(x, axis, split_axis=0, concat_axis=0, tiled=True)]
    ppermute x0 -> x8, starting transfers between devices: none -> 11.8 us  [swap(): lax.ppermute(x, axis, [(i, i ^ mask) for i in range(lax.axis_size(axis))])]
    dot_general x7 -> x0, matrix products: 8.82 us -> none  [the longest x1 2.86 us: encode_block(): jnp.dot(a_inner, all_x, preferred_element_type=jnp.float32)]
  transfers between devices with their start and end apart: 7 -> 11, of which waited for: 5 -> 9; matrix products, arithmetic and copies ran while one was open for 10% -> 2% of each run, Pallas kernels for 0% -> 2%
where the time goes in v1:
time: 93 us; the launch traced here: 92.3 us
  waiting for transfers between devices  35.8 us (38%)
  starting transfers between devices  23.3 us (25%)
  blocking collectives  13.6 us (15%)
  Pallas kernels  8.63 us (9%)
  local copies, waits for them, and re-layouts  8.6 us (9%)
  other arithmetic  1.66 us (2%)
    ppermute x8, waiting for transfers between devices, swap(): lax.ppermute(x, axis, [(i, i ^ mask) for i in range(lax.axis_size(axis))])  21.6 us
    all_to_all x3, waiting for transfers between devices, exchange(): return lax.all_to_all(x, axis, split_axis=0, concat_axis=0, tiled=True)  14.3 us
    all_to_all x1, blocking collectives, exchange(): return lax.all_to_all(x, axis, split_axis=0, concat_axis=0, tiled=True)  13.6 us
    ppermute x8, starting transfers between devices, swap(): lax.ppermute(x, axis, [(i, i ^ mask) for i in range(lax.axis_size(axis))])  11.8 us
    all_to_all x3, starting transfers between devices, exchange(): return lax.all_to_all(x, axis, split_axis=0, concat_axis=0, tiled=True)  11.5 us
    pallas_call x7, Pallas kernels, call(): pl.pallas_call(kernel, out_shape=[jax.ShapeDtypeStruct(s, t) for s, t in...  8.63 us
    unnamed x28, local copies, waits for them, and re-layouts  8 us
  transfers between devices with their start and end apart: 11, of which 9 were waited for; matrix products, arithmetic and copies ran while one was open for 2% of the time, Pallas kernels for 2%

profile of v1, /device:TPU:0, one launch (start us, length us, event | category | flops | bytes accessed | tf_op | source)
XLA Modules:
  0.0 92.3 jit_solution(3199545843266583836)
XLA Ops:
  3.0 13.6 %all_to_all.26 = s32[8,1,128]{2,1,0:T(1,128)S(1)} all-to-all(s32[8,1,128]{2,1,0:T(1,128)S(1)} %bitcast.35), channel_id=1, replica_groups=mesh['dom'=8,'rep'=4] {'dom'}, dimensions={0} | all-to-all | bytes 8192 | tf_op jit(solution)/shard_map/all_to_all | solution.py:175
  16.6 1.0 %copy-done.1 = bf16[1024,256]{1,0:T(8,128)(2,1)S(1)} copy-done((bf16[1024,256]{1,0:T(8,128)(2,1)S(1)}, bf16[1024,256]{1,0:T(8,128)(2,1)}, u32[]{:S(2)}) %copy-start.1) | copy-done | bytes 524312
  17.6 1.2 %shard_map.175 = bf16[256,256]{1,0:T(8,128)(2,1)} custom-call(s32[8,128]{1,0:T(8,128)S(1)} %bitcast.32, bf16[1024,256]{1,0:T(8,128)(2,1)S(1)} %copy-done.1), custom_call_target="tpu_custom_call" | custom-call | tf_op jit(solution)/shard_map/pallas_call | solution.py:161
  18.8 3.4 %all-to-all-start.1 = ((bf16[8,32,256]{2,1,0:T(8,128)(2,1)}), bf16[8,32,256]{2,1,0:T(8,128)(2,1)S(1)}, u32[]{:S(2)}, u32[]{:S(2)}) async-start(bf16[8,32,256]{2,1,0:T(8,128)(2,1)} %bitcast.7), calls=%async_computation.1 | async-start | bytes 262144 | tf_op jit(solution)/shard_map/all_to_all | solution.py:175
  22.2 1.6 %copy-done = bf16[1024,1024]{1,0:T(8,128)(2,1)S(1)} copy-done((bf16[1024,1024]{1,0:T(8,128)(2,1)S(1)}, bf16[1024,1024]{1,0:T(8,128)(2,1)}, u32[]{:S(2)}) %copy-start) | copy-done | bytes 2097176
  23.8 1.0 %copy-done.2 = bf16[1024,256]{1,0:T(8,128)(2,1)S(1)} copy-done((bf16[1024,256]{1,0:T(8,128)(2,1)S(1)}, bf16[1024,256]{1,0:T(8,128)(2,1)}, u32[]{:S(2)}) %copy-start.2) | copy-done | bytes 524312
  28.0 1.5 %all-to-all-done.1 = bf16[8,32,256]{2,1,0:T(8,128)(2,1)S(1)} async-done(((bf16[8,32,256]{2,1,0:T(8,128)(2,1)}), bf16[8,32,256]{2,1,0:T(8,128)(2,1)S(1)}, u32[]{:S(2)}, u32[]{:S(2)}) %all-to-all-start.1) | async-done | bytes 131104 | tf_op jit(solution)/shard_map/all_to_all | solution.py:175
  29.5 2.6 %shard_map.176 = (bf16[1024,256]{1,0:T(8,128)(2,1)}, bf16[1024,256]{1,0:T(8,128)(2,1)}) custom-call(s32[8,128]{1,0:T(8,128)S(1)} %bitcast.33, f32[1024,256]{1,0:T(8,128)S(1)} %get-tuple-element.23.agg_ref, f32[1024,256]{1,0:T(8,128)S(1)} %get-tuple-element.24.base_ref, bf16[256,256]{1,0:T(8,128)(2,1)S(1)} %bitcast.31, bf16[1024,256]{1,0:T(8,128)(2,1)S(1)} %copy-done.3, ...), custom_call_target="tpu_custom_call" | custom-call | tf_op jit(solution)/shard_map/pallas_call | solution.py:161
  32.0 4.5 %all-to-all-start.2 = ((bf16[8,128,256]{2,1,0:T(8,128)(2,1)}), bf16[8,128,256]{2,1,0:T(8,128)(2,1)S(1)}, u32[]{:S(2)}, u32[]{:S(2)}) async-start(bf16[8,128,256]{2,1,0:T(8,128)(2,1)} %bitcast.10), calls=%async_computation.2 | async-start | bytes 1048576 | tf_op jit(solution)/shard_map/all_to_all | solution.py:175
  36.5 12.8 %all-to-all-done.2 = bf16[8,128,256]{2,1,0:T(8,128)(2,1)S(1)} async-done(((bf16[8,128,256]{2,1,0:T(8,128)(2,1)}), bf16[8,128,256]{2,1,0:T(8,128)(2,1)S(1)}, u32[]{:S(2)}, u32[]{:S(2)}) %all-to-all-start.2) | async-done | bytes 524320 | tf_op jit(solution)/shard_map/all_to_all | solution.py:175
  49.3 2.7 %shard_map.177 = (bf16[1024,256]{1,0:T(8,128)(2,1)}, bf16[256,256]{1,0:T(8,128)(2,1)S(1)}, bf16[256,256]{1,0:T(8,128)(2,1)S(1)}, f32[8,256]{1,0:T(8,128)S(1)}) custom-call(bf16[1024,256]{1,0:T(8,128)(2,1)S(1)} %bitcast.30, s32[1,512]{1,0:T(1,128)S(1)} %get-tuple-element.22.place_ref, s32[512,1]{1,0:T(8,128)S(1)} %get-tuple-element.27.place_col_ref, ...), custom_call_target="tpu_custom_call" | custom-call | tf_op jit(solution)/shard_map/pallas_call | solution.py:161
  52.0 3.7 %all-to-all-start.3 = ((bf16[8,128,256]{2,1,0:T(8,128)(2,1)}), bf16[8,128,256]{2,1,0:T(8,128)(2,1)S(1)}, u32[]{:S(2)}, u32[]{:S(2)}) async-start(bf16[8,128,256]{2,1,0:T(8,128)(2,1)} %bitcast.13), calls=%async_computation.3 | async-start | bytes 1048576 | tf_op jit(solution)/shard_map/all_to_all | solution.py:175
  55.9 1.3 %collective-permute-done.2 = f32[136,256]{1,0:T(8,128)S(1)} collective-permute-done((f32[136,256]{1,0:T(8,128)S(1)}, f32[136,256]{1,0:T(8,128)S(1)}, u32[]{:S(2)}, u32[]{:S(2)}) %collective-permute-start.2) | collective-permute-done | bytes 139296 | tf_op jit(solution)/shard_map/ppermute | solution.py:171
  57.3 1.6 %collective-permute-start.3 = (f32[136,256]{1,0:T(8,128)S(1)}, f32[136,256]{1,0:T(8,128)S(1)}, u32[]{:S(2)}, u32[]{:S(2)}) collective-permute-start(f32[136,256]{1,0:T(8,128)S(1)} %add.23), channel_id=1, source_target_pairs={{0,2},{1,3},{2,0},{3,1},{4,6},{5,7},{6,4},{7,5},{8,10},{9,11},{10,... | collective-permute-start | bytes 417800 | tf_op jit(solution)/shard_map/ppermute | solution.py:171
  58.9 4.2 %collective-permute-done.3 = f32[136,256]{1,0:T(8,128)S(1)} collective-permute-done((f32[136,256]{1,0:T(8,128)S(1)}, f32[136,256]{1,0:T(8,128)S(1)}, u32[]{:S(2)}, u32[]{:S(2)}) %collective-permute-start.3) | collective-permute-done | bytes 139296 | tf_op jit(solution)/shard_map/ppermute | solution.py:171
  63.1 2.1 %collective-permute-start.4 = (f32[136,256]{1,0:T(8,128)S(1)}, f32[136,256]{1,0:T(8,128)S(1)}, u32[]{:S(2)}, u32[]{:S(2)}) collective-permute-start(f32[136,256]{1,0:T(8,128)S(1)} %add.24), channel_id=1, source_target_pairs={{0,4},{4,0},{8,12},{12,8},{16,20},{20,16},{24,28},{28,24},{1,5},{5... | collective-permute-start | bytes 417800 | tf_op jit(solution)/shard_map/ppermute | solution.py:171
  65.2 3.9 %collective-permute-done.4 = f32[136,256]{1,0:T(8,128)S(1)} collective-permute-done((f32[136,256]{1,0:T(8,128)S(1)}, f32[136,256]{1,0:T(8,128)S(1)}, u32[]{:S(2)}, u32[]{:S(2)}) %collective-permute-start.4) | collective-permute-done | bytes 139296 | tf_op jit(solution)/shard_map/ppermute | solution.py:171
  69.1 2.0 %collective-permute-start.5 = (f32[136,256]{1,0:T(8,128)S(1)}, f32[136,256]{1,0:T(8,128)S(1)}, u32[]{:S(2)}, u32[]{:S(2)}) collective-permute-start(f32[136,256]{1,0:T(8,128)S(1)} %add.25), channel_id=1, source_target_pairs={{0,8},{4,12},{8,0},{12,4},{16,24},{20,28},{24,16},{28,20},{1,9},{5... | collective-permute-start | bytes 417800 | tf_op jit(solution)/shard_map/ppermute | solution.py:171
  71.0 3.2 %collective-permute-done.5 = f32[136,256]{1,0:T(8,128)S(1)} collective-permute-done((f32[136,256]{1,0:T(8,128)S(1)}, f32[136,256]{1,0:T(8,128)S(1)}, u32[]{:S(2)}, u32[]{:S(2)}) %collective-permute-start.5) | collective-permute-done | bytes 139296 | tf_op jit(solution)/shard_map/ppermute | solution.py:171
  74.2 3.9 %collective-permute-start.6 = (f32[136,256]{1,0:T(8,128)S(1)}, f32[136,256]{1,0:T(8,128)S(1)}, u32[]{:S(2)}, u32[]{:S(2)}) collective-permute-start(f32[136,256]{1,0:T(8,128)S(1)} %add.26), channel_id=1, source_target_pairs={{0,16},{4,20},{8,24},{12,28},{16,0},{20,4},{24,8},{28,12},{1,17},{... | collective-permute-start | bytes 417800 | tf_op jit(solution)/shard_map/ppermute | solution.py:171
  78.1 4.5 %collective-permute-done.6 = f32[136,256]{1,0:T(8,128)S(1)} collective-permute-done((f32[136,256]{1,0:T(8,128)S(1)}, f32[136,256]{1,0:T(8,128)S(1)}, u32[]{:S(2)}, u32[]{:S(2)}) %collective-permute-start.6) | collective-permute-done | bytes 139296 | tf_op jit(solution)/shard_map/ppermute | solution.py:171
  84.2 1.5 %collective-permute-done = f32[512,256]{1,0:T(8,128)S(1)} collective-permute-done((f32[512,256]{1,0:T(8,128)S(1)}, f32[512,256]{1,0:T(8,128)S(1)}, u32[]{:S(2)}, u32[]{:S(2)}) %collective-permute-start) | collective-permute-done | bytes 524320 | tf_op jit(solution)/shard_map/ppermute | solution.py:171
  85.8 1.6 %collective-permute-start.1 = (bf16[1,256,256]{2,1,0:T(8,128)(2,1)S(1)}, bf16[1,256,256]{2,1,0:T(8,128)(2,1)S(1)}, u32[]{:S(2)}, u32[]{:S(2)}) collective-permute-start(bf16[1,256,256]{2,1,0:T(8,128)(2,1)S(1)} %fusion.2), channel_id=1, source_target_pairs={{0,2},{1,3},{2,0},{3,1},{4,6},{5,7},{6,4},{7,5},{8,10},{9,11},{10,... | collective-permute-start | bytes 393224 | tf_op jit(solution)/shard_map/ppermute | solution.py:171
  88.7 3.0 %collective-permute-done.1 = bf16[1,256,256]{2,1,0:T(8,128)(2,1)S(1)} collective-permute-done((bf16[1,256,256]{2,1,0:T(8,128)(2,1)S(1)}, bf16[1,256,256]{2,1,0:T(8,128)(2,1)S(1)}, u32[]{:S(2)}, u32[]{:S(2)}) %collective-permute-start.1) | collective-permute-done | bytes 131104 | tf_op jit(solution)/shard_map/ppermute | solution.py:171
  (48 shorter events, 9.5 us)
Async XLA Ops:
  0.6 0.7 copy-start.7
  1.3 0.7 copy-start.8
  2.0 0.7 copy-start.9
  16.6 1.0 %copy-start.1 = (bf16[1024,256]{1,0:T(8,128)(2,1)S(1)}, bf16[1024,256]{1,0:T(8,128)(2,1)}, u32[]{:S(2)}) copy-start(bf16[1024,256]{1,0:T(8,128)(2,1)} %history_ref.1) | copy-start | bytes 1572868
  17.6 11.9 %copy-start.3 = (bf16[1024,256]{1,0:T(8,128)(2,1)S(1)}, bf16[1024,256]{1,0:T(8,128)(2,1)}, u32[]{:S(2)}) copy-start(bf16[1024,256]{1,0:T(8,128)(2,1)} %adj_ref.3) | copy-start | bytes 1572868
  17.6 11.9 %copy-start.4 = (bf16[256,256]{1,0:T(8,128)(2,1)S(1)}, bf16[256,256]{1,0:T(8,128)(2,1)}, u32[]{:S(2)}) copy-start(bf16[256,256]{1,0:T(8,128)(2,1)} %w_ref.3) | copy-start | bytes 393220
  18.8 10.7 %all-to-all-start.1 = ((bf16[8,32,256]{2,1,0:T(8,128)(2,1)}), bf16[8,32,256]{2,1,0:T(8,128)(2,1)S(1)}, u32[]{:S(2)}, u32[]{:S(2)}) async-start(bf16[8,32,256]{2,1,0:T(8,128)(2,1)} %bitcast.7), calls=%async_computation.1 | async-start | bytes 262144 | tf_op jit(solution)/shard_map/all_to_all | solution.py:175
  22.2 1.6 %copy-start = (bf16[1024,1024]{1,0:T(8,128)(2,1)S(1)}, bf16[1024,1024]{1,0:T(8,128)(2,1)}, u32[]{:S(2)}) copy-start(bf16[1024,1024]{1,0:T(8,128)(2,1)} %adj_ref.2) | copy-start | bytes 6291460
  23.8 1.0 %copy-start.2 = (bf16[1024,256]{1,0:T(8,128)(2,1)S(1)}, bf16[1024,256]{1,0:T(8,128)(2,1)}, u32[]{:S(2)}) copy-start(bf16[1024,256]{1,0:T(8,128)(2,1)} %feats_ref.1) | copy-start | bytes 1572868
  24.8 0.9 copy-start.6
  25.7 0.7 copy-start.10
  27.9 8.6 %copy-start.13 = (bf16[256]{0:T(256)(128)(2,1)S(1)}, bf16[256]{0:T(256)(128)(2,1)}, u32[]{:S(2)}) copy-start(bf16[256]{0:T(256)(128)(2,1)} %param.27) | copy-start | bytes 1540
  28.0 21.3 %copy-start.5 = (bf16[256,256]{1,0:T(8,128)(2,1)S(1)}, bf16[256,256]{1,0:T(8,128)(2,1)}, u32[]{:S(2)}) copy-start(bf16[256,256]{1,0:T(8,128)(2,1)} %w1_ref.1) | copy-start | bytes 393220
  28.0 21.3 %copy-start.12 = (f32[256]{0:T(256)S(1)}, f32[256]{0:T(256)}, u32[]{:S(2)}) copy-start(f32[256]{0:T(256)} %param.26) | copy-start | bytes 3076
  32.0 17.3 %all-to-all-start.2 = ((bf16[8,128,256]{2,1,0:T(8,128)(2,1)}), bf16[8,128,256]{2,1,0:T(8,128)(2,1)S(1)}, u32[]{:S(2)}, u32[]{:S(2)}) async-start(bf16[8,128,256]{2,1,0:T(8,128)(2,1)} %bitcast.10), calls=%async_computation.2 | async-start | bytes 1048576 | tf_op jit(solution)/shard_map/all_to_all | solution.py:175
  52.0 30.8 %all-to-all-start.3 = ((bf16[8,128,256]{2,1,0:T(8,128)(2,1)}), bf16[8,128,256]{2,1,0:T(8,128)(2,1)S(1)}, u32[]{:S(2)}, u32[]{:S(2)}) async-start(bf16[8,128,256]{2,1,0:T(8,128)(2,1)} %bitcast.13), calls=%async_computation.3 | async-start | bytes 1048576 | tf_op jit(solution)/shard_map/all_to_all | solution.py:175
  55.8 1.4 %collective-permute-start.2 = (f32[136,256]{1,0:T(8,128)S(1)}, f32[136,256]{1,0:T(8,128)S(1)}, u32[]{:S(2)}, u32[]{:S(2)}) collective-permute-start(f32[136,256]{1,0:T(8,128)S(1)} %get-tuple-element.36), channel_id=1, source_target_pairs={{0,1},{1,0},{2,3},{3,2},{4,5},{5,4},{6,7},{7,6},{8,9},{9,8},{10,11... | collective-permute-start | bytes 417800 | tf_op jit(solution)/shard_map/ppermute | solution.py:171
  57.3 5.8 %collective-permute-start.3 = (f32[136,256]{1,0:T(8,128)S(1)}, f32[136,256]{1,0:T(8,128)S(1)}, u32[]{:S(2)}, u32[]{:S(2)}) collective-permute-start(f32[136,256]{1,0:T(8,128)S(1)} %add.23), channel_id=1, source_target_pairs={{0,2},{1,3},{2,0},{3,1},{4,6},{5,7},{6,4},{7,5},{8,10},{9,11},{10,... | collective-permute-start | bytes 417800 | tf_op jit(solution)/shard_map/ppermute | solution.py:171
  63.1 5.9 %collective-permute-start.4 = (f32[136,256]{1,0:T(8,128)S(1)}, f32[136,256]{1,0:T(8,128)S(1)}, u32[]{:S(2)}, u32[]{:S(2)}) collective-permute-start(f32[136,256]{1,0:T(8,128)S(1)} %add.24), channel_id=1, source_target_pairs={{0,4},{4,0},{8,12},{12,8},{16,20},{20,16},{24,28},{28,24},{1,5},{5... | collective-permute-start | bytes 417800 | tf_op jit(solution)/shard_map/ppermute | solution.py:171
  69.1 5.1 %collective-permute-start.5 = (f32[136,256]{1,0:T(8,128)S(1)}, f32[136,256]{1,0:T(8,128)S(1)}, u32[]{:S(2)}, u32[]{:S(2)}) collective-permute-start(f32[136,256]{1,0:T(8,128)S(1)} %add.25), channel_id=1, source_target_pairs={{0,8},{4,12},{8,0},{12,4},{16,24},{20,28},{24,16},{28,20},{1,9},{5... | collective-permute-start | bytes 417800 | tf_op jit(solution)/shard_map/ppermute | solution.py:171
  74.2 8.4 %collective-permute-start.6 = (f32[136,256]{1,0:T(8,128)S(1)}, f32[136,256]{1,0:T(8,128)S(1)}, u32[]{:S(2)}, u32[]{:S(2)}) collective-permute-start(f32[136,256]{1,0:T(8,128)S(1)} %add.26), channel_id=1, source_target_pairs={{0,16},{4,20},{8,24},{12,28},{16,0},{20,4},{24,8},{28,12},{1,17},{... | collective-permute-start | bytes 417800 | tf_op jit(solution)/shard_map/ppermute | solution.py:171
  82.6 1.5 %collective-permute-start.7 = (f32[136,256]{1,0:T(8,128)S(1)}, f32[136,256]{1,0:T(8,128)S(1)}, u32[]{:S(2)}, u32[]{:S(2)}) collective-permute-start(f32[136,256]{1,0:T(8,128)S(1)} %add.27), channel_id=1, source_target_pairs={{0,1},{1,0},{2,3},{3,2},{4,5},{5,4},{6,7},{7,6},{8,9},{9,8},{10,11... | collective-permute-start | bytes 417800 | tf_op jit(solution)/shard_map/ppermute | solution.py:171
  83.6 2.1 %collective-permute-start = (f32[512,256]{1,0:T(8,128)S(1)}, f32[512,256]{1,0:T(8,128)S(1)}, u32[]{:S(2)}, u32[]{:S(2)}) collective-permute-start(f32[512,256]{1,0:T(8,128)S(1)} %get-tuple-element.31), channel_id=1, source_target_pairs={{0,1},{1,0},{2,3},{3,2},{4,5},{5,4},{6,7},{7,6},{8,9},{9,8},{10,11... | collective-permute-start | bytes 1572872 | tf_op jit(solution)/shard_map/ppermute | solution.py:171
  85.8 5.8 %collective-permute-start.1 = (bf16[1,256,256]{2,1,0:T(8,128)(2,1)S(1)}, bf16[1,256,256]{2,1,0:T(8,128)(2,1)S(1)}, u32[]{:S(2)}, u32[]{:S(2)}) collective-permute-start(bf16[1,256,256]{2,1,0:T(8,128)(2,1)S(1)} %fusion.2), channel_id=1, source_target_pairs={{0,2},{1,3},{2,0},{3,1},{4,6},{5,7},{6,4},{7,5},{8,10},{9,11},{10,... | collective-permute-start | bytes 393224 | tf_op jit(solution)/shard_map/ppermute | solution.py:171
  (1 other events, 0.7 us)

commit v2 on v1

v2 whole, which is shorter than its diff:
```python
import functools

import jax
import jax.numpy as jnp
from jax import lax
from jax.experimental import pallas as pl
from jax.experimental.pallas import tpu as pltpu
from jax.sharding import PartitionSpec as P

F32 = jnp.float32
BF16 = jnp.bfloat16
I32 = jnp.int32
VMEM_BYTES = 24 * 1024 * 1024
CHUNKS = 4


def iota(shape, dim):
    return lax.broadcasted_iota(I32, shape, dim)


def split_index(index, size):
    if size & (size - 1) == 0:
        return lax.shift_right_logical(index, size.bit_length() - 1), index & (size - 1)
    return lax.div(index, size), lax.rem(index, size)


def dot(a, b, dims=((1,), (0,))):
    return lax.dot_general(a, b, (dims, ((), ())), preferred_element_type=F32)


def exact_dot(a, ids, dims, ids_first):
    high = lax.shift_right_logical(ids, 8).astype(F32).astype(BF16)
    low = (ids & 255).astype(F32).astype(BF16)
    if ids_first:
        return dot(high, a, dims) * 256.0 + dot(low, a, dims)
    return dot(a, high, dims) * 256.0 + dot(a, low, dims)


def ones_where(mask):
    return jnp.where(mask, 1.0, 0.0).astype(BF16)


def as_column(ids, count):
    n, w = ids.shape
    rows = n * count
    source, _ = split_index(iota((rows, n), 0), count)
    picked = exact_dot(ones_where(source == iota((rows, n), 1)), ids, ((1,), (0,)), False)
    _, lane = split_index(iota((rows, w), 0), count)
    return jnp.sum(jnp.where(lane == iota((rows, w), 1), picked, 0.0), axis=1, keepdims=True).astype(I32)


def as_row(ids, count):
    n, w = ids.shape
    rows = n * count
    _, lane = split_index(iota((w, rows), 1), count)
    picked = exact_dot(ones_where(lane == iota((w, rows), 0)), ids, ((1,), (0,)), True)
    source, _ = split_index(iota((n, rows), 1), count)
    return jnp.sum(jnp.where(source == iota((n, rows), 0), picked, 0.0), axis=0, keepdims=True).astype(I32)


def row_to_column(row):
    size = row.shape[1]
    same = iota((size, size), 0) == iota((size, size), 1)
    return jnp.sum(jnp.where(same, row, 0.0), axis=1, keepdims=True)


def loads(sources, targets, sem):
    copies = [pltpu.make_async_copy(src, dst, sem.at[i]) for i, (src, dst) in enumerate(zip(sources, targets))]
    for copy in copies:
        copy.start()
    return copies


def wait(copies):
    for copy in copies:
        copy.wait()


def request_kernel(cap, owner_hbm, local_hbm, halo_hbm, word_ref, place_ref, owner_ref, local_ref, halo_ref, sem):
    wait(loads((owner_hbm, local_hbm, halo_hbm), (owner_ref, local_ref, halo_ref), sem))
    n = word_ref.shape[0]
    owner = jnp.concatenate([owner_ref[0:1, :], owner_ref[1:2, :]], axis=1)
    local = jnp.concatenate([local_ref[0:1, :], local_ref[1:2, :]], axis=1)
    ends = owner.shape[1]
    match = iota((n, ends), 0) == owner
    upto = ones_where(iota((ends, ends), 0) <= iota((ends, ends), 1))
    count = dot(ones_where(match), upto)
    slot = jnp.sum(jnp.where(match, count, 0.0), axis=0, keepdims=True).astype(I32) - 1
    place_ref[...] = owner * cap + slot
    at_slot = ones_where(iota((cap, ends), 0) == slot)
    wanted = jnp.where(match, local, 0)
    ids = exact_dot(at_slot, wanted, ((1,), (1,)), True).astype(I32)
    word_ref[...] = ids
    halo = halo_ref.shape[1]
    word_ref[:, :halo] = ids[:, :halo] + lax.shift_left(halo_ref[...], 16)


def store(value, buffer, out_ref, sem, chunks):
    rows = out_ref.shape[0] // chunks
    copies = []
    for j in range(chunks):
        at = pl.ds(j * rows, rows)
        buffer[at, :] = value(j * rows, rows)
        copy = pltpu.make_async_copy(buffer.at[at, :], out_ref.at[at, :], sem.at[j])
        copy.start()
        copies.append(copy)
    return copies


def load_kernel(history_hbm, history_ref, sem):
    wait(loads((history_hbm,), (history_ref,), sem))


def inner_kernel(
    cap, word_ref, feats_hbm, inner_hbm, self_hbm, b_hbm, halo_hbm, nbr_hbm,
    ids_ref, agg_ref, base_ref, halo_ref, nbr_ref, feats_ref, inner_ref, self_ref, b_ref, sem,
):
    copies = loads(
        (feats_hbm, inner_hbm, self_hbm, b_hbm, halo_hbm, nbr_hbm),
        (feats_ref, inner_ref, self_ref, b_ref, halo_ref, nbr_ref), sem,
    )
    ids_ref[...] = as_column(word_ref[...] & 65535, cap)
    wait(copies)
    feats = feats_ref[...]
    agg_ref[...] = dot(inner_ref[...], feats)
    base_ref[...] = dot(feats, self_ref[...]) + b_ref[...]


def edge_mask_kernel(
    place_ref, label_hbm, w1_hbm, b1_hbm, w2_hbm,
    gather_ref, scatter_ref, target_ref, w1_ref, b1_ref, w2_ref, label_ref, sem,
):
    copies = loads((label_hbm, w1_hbm, b1_hbm, w2_hbm), (label_ref, w1_ref, b1_ref, w2_ref), sem)
    place = place_ref[...]
    column = row_to_column(place.astype(F32)).astype(I32)
    gather_ref[...] = ones_where(column == iota(gather_ref.shape, 1))
    scatter_ref[...] = ones_where(iota(scatter_ref.shape, 0) == place)
    wait(copies)
    target_ref[...] = row_to_column(label_ref[...].astype(F32))


def sum_mask_kernel(cap, blocks, rep_ref, word_ref, mask_ref):
    ids = as_row(word_ref[...] & 65535, cap)
    size = mask_ref.shape[0] // blocks
    for j in range(blocks):
        node = iota((size, ids.shape[1]), 0) + (rep_ref[0] ^ j) * size
        mask_ref[j * size:(j + 1) * size, :] = ones_where(node == ids)


def halo_kernel(cap, word_ref, history_ref, out_ref):
    ids = as_column(lax.shift_right_logical(word_ref[...], 16), cap)
    nodes = history_ref.shape[0]
    out_ref[...] = dot(ones_where(ids == iota((ids.shape[0], nodes), 1)), history_ref[...]).astype(BF16)


def embed_kernel(ids_ref, agg_ref, base_ref, halo_ref, adj_ref, w_ref, embed_hbm, out_hbm, embed_ref, out_ref, embed_sem, out_sem):
    agg = (agg_ref[...] + dot(adj_ref[...], halo_ref[...])).astype(BF16)
    embed = jnp.maximum(base_ref[...] + dot(agg, w_ref[...]), 0.0).astype(BF16)
    copies = store(lambda at, size: embed[at:at + size], embed_ref, embed_hbm, embed_sem, 1)

    def fetched(at, size):
        mask = ones_where(ids_ref[at:at + size, :] == iota((size, embed.shape[0]), 1))
        return dot(mask, embed).astype(BF16)

    copies += store(fetched, out_ref, out_hbm, out_sem, CHUNKS)
    wait(copies)


def decode_kernel(
    rep_ref, ends_ref, gather_ref, target_ref, w1_ref, b1_ref, w2_ref, rows_ref, d_pre_ref, keep_ref, send_ref
):
    queries = d_pre_ref.shape[0]
    rows = dot(gather_ref[...], ends_ref[...])
    rows_ref[...] = rows.astype(BF16)
    z = (rows[:queries] * rows[queries:]).astype(BF16)
    pre = dot(z, w1_ref[...]) + b1_ref[...]
    sig = jax.nn.sigmoid(pre)
    hidden = (pre * sig).astype(BF16).astype(F32)
    w2 = w2_ref[...].astype(F32)
    logit = jnp.sum(hidden * w2, axis=1, keepdims=True)
    dlogit = jax.nn.sigmoid(logit) - target_ref[...]
    d_pre = (dlogit * w2 * (sig * (1.0 + pre * (1.0 - sig)))).astype(BF16)
    d_pre_ref[...] = d_pre
    grad = dot(z, d_pre, ((0,), (0,)))
    half = grad.shape[0] // 2
    odd = (rep_ref[0] & 1) == 1
    low, high = grad[:half], grad[half:]
    keep_ref[:half] = jnp.where(odd, high, low)
    send_ref[:half] = jnp.where(odd, low, high)
    bias = jnp.sum(d_pre.astype(F32), axis=0, keepdims=True)
    outer = jnp.sum(hidden * dlogit, axis=0, keepdims=True)
    first = iota((keep_ref.shape[0] - half, keep_ref.shape[1]), 0)
    aux = jnp.where(first == 0, bias, jnp.where(first == 1, outer, 0.0))
    keep_ref[half:] = aux
    send_ref[half:] = aux


def grads_kernel(rows_ref, d_pre_ref, w1_ref, scatter_ref, grads_hbm, grads_ref, sem):
    queries = d_pre_ref.shape[0]
    dz = dot(d_pre_ref[...], w1_ref[...], ((1,), (1,)))
    head, tail = rows_ref[:queries, :].astype(F32), rows_ref[queries:, :].astype(F32)
    grads = jnp.concatenate([dz * tail, dz * head], axis=0).astype(BF16)
    wait(store(lambda at, size: dot(scatter_ref[at:at + size, :], grads).astype(BF16), grads_ref, grads_hbm, sem, CHUNKS))


def join_kernel(rep_ref, mine_ref, other_ref, grad_ref, bias_ref, outer_ref):
    half = grad_ref.shape[0] // 2
    odd = (rep_ref[0] & 1) == 1
    mine, other = mine_ref[...], other_ref[...]
    low = jnp.where(odd, other, mine)
    grad_ref[:half] = low[:half]
    grad_ref[half:] = jnp.where(odd, mine, other)[:half]
    bias_ref[...] = low[half:half + 1]
    outer_ref[...] = low[half + 1:half + 2]


def scatter_kernel(size, mask_ref, grads_ref, keep_ref, send_ref):
    grads = grads_ref[...]
    for j in range(mask_ref.shape[0] // size):
        sums = dot(mask_ref[j * size:(j + 1) * size, :], grads)
        out = send_ref if j % 2 else keep_ref
        out[(j // 2) * size:(j // 2 + 1) * size, :] = sums


def call(kernel, outs, *args, scalar=False, hbm_in=(), hbm_out=(), far_out=(), scratch=()):
    far_out = tuple(far_out) + tuple(hbm_out)
    space = pl.BlockSpec(memory_space=pltpu.VMEM)
    far = pl.BlockSpec(memory_space=pltpu.HBM)
    in_specs = [far if i in hbm_in else space for i in range(len(args))]
    if scalar:
        in_specs[0] = pl.BlockSpec(memory_space=pltpu.SMEM)
    args = [pltpu.with_memory_space_constraint(x, pltpu.HBM) if i in hbm_in else x for i, x in enumerate(args)]
    return pl.pallas_call(
        kernel,
        out_shape=[(pltpu.HBM if i in far_out else pltpu.VMEM)(s, t) for i, (s, t) in enumerate(outs)],
        in_specs=in_specs,
        out_specs=[far if i in hbm_out else space for i in range(len(outs))],
        scratch_shapes=list(scratch),
        compiler_params=pltpu.CompilerParams(vmem_limit_bytes=VMEM_BYTES),
    )(*args)


def swap(x, axis, mask):
    return lax.ppermute(x, axis, [(i, i ^ mask) for i in range(lax.axis_size(axis))])


def reduce_pairs(x, axis, mask):
    mine = x.astype(BF16)
    return mine.astype(F32) + swap(mine, axis, mask).astype(F32)


def reduce_fours(x, axis, mask):
    mine = x.astype(BF16)
    first, second, third = (swap(mine, axis, mask * k).astype(F32) for k in (1, 2, 3))
    return (mine.astype(F32) + first) + (second + third)


def exchange(x, axis):
    return lax.all_to_all(x, axis, split_axis=0, concat_axis=0, tiled=True)


def per_device(
    feats, history, adj_inner, adj_halo, halo_rows, w_self, w_nbr, b_enc,
    edge_owner, edge_rows, labels, w_dec1, b_dec1, w_dec2,
):
    n_dom = lax.axis_size("dom")
    n_rep = lax.axis_size("rep")
    nodes, width = feats.shape
    queries = edge_owner.shape[0]
    cap_halo = halo_rows.shape[1]
    cap = max(2, 4 * queries // n_dom)
    slots = n_dom * cap
    rep = lax.axis_index("rep").astype(I32).reshape(1)

    ends = 2 * queries
    word, place = call(
        functools.partial(request_kernel, cap),
        [((n_dom, cap), I32), ((1, ends), I32)],
        edge_owner.T, edge_rows.T, halo_rows,
        far_out=(0,),
        hbm_in=(0, 1, 2),
        scratch=(
            pltpu.VMEM((2, queries), I32), pltpu.VMEM((2, queries), I32), pltpu.VMEM(halo_rows.shape, I32),
            pltpu.SemaphoreType.DMA((3,)),
        ),
    )
    word = exchange(word, "dom")
    (history,) = call(
        load_kernel, [(history.shape, BF16)], history, hbm_in=(0,), scratch=(pltpu.SemaphoreType.DMA((1,)),)
    )
    (halo,) = call(
        functools.partial(halo_kernel, cap_halo), [((n_dom * cap_halo, width), BF16)], word, history, far_out=(0,)
    )
    halo = exchange(halo.reshape(n_dom, cap_halo, width), "dom").reshape(-1, width)
    fetch, agg, base, adj_halo, w_nbr = call(
        functools.partial(inner_kernel, cap),
        [
            ((slots, 1), I32), ((nodes, width), F32), ((nodes, width), F32),
            (adj_halo.shape, BF16), (w_nbr.shape, BF16),
        ],
        word, feats, adj_inner, w_self, b_enc.reshape(1, -1), adj_halo, w_nbr,
        hbm_in=(1, 2, 3, 4, 5, 6),
        scratch=(
            pltpu.VMEM(feats.shape, BF16), pltpu.VMEM(adj_inner.shape, BF16), pltpu.VMEM(w_self.shape, BF16),
            pltpu.VMEM((1, width), F32), pltpu.SemaphoreType.DMA((6,)),
        ),
    )
    embed, fetched = call(
        embed_kernel,
        [((nodes, width), BF16), ((slots, width), BF16)],
        fetch, agg, base, halo, adj_halo, w_nbr,
        hbm_out=(0, 1),
        scratch=(
            pltpu.VMEM((nodes, width), BF16), pltpu.VMEM((slots, width), BF16),
            pltpu.SemaphoreType.DMA((1,)), pltpu.SemaphoreType.DMA((CHUNKS,)),
        ),
    )
    fetched = exchange(fetched.reshape(n_dom, cap, width), "dom").reshape(-1, width)
    gather, scatter, target, w1, b1, w2 = call(
        edge_mask_kernel,
        [
            ((ends, slots), BF16), ((slots, ends), BF16), ((queries, 1), F32),
            (w_dec1.shape, BF16), ((1, width), F32), ((1, width), BF16),
        ],
        place, labels.reshape(1, -1), w_dec1, b_dec1.reshape(1, -1), w_dec2.reshape(1, -1),
        hbm_in=(1, 2, 3, 4),
        scratch=(pltpu.VMEM((1, queries), I32), pltpu.SemaphoreType.DMA((4,))),
    )
    half = width // 2
    rows, d_pre, keep, send = call(
        decode_kernel,
        [((ends, width), BF16), ((queries, width), BF16), ((half + 8, width), F32), ((half + 8, width), F32)],
        rep, fetched, gather, target, w1, b1, w2, scalar=True,
    )
    weights = keep + swap(send, "rep", 1)
    step = 2
    while step < n_rep:
        weights = reduce_pairs(weights, "rep", step)
        step *= 2
    step = 1
    while 4 * step <= n_dom // 2:
        weights = reduce_fours(weights, "dom", step)
        step *= 4
    (grads,) = call(
        grads_kernel,
        [((slots, width), BF16)],
        rows, d_pre, w1, scatter,
        hbm_out=(0,),
        scratch=(pltpu.VMEM((slots, width), BF16), pltpu.SemaphoreType.DMA((CHUNKS,))),
    )
    back = exchange(grads.reshape(n_dom, cap, width), "dom").reshape(-1, width)

    back, weights = lax.optimization_barrier((back, weights))
    size = nodes // n_rep
    (mask,) = call(
        functools.partial(sum_mask_kernel, cap, n_rep), [((nodes, slots), BF16)], rep, word, scalar=True
    )
    keep, send = call(
        functools.partial(scatter_kernel, size),
        [((nodes // 2, width), F32), ((nodes // 2, width), F32)],
        mask, back,
    )
    sums = keep + swap(send, "rep", 1)
    rep_step = 2
    while rep_step < n_rep:
        blocks = sums.reshape(-1, 2, size, width)
        away = swap(blocks[:, 1].astype(BF16), "rep", rep_step)
        if step < n_dom:
            mine = weights.astype(BF16)
            others = swap(mine, "dom", step)
            others, away = lax.optimization_barrier((others, away))
            weights = mine.astype(F32) + others.astype(F32)
            step *= 2
        sums = blocks[:, 0] + away.astype(F32)
        rep_step *= 2
    grad_embed = sums.reshape(size, width)
    while step < n_dom:
        weights = reduce_pairs(weights, "dom", step)
        step *= 2

    others = swap(weights, "rep", 1)
    grad_dec1, grad_bias1, grad_dec2 = call(
        join_kernel,
        [((width, width), F32), ((1, width), F32), ((1, width), F32)],
        rep, weights, others, scalar=True, far_out=(0, 1, 2),
    )
    return embed, grad_embed, grad_dec1, grad_bias1[0], grad_dec2[0]


def solution(mesh):
    placed = (
        P("dom", None), P("dom", None), P("dom", None), P("dom", None), P("dom", None),
        P(), P(), P(),
        P(("dom", "rep"), None), P(("dom", "rep"), None), P(("dom", "rep")),
        P(), P(), P(),
    )
    return jax.shard_map(
        per_device,
        mesh=mesh,
        in_specs=placed,
        out_specs=(P("dom", None), P(("dom", "rep"), None), P(), P(), P()),
        check_vma=False,
    )
```

time: 93 us -> 80.1 us (0.86)
  blocking collectives: 13.6 us -> 0 us
  local copies, waits for them, and re-layouts: 8.6 us -> 0.59 us
  Pallas kernels: 8.63 us -> 14.2 us
  starting transfers between devices: 23.3 us -> 27.3 us
    all_to_all x1 -> x0, blocking collectives: 13.6 us -> none  [exchange(): return lax.all_to_all(x, axis, split_axis=0, concat_axis=0, tiled=True)]
    unnamed x28 -> x2, local copies, waits for them, and re-layouts: 8 us -> 0.01 us
    ppermute x8 -> x9, waiting for transfers between devices: 21.6 us -> 14.6 us  [swap(): lax.ppermute(x, axis, [(i, i ^ mask) for i in range(lax.axis_size(axis))])]
    all_to_all x3 -> x4, waiting for transfers between devices: 14.3 us -> 21.2 us  [exchange(): return lax.all_to_all(x, axis, split_axis=0, concat_axis=0, tiled=True)]
    all_to_all x3 -> x4, starting transfers between devices: 11.5 us -> 17.8 us  [exchange(): return lax.all_to_all(x, axis, split_axis=0, concat_axis=0, tiled=True)]
    pallas_call x7 -> x11, Pallas kernels: 8.63 us -> 14.2 us  [call(): pl.pallas_call(kernel, out_shape=[(pltpu.HBM if i in far_out else pltpu.V...]
    ppermute x8 -> x9, starting transfers between devices: 11.8 us -> 9.47 us  [swap(): lax.ppermute(x, axis, [(i, i ^ mask) for i in range(lax.axis_size(axis))])]
  transfers between devices with their start and end apart: 11 -> 13, of which waited for: 9 -> 11; matrix products, arithmetic and copies ran while one was open for 2% -> 2% of each run, Pallas kernels for 2% -> 9%
where the time goes in v2:
time: 80.1 us; the launch traced here: 79.5 us
  waiting for transfers between devices  35.7 us (45%)
  starting transfers between devices  27.3 us (34%)
  Pallas kernels  14.2 us (18%)
  other arithmetic  0.89 us (1%)
    all_to_all x4, waiting for transfers between devices, exchange(): return lax.all_to_all(x, axis, split_axis=0, concat_axis=0, tiled=True)  21.2 us
    all_to_all x4, starting transfers between devices, exchange(): return lax.all_to_all(x, axis, split_axis=0, concat_axis=0, tiled=True)  17.8 us
    ppermute x9, waiting for transfers between devices, swap(): lax.ppermute(x, axis, [(i, i ^ mask) for i in range(lax.axis_size(axis))])  14.6 us
    pallas_call x11, Pallas kernels, call(): pl.pallas_call(kernel, out_shape=[(pltpu.HBM if i in far_out else pltpu.V...  14.2 us
    ppermute x9, starting transfers between devices, swap(): lax.ppermute(x, axis, [(i, i ^ mask) for i in range(lax.axis_size(axis))])  9.47 us
  transfers between devices with their start and end apart: 13, of which 11 were waited for; matrix products, arithmetic and copies ran while one was open for 2% of the time, Pallas kernels for 9%

profile of v2, /device:TPU:0, one launch (start us, length us, event | category | flops | bytes accessed | tf_op | source)
XLA Modules:
  0.0 79.5 jit_solution(4448587747911164352)
XLA Ops:
  0.6 1.7 %shard_map.173 = (s32[8,128]{1,0:T(8,128)}, s32[1,512]{1,0:T(1,128)S(1)}) custom-call(s32[2,256]{1,0:T(2,128)} %bitcast.41, s32[2,256]{1,0:T(2,128)} %bitcast.42, s32[8,32]{1,0:T(8,128)} %halo_hbm.2), custom_call_target="tpu_custom_call" | custom-call | tf_op jit(solution)/shard_map/pallas_call | solution.py:233
  2.3 7.3 %all-to-all-start = ((s32[8,1,128]{2,1,0:T(1,128)}), s32[8,1,128]{2,1,0:T(1,128)S(1)}, u32[]{:S(2)}, u32[]{:S(2)}) async-start(s32[8,1,128]{2,1,0:T(1,128)} %bitcast.40), calls=%async_computation | async-start | bytes 8192 | tf_op jit(solution)/shard_map/all_to_all | solution.py:259
  9.6 1.0 %shard_map.175.history_ref = bf16[1024,256]{1,0:T(8,128)(2,1)S(1)} custom-call(bf16[1024,256]{1,0:T(8,128)(2,1)} %history_hbm.1), custom_call_target="tpu_custom_call" | custom-call | tf_op jit(solution)/shard_map/pallas_call | solution.py:233
  10.7 5.3 %all-to-all-done = s32[8,1,128]{2,1,0:T(1,128)S(1)} async-done(((s32[8,1,128]{2,1,0:T(1,128)}), s32[8,1,128]{2,1,0:T(1,128)S(1)}, u32[]{:S(2)}, u32[]{:S(2)}) %all-to-all-start) | async-done | bytes 4128 | tf_op jit(solution)/shard_map/all_to_all | solution.py:259
  16.0 1.2 %shard_map.176 = bf16[256,256]{1,0:T(8,128)(2,1)} custom-call(s32[8,128]{1,0:T(8,128)S(1)} %bitcast.32, bf16[1024,256]{1,0:T(8,128)(2,1)S(1)} %shard_map.175.history_ref), custom_call_target="tpu_custom_call" | custom-call | tf_op jit(solution)/shard_map/pallas_call | solution.py:233
  17.2 3.4 %all-to-all-start.1 = ((bf16[8,32,256]{2,1,0:T(8,128)(2,1)}), bf16[8,32,256]{2,1,0:T(8,128)(2,1)S(1)}, u32[]{:S(2)}, u32[]{:S(2)}) async-start(bf16[8,32,256]{2,1,0:T(8,128)(2,1)} %bitcast.38), calls=%async_computation.1 | async-start | bytes 262144 | tf_op jit(solution)/shard_map/all_to_all | solution.py:259
  20.6 2.8 %shard_map.174 = (s32[1024,1]{1,0:T(8,128)S(1)}, f32[1024,256]{1,0:T(8,128)S(1)}, f32[1024,256]{1,0:T(8,128)S(1)}, bf16[1024,256]{1,0:T(8,128)(2,1)S(1)}, bf16[256,256]{1,0:T(8,128)(2,1)S(1)}) custom-call(s32[8,128]{1,0:T(8,128)S(1)} %bitcast.33, bf16[1024,256]{1,0:T(8,128)(2,1)} %feats_hbm.1, bf16[1024,1024]{1,0:T(8,128)(2,1)} %inner_hbm.1, ...), custom_call_target="tpu_custom_call" | custom-call | tf_op jit(solution)/shard_map/pallas_call | solution.py:233
  23.4 4.5 %all-to-all-done.1 = bf16[8,32,256]{2,1,0:T(8,128)(2,1)S(1)} async-done(((bf16[8,32,256]{2,1,0:T(8,128)(2,1)}), bf16[8,32,256]{2,1,0:T(8,128)(2,1)S(1)}, u32[]{:S(2)}, u32[]{:S(2)}) %all-to-all-start.1) | async-done | bytes 131104 | tf_op jit(solution)/shard_map/all_to_all | solution.py:259
  27.9 1.8 %shard_map.177 = (bf16[1024,256]{1,0:T(8,128)(2,1)}, bf16[1024,256]{1,0:T(8,128)(2,1)}) custom-call(s32[1024,1]{1,0:T(8,128)S(1)} %get-tuple-element.34.ids_ref, f32[1024,256]{1,0:T(8,128)S(1)} %get-tuple-element.35.agg_ref, f32[1024,256]{1,0:T(8,128)S(1)} %get-tuple-element.36.base_ref, bf16[256,256]{1,0:T(8,128)(2,1)S(1)} %bitcast.31, ...), custom_call_target="tpu_custom_call" | custom-call | tf_op jit(solution)/shard_map/pallas_call | solution.py:233
  29.7 3.5 %all-to-all-start.2 = ((bf16[8,128,256]{2,1,0:T(8,128)(2,1)}), bf16[8,128,256]{2,1,0:T(8,128)(2,1)S(1)}, u32[]{:S(2)}, u32[]{:S(2)}) async-start(bf16[8,128,256]{2,1,0:T(8,128)(2,1)} %bitcast.39), calls=%async_computation.2 | async-start | bytes 1048576 | tf_op jit(solution)/shard_map/all_to_all | solution.py:259
  33.8 1.1 %shard_map.179 = (bf16[512,1024]{1,0:T(8,128)(2,1)S(1)}, bf16[1024,512]{1,0:T(8,128)(2,1)S(1)}, f32[256,1]{1,0:T(8,128)S(1)}, bf16[256,256]{1,0:T(8,128)(2,1)S(1...) custom-call(s32[1,512]{1,0:T(1,128)S(1)} %get-tuple-element.41.place_ref, s32[1,256]{1,0:T(1,128)} %bitcast.44, ...), custom_call_target="tpu_custom_call" | custom-call | tf_op jit(solution)/shard_map/pallas_call | solution.py:233
  34.9 10.5 %all-to-all-done.2 = bf16[8,128,256]{2,1,0:T(8,128)(2,1)S(1)} async-done(((bf16[8,128,256]{2,1,0:T(8,128)(2,1)}), bf16[8,128,256]{2,1,0:T(8,128)(2,1)S(1)}, u32[]{:S(2)}, u32[]{:S(2)}) %all-to-all-start.2) | async-done | bytes 524320 | tf_op jit(solution)/shard_map/all_to_all | solution.py:259
  46.4 1.4 %shard_map.181 = bf16[1024,256]{1,0:T(8,128)(2,1)} custom-call(bf16[512,256]{1,0:T(8,128)(2,1)S(1)} %get-tuple-element.47.rows_ref, bf16[256,256]{1,0:T(8,128)(2,1)S(1)} %get-tuple-element.48.d_pre_ref, bf16[256,256]{1,0:T(8,128)(2,1)S(1)} %get-tuple-element.44.w1_ref, bf16[1024,512]{1,0:T(8,128)(2,1)S(1)} %get-tuple-element.49.scatter_ref), custom_call_target="tpu_custom_call" | custom-call | tf_op jit(solution)/shard_map/pallas_call | solution.py:233
  47.8 3.7 %all-to-all-start.3 = ((bf16[8,128,256]{2,1,0:T(8,128)(2,1)}), bf16[8,128,256]{2,1,0:T(8,128)(2,1)S(1)}, u32[]{:S(2)}, u32[]{:S(2)}) async-start(bf16[8,128,256]{2,1,0:T(8,128)(2,1)} %bitcast.35), calls=%async_computation.3 | async-start | bytes 1048576 | tf_op jit(solution)/shard_map/all_to_all | solution.py:259
  51.6 1.5 %collective-permute-start.1 = (bf16[136,256]{1,0:T(8,128)(2,1)S(1)}, bf16[136,256]{1,0:T(8,128)(2,1)S(1)}, u32[]{:S(2)}, u32[]{:S(2)}) collective-permute-start(bf16[136,256]{1,0:T(8,128)(2,1)S(1)} %add_convert_fusion.1), channel_id=1, source_target_pairs={{0,2},{1,3},{2,0},{3,1},{4,6},{5,7},{6,4},{7,5},{8,10},{9,11},{10,... | collective-permute-start | bytes 208904 | tf_op jit(solution)/shard_map/ppermute | solution.py:244
  53.1 2.9 %collective-permute-done.1 = bf16[136,256]{1,0:T(8,128)(2,1)S(1)} collective-permute-done((bf16[136,256]{1,0:T(8,128)(2,1)S(1)}, bf16[136,256]{1,0:T(8,128)(2,1)S(1)}, u32[]{:S(2)}, u32[]{:S(2)}) %collective-permute-start.1) | collective-permute-done | bytes 69664 | tf_op jit(solution)/shard_map/ppermute | solution.py:244
  56.1 2.0 %collective-permute-start.2 = (bf16[136,256]{1,0:T(8,128)(2,1)S(1)}, bf16[136,256]{1,0:T(8,128)(2,1)S(1)}, u32[]{:S(2)}, u32[]{:S(2)}) collective-permute-start(bf16[136,256]{1,0:T(8,128)(2,1)S(1)} %add_convert_fusion), channel_id=1, source_target_pairs={{0,4},{4,0},{8,12},{12,8},{16,20},{20,16},{24,28},{28,24},{1,5},{5... | collective-permute-start | bytes 208904 | tf_op jit(solution)/shard_map/ppermute | solution.py:244
  58.0 1.5 %collective-permute-start.3 = (bf16[136,256]{1,0:T(8,128)(2,1)S(1)}, bf16[136,256]{1,0:T(8,128)(2,1)S(1)}, u32[]{:S(2)}, u32[]{:S(2)}) collective-permute-start(bf16[136,256]{1,0:T(8,128)(2,1)S(1)} %add_convert_fusion), channel_id=1, source_target_pairs={{0,8},{4,12},{8,0},{12,4},{16,24},{20,28},{24,16},{28,20},{1,9},{5... | collective-permute-start | bytes 208904 | tf_op jit(solution)/shard_map/ppermute | solution.py:244
  61.1 2.6 %collective-permute-done.3 = bf16[136,256]{1,0:T(8,128)(2,1)S(1)} collective-permute-done((bf16[136,256]{1,0:T(8,128)(2,1)S(1)}, bf16[136,256]{1,0:T(8,128)(2,1)S(1)}, u32[]{:S(2)}, u32[]{:S(2)}) %collective-permute-start.3) | collective-permute-done | bytes 69664 | tf_op jit(solution)/shard_map/ppermute | solution.py:244
  63.7 2.0 %collective-permute-done.4 = bf16[136,256]{1,0:T(8,128)(2,1)S(1)} collective-permute-done((bf16[136,256]{1,0:T(8,128)(2,1)S(1)}, bf16[136,256]{1,0:T(8,128)(2,1)S(1)}, u32[]{:S(2)}, u32[]{:S(2)}) %collective-permute-start.4) | collective-permute-done | bytes 69664 | tf_op jit(solution)/shard_map/ppermute | solution.py:244
  67.5 1.9 %collective-permute-done.5 = f32[512,256]{1,0:T(8,128)S(1)} collective-permute-done((f32[512,256]{1,0:T(8,128)S(1)}, f32[512,256]{1,0:T(8,128)S(1)}, u32[]{:S(2)}, u32[]{:S(2)}) %collective-permute-start.5) | collective-permute-done | bytes 524320 | tf_op jit(solution)/shard_map/ppermute | solution.py:244
  69.5 1.5 %collective-permute-start.7 = (bf16[1,256,256]{2,1,0:T(8,128)(2,1)S(1)}, bf16[1,256,256]{2,1,0:T(8,128)(2,1)S(1)}, u32[]{:S(2)}, u32[]{:S(2)}) collective-permute-start(bf16[1,256,256]{2,1,0:T(8,128)(2,1)S(1)} %fusion.2), channel_id=1, source_target_pairs={{0,2},{1,3},{2,0},{3,1},{4,6},{5,7},{6,4},{7,5},{8,10},{9,11},{10,... | collective-permute-start | bytes 393224 | tf_op jit(solution)/shard_map/ppermute | solution.py:244
  71.0 2.6 %collective-permute-start.6 = (bf16[136,256]{1,0:T(8,128)(2,1)S(1)}, bf16[136,256]{1,0:T(8,128)(2,1)S(1)}, u32[]{:S(2)}, u32[]{:S(2)}) collective-permute-start(bf16[136,256]{1,0:T(8,128)(2,1)S(1)} %add_add_fusion), channel_id=1, source_target_pairs={{0,16},{4,20},{8,24},{12,28},{16,0},{20,4},{24,8},{28,12},{1,17},{... | collective-permute-start | bytes 208904 | tf_op jit(solution)/shard_map/ppermute | solution.py:244
  73.6 3.7 %collective-permute-done.6 = bf16[136,256]{1,0:T(8,128)(2,1)S(1)} collective-permute-done((bf16[136,256]{1,0:T(8,128)(2,1)S(1)}, bf16[136,256]{1,0:T(8,128)(2,1)S(1)}, u32[]{:S(2)}, u32[]{:S(2)}) %collective-permute-start.6) | collective-permute-done | bytes 69664 | tf_op jit(solution)/shard_map/ppermute | solution.py:244
  (23 shorter events, 7.3 us)
Async XLA Ops:
  2.3 13.7 %all-to-all-start = ((s32[8,1,128]{2,1,0:T(1,128)}), s32[8,1,128]{2,1,0:T(1,128)S(1)}, u32[]{:S(2)}, u32[]{:S(2)}) async-start(s32[8,1,128]{2,1,0:T(1,128)} %bitcast.40), calls=%async_computation | async-start | bytes 8192 | tf_op jit(solution)/shard_map/all_to_all | solution.py:259
  17.2 10.7 %all-to-all-start.1 = ((bf16[8,32,256]{2,1,0:T(8,128)(2,1)}), bf16[8,32,256]{2,1,0:T(8,128)(2,1)S(1)}, u32[]{:S(2)}, u32[]{:S(2)}) async-start(bf16[8,32,256]{2,1,0:T(8,128)(2,1)} %bitcast.38), calls=%async_computation.1 | async-start | bytes 262144 | tf_op jit(solution)/shard_map/all_to_all | solution.py:259
  27.9 5.3 %copy-start = (bf16[256]{0:T(256)(128)(2,1)S(1)}, bf16[256]{0:T(256)(128)(2,1)}, u32[]{:S(2)}) copy-start(bf16[256]{0:T(256)(128)(2,1)} %param.27) | copy-start | bytes 1540
  29.7 15.6 %all-to-all-start.2 = ((bf16[8,128,256]{2,1,0:T(8,128)(2,1)}), bf16[8,128,256]{2,1,0:T(8,128)(2,1)S(1)}, u32[]{:S(2)}, u32[]{:S(2)}) async-start(bf16[8,128,256]{2,1,0:T(8,128)(2,1)} %bitcast.39), calls=%async_computation.2 | async-start | bytes 1048576 | tf_op jit(solution)/shard_map/all_to_all | solution.py:259
  46.3 5.2 %collective-permute-start = (f32[136,256]{1,0:T(8,128)S(1)}, f32[136,256]{1,0:T(8,128)S(1)}, u32[]{:S(2)}, u32[]{:S(2)}) collective-permute-start(f32[136,256]{1,0:T(8,128)S(1)} %get-tuple-element.51), channel_id=1, source_target_pairs={{0,1},{1,0},{2,3},{3,2},{4,5},{5,4},{6,7},{7,6},{8,9},{9,8},{10,11... | collective-permute-start | bytes 417800 | tf_op jit(solution)/shard_map/ppermute | solution.py:244
  47.8 18.9 %all-to-all-start.3 = ((bf16[8,128,256]{2,1,0:T(8,128)(2,1)}), bf16[8,128,256]{2,1,0:T(8,128)(2,1)S(1)}, u32[]{:S(2)}, u32[]{:S(2)}) async-start(bf16[8,128,256]{2,1,0:T(8,128)(2,1)} %bitcast.35), calls=%async_computation.3 | async-start | bytes 1048576 | tf_op jit(solution)/shard_map/all_to_all | solution.py:259
  51.6 4.5 %collective-permute-start.1 = (bf16[136,256]{1,0:T(8,128)(2,1)S(1)}, bf16[136,256]{1,0:T(8,128)(2,1)S(1)}, u32[]{:S(2)}, u32[]{:S(2)}) collective-permute-start(bf16[136,256]{1,0:T(8,128)(2,1)S(1)} %add_convert_fusion.1), channel_id=1, source_target_pairs={{0,2},{1,3},{2,0},{3,1},{4,6},{5,7},{6,4},{7,5},{8,10},{9,11},{10,... | collective-permute-start | bytes 208904 | tf_op jit(solution)/shard_map/ppermute | solution.py:244
  56.1 5.0 %collective-permute-start.2 = (bf16[136,256]{1,0:T(8,128)(2,1)S(1)}, bf16[136,256]{1,0:T(8,128)(2,1)S(1)}, u32[]{:S(2)}, u32[]{:S(2)}) collective-permute-start(bf16[136,256]{1,0:T(8,128)(2,1)S(1)} %add_convert_fusion), channel_id=1, source_target_pairs={{0,4},{4,0},{8,12},{12,8},{16,20},{20,16},{24,28},{28,24},{1,5},{5... | collective-permute-start | bytes 208904 | tf_op jit(solution)/shard_map/ppermute | solution.py:244
  58.0 5.7 %collective-permute-start.3 = (bf16[136,256]{1,0:T(8,128)(2,1)S(1)}, bf16[136,256]{1,0:T(8,128)(2,1)S(1)}, u32[]{:S(2)}, u32[]{:S(2)}) collective-permute-start(bf16[136,256]{1,0:T(8,128)(2,1)S(1)} %add_convert_fusion), channel_id=1, source_target_pairs={{0,8},{4,12},{8,0},{12,4},{16,24},{20,28},{24,16},{28,20},{1,9},{5... | collective-permute-start | bytes 208904 | tf_op jit(solution)/shard_map/ppermute | solution.py:244
  59.5 6.2 %collective-permute-start.4 = (bf16[136,256]{1,0:T(8,128)(2,1)S(1)}, bf16[136,256]{1,0:T(8,128)(2,1)S(1)}, u32[]{:S(2)}, u32[]{:S(2)}) collective-permute-start(bf16[136,256]{1,0:T(8,128)(2,1)S(1)} %add_convert_fusion), channel_id=1, source_target_pairs={{0,12},{4,8},{8,4},{12,0},{16,28},{20,24},{24,20},{28,16},{1,13},{... | collective-permute-start | bytes 208904 | tf_op jit(solution)/shard_map/ppermute | solution.py:244
  67.4 2.0 %collective-permute-start.5 = (f32[512,256]{1,0:T(8,128)S(1)}, f32[512,256]{1,0:T(8,128)S(1)}, u32[]{:S(2)}, u32[]{:S(2)}) collective-permute-start(f32[512,256]{1,0:T(8,128)S(1)} %get-tuple-element.54), channel_id=1, source_target_pairs={{0,1},{1,0},{2,3},{3,2},{4,5},{5,4},{6,7},{7,6},{8,9},{9,8},{10,11... | collective-permute-start | bytes 1572872 | tf_op jit(solution)/shard_map/ppermute | solution.py:244
  69.5 7.9 %collective-permute-start.7 = (bf16[1,256,256]{2,1,0:T(8,128)(2,1)S(1)}, bf16[1,256,256]{2,1,0:T(8,128)(2,1)S(1)}, u32[]{:S(2)}, u32[]{:S(2)}) collective-permute-start(bf16[1,256,256]{2,1,0:T(8,128)(2,1)S(1)} %fusion.2), channel_id=1, source_target_pairs={{0,2},{1,3},{2,0},{3,1},{4,6},{5,7},{6,4},{7,5},{8,10},{9,11},{10,... | collective-permute-start | bytes 393224 | tf_op jit(solution)/shard_map/ppermute | solution.py:244
  71.0 6.3 %collective-permute-start.6 = (bf16[136,256]{1,0:T(8,128)(2,1)S(1)}, bf16[136,256]{1,0:T(8,128)(2,1)S(1)}, u32[]{:S(2)}, u32[]{:S(2)}) collective-permute-start(bf16[136,256]{1,0:T(8,128)(2,1)S(1)} %add_add_fusion), channel_id=1, source_target_pairs={{0,16},{4,20},{8,24},{12,28},{16,0},{20,4},{24,8},{28,12},{1,17},{... | collective-permute-start | bytes 208904 | tf_op jit(solution)/shard_map/ppermute | solution.py:244
  77.4 1.4 %collective-permute-start.8 = (f32[136,256]{1,0:T(8,128)S(1)}, f32[136,256]{1,0:T(8,128)S(1)}, u32[]{:S(2)}, u32[]{:S(2)}) collective-permute-start(f32[136,256]{1,0:T(8,128)S(1)} %convert_add_fusion.mine_ref), channel_id=1, source_target_pairs={{0,1},{1,0},{2,3},{3,2},{4,5},{5,4},{6,7},{7,6},{8,9},{9,8},{10,11... | collective-permute-start | bytes 417800 | tf_op jit(solution)/shard_map/ppermute | solution.py:244

commit v3 on v2

--- a/solution.py
+++ b/solution.py
@@ -12,6 +12,7 @@
 I32 = jnp.int32
 VMEM_BYTES = 24 * 1024 * 1024
 CHUNKS = 4
+X_PARTS = 2
 
 
 def iota(shape, dim):
@@ -107,19 +108,14 @@
     return copies
 
 
-def load_kernel(history_hbm, history_ref, sem):
-    wait(loads((history_hbm,), (history_ref,), sem))
-
-
 def inner_kernel(
-    cap, word_ref, feats_hbm, inner_hbm, self_hbm, b_hbm, halo_hbm, nbr_hbm,
-    ids_ref, agg_ref, base_ref, halo_ref, nbr_ref, feats_ref, inner_ref, self_ref, b_ref, sem,
+    feats_hbm, inner_hbm, self_hbm, b_hbm, halo_hbm, nbr_hbm, history_hbm,
+    agg_ref, base_ref, halo_ref, nbr_ref, history_ref, feats_ref, inner_ref, self_ref, b_ref, sem,
 ):
     copies = loads(
-        (feats_hbm, inner_hbm, self_hbm, b_hbm, halo_hbm, nbr_hbm),
-        (feats_ref, inner_ref, self_ref, b_ref, halo_ref, nbr_ref), sem,
-    )
-    ids_ref[...] = as_column(word_ref[...] & 65535, cap)
+        (feats_hbm, inner_hbm, self_hbm, b_hbm, halo_hbm, nbr_hbm, history_hbm),
+        (feats_ref, inner_ref, self_ref, b_ref, halo_ref, nbr_ref, history_ref), sem,
+    )
     wait(copies)
     feats = feats_ref[...]
     agg_ref[...] = dot(inner_ref[...], feats)
@@ -139,15 +135,16 @@
     target_ref[...] = row_to_column(label_ref[...].astype(F32))
 
 
-def sum_mask_kernel(cap, blocks, rep_ref, word_ref, mask_ref):
+def sum_mask_kernel(cap, rep_ref, word_ref, *mask_refs):
     ids = as_row(word_ref[...] & 65535, cap)
-    size = mask_ref.shape[0] // blocks
-    for j in range(blocks):
+    size = mask_refs[0].shape[0]
+    for j, mask_ref in enumerate(mask_refs):
         node = iota((size, ids.shape[1]), 0) + (rep_ref[0] ^ j) * size
-        mask_ref[j * size:(j + 1) * size, :] = ones_where(node == ids)
-
-
-def halo_kernel(cap, word_ref, history_ref, out_ref):
+        mask_ref[...] = ones_where(node == ids)
+
+
+def halo_kernel(cap, cap_edge, word_ref, history_ref, out_ref, ids_ref):
+    ids_ref[...] = as_column(word_ref[...] & 65535, cap_edge)
     ids = as_column(lax.shift_right_logical(word_ref[...], 16), cap)
     nodes = history_ref.shape[0]
     out_ref[...] = dot(ones_where(ids == iota((ids.shape[0], nodes), 1)), history_ref[...]).astype(BF16)
@@ -195,15 +192,26 @@
     send_ref[half:] = aux
 
 
-def grads_kernel(rows_ref, d_pre_ref, w1_ref, scatter_ref, grads_hbm, grads_ref, sem):
+def grads_kernel(rows_ref, d_pre_ref, w1_ref, grads_ref):
     queries = d_pre_ref.shape[0]
     dz = dot(d_pre_ref[...], w1_ref[...], ((1,), (1,)))
-    head, tail = rows_ref[:queries, :].astype(F32), rows_ref[queries:, :].astype(F32)
-    grads = jnp.concatenate([dz * tail, dz * head], axis=0).astype(BF16)
-    wait(store(lambda at, size: dot(scatter_ref[at:at + size, :], grads).astype(BF16), grads_ref, grads_hbm, sem, CHUNKS))
-
-
-def join_kernel(rep_ref, mine_ref, other_ref, grad_ref, bias_ref, outer_ref):
+    grads_ref[:queries, :] = (dz * rows_ref[queries:, :].astype(F32)).astype(BF16)
+    grads_ref[queries:, :] = (dz * rows_ref[:queries, :].astype(F32)).astype(BF16)
+
+
+def place_kernel(grads_ref, scatter_ref, out_hbm, out_ref, sem):
+    grads = grads_ref[...]
+    wait(store(lambda at, size: dot(scatter_ref[at:at + size, :], grads).astype(BF16), out_ref, out_hbm, sem, CHUNKS))
+
+
+def final_kernel(rep_ref, mine_ref, other_ref, keep_ref, *refs):
+    away_refs, (sums_ref, grad_ref, bias_ref, outer_ref) = refs[:-4], refs[-4:]
+    rows = keep_ref.shape[0] // max(1, len(away_refs))
+    for i, away_ref in enumerate(away_refs):
+        at = pl.ds(i * rows, rows)
+        sums_ref[at, :] = keep_ref[at, :] + away_ref[...].astype(F32)
+    if not away_refs:
+        sums_ref[...] = keep_ref[...]
     half = grad_ref.shape[0] // 2
     odd = (rep_ref[0] & 1) == 1
     mine, other = mine_ref[...], other_ref[...]
@@ -214,12 +222,8 @@
     outer_ref[...] = low[half + 1:half + 2]
 
 
-def scatter_kernel(size, mask_ref, grads_ref, keep_ref, send_ref):
-    grads = grads_ref[...]
-    for j in range(mask_ref.shape[0] // size):
-        sums = dot(mask_ref[j * size:(j + 1) * size, :], grads)
-        out = send_ref if j % 2 else keep_ref
-        out[(j // 2) * size:(j // 2 + 1) * size, :] = sums
+def scatter_kernel(mask_ref, grads_ref, out_ref):
+    out_ref[...] = dot(mask_ref[...], grads_ref[...]).astype(out_ref.dtype)
 
 
 def call(kernel, outs, *args, scalar=False, hbm_in=(), hbm_out=(), far_out=(), scratch=()):
@@ -285,30 +289,29 @@
         ),
     )
     word = exchange(word, "dom")
-    (history,) = call(
-        load_kernel, [(history.shape, BF16)], history, hbm_in=(0,), scratch=(pltpu.SemaphoreType.DMA((1,)),)
-    )
-    (halo,) = call(
-        functools.partial(halo_kernel, cap_halo), [((n_dom * cap_halo, width), BF16)], word, history, far_out=(0,)
-    )
-    halo = exchange(halo.reshape(n_dom, cap_halo, width), "dom").reshape(-1, width)
-    fetch, agg, base, adj_halo, w_nbr = call(
-        functools.partial(inner_kernel, cap),
+    agg, base, adj_halo, w_nbr, history = call(
+        inner_kernel,
         [
-            ((slots, 1), I32), ((nodes, width), F32), ((nodes, width), F32),
-            (adj_halo.shape, BF16), (w_nbr.shape, BF16),
+            ((nodes, width), F32), ((nodes, width), F32),
+            (adj_halo.shape, BF16), (w_nbr.shape, BF16), (history.shape, BF16),
         ],
-        word, feats, adj_inner, w_self, b_enc.reshape(1, -1), adj_halo, w_nbr,
-        hbm_in=(1, 2, 3, 4, 5, 6),
+        feats, adj_inner, w_self, b_enc.reshape(1, -1), adj_halo, w_nbr, history,
+        hbm_in=(0, 1, 2, 3, 4, 5, 6),
         scratch=(
             pltpu.VMEM(feats.shape, BF16), pltpu.VMEM(adj_inner.shape, BF16), pltpu.VMEM(w_self.shape, BF16),
-            pltpu.VMEM((1, width), F32), pltpu.SemaphoreType.DMA((6,)),
+            pltpu.VMEM((1, width), F32), pltpu.SemaphoreType.DMA((7,)),
         ),
     )
+    halo, ids = call(
+        functools.partial(halo_kernel, cap_halo, cap),
+        [((n_dom * cap_halo, width), BF16), ((slots, 1), I32)],
+        word, history,
+    )
+    halo = exchange(halo.reshape(n_dom, cap_halo, width), "dom").reshape(-1, width)
     embed, fetched = call(
         embed_kernel,
         [((nodes, width), BF16), ((slots, width), BF16)],
-        fetch, agg, base, halo, adj_halo, w_nbr,
+        ids, agg, base, halo, adj_halo, w_nbr,
         hbm_out=(0, 1),
         scratch=(
             pltpu.VMEM((nodes, width), BF16), pltpu.VMEM((slots, width), BF16),
@@ -333,56 +336,62 @@
         rep, fetched, gather, target, w1, b1, w2, scalar=True,
     )
     weights = keep + swap(send, "rep", 1)
+    (grads,) = call(grads_kernel, [((ends, width), BF16)], rows, d_pre, w1)
+    grads, weights = lax.optimization_barrier((grads, weights))
     step = 2
     while step < n_rep:
         weights = reduce_pairs(weights, "rep", step)
         step *= 2
+    (placed,) = call(
+        place_kernel,
+        [((slots, width), BF16)],
+        grads, scatter,
+        hbm_out=(0,),
+        scratch=(pltpu.VMEM((slots, width), BF16), pltpu.SemaphoreType.DMA((CHUNKS,))),
+    )
+    back = exchange(placed.reshape(n_dom, cap, width), "dom").reshape(-1, width)
     step = 1
     while 4 * step <= n_dom // 2:
         weights = reduce_fours(weights, "dom", step)
         step *= 4
-    (grads,) = call(
-        grads_kernel,
-        [((slots, width), BF16)],
-        rows, d_pre, w1, scatter,
-        hbm_out=(0,),
-        scratch=(pltpu.VMEM((slots, width), BF16), pltpu.SemaphoreType.DMA((CHUNKS,))),
-    )
-    back = exchange(grads.reshape(n_dom, cap, width), "dom").reshape(-1, width)
 
     back, weights = lax.optimization_barrier((back, weights))
     size = nodes // n_rep
-    (mask,) = call(
-        functools.partial(sum_mask_kernel, cap, n_rep), [((nodes, slots), BF16)], rep, word, scalar=True
-    )
-    keep, send = call(
-        functools.partial(scatter_kernel, size),
-        [((nodes // 2, width), F32), ((nodes // 2, width), F32)],
-        mask, back,
-    )
-    sums = keep + swap(send, "rep", 1)
-    rep_step = 2
+    masks = call(
+        functools.partial(sum_mask_kernel, cap), [((size, slots), BF16)] * n_rep, rep, word, scalar=True
+    )
+
+    def block_sum(j, dtype):
+        (out,) = call(scatter_kernel, [((size, width), dtype)], masks[j], back)
+        return out
+
+    sums = {}
+    for j in reversed(range(0, n_rep, 2)):
+        send = block_sum(j + 1, BF16)
+        sums[j] = block_sum(j, F32) + swap(send, "rep", 1).astype(F32)
+    rep_step, away = 2, []
     while rep_step < n_rep:
-        blocks = sums.reshape(-1, 2, size, width)
-        away = swap(blocks[:, 1].astype(BF16), "rep", rep_step)
-        if step < n_dom:
-            mine = weights.astype(BF16)
-            others = swap(mine, "dom", step)
-            others, away = lax.optimization_barrier((others, away))
-            weights = mine.astype(F32) + others.astype(F32)
-            step *= 2
-        sums = blocks[:, 0] + away.astype(F32)
+        for j in range(0, n_rep, 2 * rep_step):
+            parts = jnp.split(sums[j + rep_step].astype(BF16), X_PARTS, axis=0)
+            away = [swap(part, "rep", rep_step) for part in parts]
+            if step < n_dom:
+                mine = weights.astype(BF16)
+                others = swap(mine, "dom", step)
+                others, away[0] = lax.optimization_barrier((others, away[0]))
+                weights = mine.astype(F32) + others.astype(F32)
+                step *= 2
+            if 2 * rep_step < n_rep:
+                sums[j] = sums[j] + jnp.concatenate(away, axis=0).astype(F32)
         rep_step *= 2
-    grad_embed = sums.reshape(size, width)
     while step < n_dom:
         weights = reduce_pairs(weights, "dom", step)
         step *= 2
 
     others = swap(weights, "rep", 1)
-    grad_dec1, grad_bias1, grad_dec2 = call(
-        join_kernel,
-        [((width, width), F32), ((1, width), F32), ((1, width), F32)],
-        rep, weights, others, scalar=True, far_out=(0, 1, 2),
+    grad_embed, grad_dec1, grad_bias1, grad_dec2 = call(
+        final_kernel,
+        [((size, width), F32), ((width, width), F32), ((1, width), F32), ((1, width), F32)],
+        rep, weights, others, sums[0], *away, scalar=True, far_out=(0, 1, 2, 3),
     )
     return embed, grad_embed, grad_dec1, grad_bias1[0], grad_dec2[0]
 

time: 80.1 us -> 78.5 us (0.980)
  blocking collectives: 0 us -> 9.76 us
  waiting for transfers between devices: 35.7 us -> 28.4 us
  starting transfers between devices: 27.3 us -> 24.6 us
    all_to_all x0 -> x1, blocking collectives: none -> 9.76 us  [exchange(): return lax.all_to_all(x, axis, split_axis=0, concat_axis=0, tiled=True)]
    all_to_all x4 -> x3, waiting for transfers between devices: 21.2 us -> 15 us  [exchange(): return lax.all_to_all(x, axis, split_axis=0, concat_axis=0, tiled=True)]
    all_to_all x4 -> x3, starting transfers between devices: 17.8 us -> 14.4 us  [exchange(): return lax.all_to_all(x, axis, split_axis=0, concat_axis=0, tiled=True)]
    ppermute x9 -> x11, waiting for transfers between devices: 14.6 us -> 13.4 us  [swap(): lax.ppermute(x, axis, [(i, i ^ mask) for i in range(lax.axis_size(axis))])]
    ppermute x9 -> x11, starting transfers between devices: 9.47 us -> 10.2 us  [swap(): lax.ppermute(x, axis, [(i, i ^ mask) for i in range(lax.axis_size(axis))])]
    pallas_call x11 -> x14, Pallas kernels: 14.2 us -> 13.7 us  [call(): pl.pallas_call(kernel, out_shape=[(pltpu.HBM if i in far_out else pltpu.V...]
  transfers between devices with their start and end apart: 13 -> 14, of which waited for: 11 -> 10; matrix products, arithmetic and copies ran while one was open for 2% -> 1% of each run, Pallas kernels for 9% -> 8%
where the time goes in v3:
time: 78.5 us; the launch traced here: 78 us
  waiting for transfers between devices  28.4 us (36%)
  starting transfers between devices  24.6 us (31%)
  Pallas kernels  13.7 us (17%)
  blocking collectives  9.76 us (12%)
  between operations  0.84 us (1%)
    all_to_all x3, waiting for transfers between devices, exchange(): return lax.all_to_all(x, axis, split_axis=0, concat_axis=0, tiled=True)  15 us
    all_to_all x3, starting transfers between devices, exchange(): return lax.all_to_all(x, axis, split_axis=0, concat_axis=0, tiled=True)  14.4 us
    pallas_call x14, Pallas kernels, call(): pl.pallas_call(kernel, out_shape=[(pltpu.HBM if i in far_out else pltpu.V...  13.7 us
    ppermute x11, waiting for transfers between devices, swap(): lax.ppermute(x, axis, [(i, i ^ mask) for i in range(lax.axis_size(axis))])  13.4 us
    ppermute x11, starting transfers between devices, swap(): lax.ppermute(x, axis, [(i, i ^ mask) for i in range(lax.axis_size(axis))])  10.2 us
    all_to_all x1, blocking collectives, exchange(): return lax.all_to_all(x, axis, split_axis=0, concat_axis=0, tiled=True)  9.76 us
  transfers between devices with their start and end apart: 14, of which 10 were waited for; matrix products, arithmetic and copies ran while one was open for 1% of the time, Pallas kernels for 8%

profile of v3, /device:TPU:0, one launch (start us, length us, event | category | flops | bytes accessed | tf_op | source)
XLA Modules:
  0.0 78.0 jit_solution(14186686013138132685)
XLA Ops:
  0.6 1.7 %shard_map.173 = (s32[8,128]{1,0:T(8,128)}, s32[1,512]{1,0:T(1,128)S(1)}) custom-call(s32[2,256]{1,0:T(2,128)} %bitcast.30, s32[2,256]{1,0:T(2,128)} %bitcast.31, s32[8,32]{1,0:T(8,128)} %halo_hbm.2), custom_call_target="tpu_custom_call" | custom-call | tf_op jit(solution)/shard_map/pallas_call | solution.py:237
  2.3 7.3 %all-to-all-start = ((s32[8,1,128]{2,1,0:T(1,128)}), s32[8,1,128]{2,1,0:T(1,128)S(1)}, u32[]{:S(2)}, u32[]{:S(2)}) async-start(s32[8,1,128]{2,1,0:T(1,128)} %bitcast.29), calls=%async_computation | async-start | bytes 8192 | tf_op jit(solution)/shard_map/all_to_all | solution.py:263
  9.6 3.0 %shard_map.174 = (f32[1024,256]{1,0:T(8,128)S(1)}, f32[1024,256]{1,0:T(8,128)S(1)}, bf16[1024,256]{1,0:T(8,128)(2,1)S(1)}, bf16[256,256]{1,0:T(8,128)(2,1)S(1)}, bf16[1024,256]{1,0:T(8,128)(2,1)S(1)}) custom-call(bf16[1024,256]{1,0:T(8,128)(2,1)} %feats_hbm.1, bf16[1024,1024]{1,0:T(8,128)(2,1)} %inner_hbm.1, bf16[256,256]{1,0:T(8,128)(2,1)} %self_hbm.1, ...), custom_call_target="tpu_custom_call" | custom-call | tf_op jit(solution)/shard_map/pallas_call | solution.py:237
  12.6 3.4 %all-to-all-done = s32[8,1,128]{2,1,0:T(1,128)S(1)} async-done(((s32[8,1,128]{2,1,0:T(1,128)}), s32[8,1,128]{2,1,0:T(1,128)S(1)}, u32[]{:S(2)}, u32[]{:S(2)}) %all-to-all-start) | async-done | bytes 4128 | tf_op jit(solution)/shard_map/all_to_all | solution.py:263
  16.0 1.0 %shard_map.175 = (bf16[256,256]{1,0:T(8,128)(2,1)S(1)}, s32[1024,1]{1,0:T(8,128)S(1)}) custom-call(s32[8,128]{1,0:T(8,128)S(1)} %bitcast.25, bf16[1024,256]{1,0:T(8,128)(2,1)S(1)} %get-tuple-element.41.history_ref), custom_call_target="tpu_custom_call" | custom-call | tf_op jit(solution)/shard_map/pallas_call | solution.py:237
  17.0 9.8 %all_to_all.26 = bf16[8,32,256]{2,1,0:T(8,128)(2,1)S(1)} all-to-all(bf16[8,32,256]{2,1,0:T(8,128)(2,1)S(1)} %bitcast.24), channel_id=1, replica_groups=mesh['dom'=8,'rep'=4] {'dom'}, dimensions={0} | all-to-all | bytes 262144 | tf_op jit(solution)/shard_map/all_to_all | solution.py:263
  26.7 1.8 %shard_map.176 = (bf16[1024,256]{1,0:T(8,128)(2,1)}, bf16[1024,256]{1,0:T(8,128)(2,1)}) custom-call(s32[1024,1]{1,0:T(8,128)S(1)} %get-tuple-element.42.ids_ref, f32[1024,256]{1,0:T(8,128)S(1)} %get-tuple-element.43.agg_ref, f32[1024,256]{1,0:T(8,128)S(1)} %get-tuple-element.44.base_ref, bf16[256,256]{1,0:T(8,128)(2,1)S(1)} %bitcast.23, ...), custom_call_target="tpu_custom_call" | custom-call | tf_op jit(solution)/shard_map/pallas_call | solution.py:237
  28.5 3.5 %all-to-all-start.2 = ((bf16[8,128,256]{2,1,0:T(8,128)(2,1)}), bf16[8,128,256]{2,1,0:T(8,128)(2,1)S(1)}, u32[]{:S(2)}, u32[]{:S(2)}) async-start(bf16[8,128,256]{2,1,0:T(8,128)(2,1)} %bitcast.28), calls=%async_computation.2 | async-start | bytes 1048576 | tf_op jit(solution)/shard_map/all_to_all | solution.py:263
  32.6 1.1 %shard_map.177 = (bf16[512,1024]{1,0:T(8,128)(2,1)S(1)}, bf16[1024,512]{1,0:T(8,128)(2,1)S(1)}, f32[256,1]{1,0:T(8,128)S(1)}, bf16[256,256]{1,0:T(8,128)(2,1)S(1...) custom-call(s32[1,512]{1,0:T(1,128)S(1)} %get-tuple-element.50.place_ref, s32[1,256]{1,0:T(1,128)} %bitcast.33, ...), custom_call_target="tpu_custom_call" | custom-call | tf_op jit(solution)/shard_map/pallas_call | solution.py:237
  33.7 11.1 %all-to-all-done.2 = bf16[8,128,256]{2,1,0:T(8,128)(2,1)S(1)} async-done(((bf16[8,128,256]{2,1,0:T(8,128)(2,1)}), bf16[8,128,256]{2,1,0:T(8,128)(2,1)S(1)}, u32[]{:S(2)}, u32[]{:S(2)}) %all-to-all-start.2) | async-done | bytes 524320 | tf_op jit(solution)/shard_map/all_to_all | solution.py:263
  44.8 1.0 %shard_map.178 = (bf16[512,256]{1,0:T(8,128)(2,1)S(1)}, bf16[256,256]{1,0:T(8,128)(2,1)S(1)}, f32[136,256]{1,0:T(8,128)S(1)}, f32[136,256]{1,0:T(8,128)S(1)}) custom-call(s32[1]{0:T(128)} %bitcast.8.rep_ref, bf16[1024,256]{1,0:T(8,128)(2,1)S(1)} %bitcast.22, bf16[512,1024]{1,0:T(8,128)(2,1)S(1)} %get-tuple-element.51.gather_ref, ...), custom_call_target="tpu_custom_call" | custom-call | tf_op jit(solution)/shard_map/pallas_call | solution.py:237
  46.1 1.1 %collective-permute-done = f32[136,256]{1,0:T(8,128)S(1)} collective-permute-done((f32[136,256]{1,0:T(8,128)S(1)}, f32[136,256]{1,0:T(8,128)S(1)}, u32[]{:S(2)}, u32[]{:S(2)}) %collective-permute-start) | collective-permute-done | bytes 139296 | tf_op jit(solution)/shard_map/ppermute | solution.py:248
  47.3 1.2 %shard_map.180 = bf16[1024,256]{1,0:T(8,128)(2,1)} custom-call(bf16[512,256]{1,0:T(8,128)(2,1)S(1)} %shard_map.179.grads_ref, bf16[1024,512]{1,0:T(8,128)(2,1)S(1)} %get-tuple-element.61.scatter_ref), custom_call_target="tpu_custom_call" | custom-call | tf_op jit(solution)/shard_map/pallas_call | solution.py:237
  48.5 3.6 %all-to-all-start.3 = ((bf16[8,128,256]{2,1,0:T(8,128)(2,1)}), bf16[8,128,256]{2,1,0:T(8,128)(2,1)S(1)}, u32[]{:S(2)}, u32[]{:S(2)}) async-start(bf16[8,128,256]{2,1,0:T(8,128)(2,1)} %bitcast.27), calls=%async_computation.3 | async-start | bytes 1048576 | tf_op jit(solution)/shard_map/all_to_all | solution.py:263
  52.1 1.5 %collective-permute-start.1 = (bf16[136,256]{1,0:T(8,128)(2,1)S(1)}, bf16[136,256]{1,0:T(8,128)(2,1)S(1)}, u32[]{:S(2)}, u32[]{:S(2)}) collective-permute-start(bf16[136,256]{1,0:T(8,128)(2,1)S(1)} %add.24), channel_id=1, source_target_pairs={{0,2},{1,3},{2,0},{3,1},{4,6},{5,7},{6,4},{7,5},{8,10},{9,11},{10,... | collective-permute-start | bytes 208904 | tf_op jit(solution)/shard_map/ppermute | solution.py:248
  53.6 2.8 %collective-permute-done.1 = bf16[136,256]{1,0:T(8,128)(2,1)S(1)} collective-permute-done((bf16[136,256]{1,0:T(8,128)(2,1)S(1)}, bf16[136,256]{1,0:T(8,128)(2,1)S(1)}, u32[]{:S(2)}, u32[]{:S(2)}) %collective-permute-start.1) | collective-permute-done | bytes 69664 | tf_op jit(solution)/shard_map/ppermute | solution.py:248
  56.4 2.1 %collective-permute-start.2 = (bf16[136,256]{1,0:T(8,128)(2,1)S(1)}, bf16[136,256]{1,0:T(8,128)(2,1)S(1)}, u32[]{:S(2)}, u32[]{:S(2)}) collective-permute-start(bf16[136,256]{1,0:T(8,128)(2,1)S(1)} %add_convert_fusion.1), channel_id=1, source_target_pairs={{0,4},{4,0},{8,12},{12,8},{16,20},{20,16},{24,28},{28,24},{1,5},{5... | collective-permute-start | bytes 208904 | tf_op jit(solution)/shard_map/ppermute | solution.py:248
  58.5 1.5 %collective-permute-start.3 = (bf16[136,256]{1,0:T(8,128)(2,1)S(1)}, bf16[136,256]{1,0:T(8,128)(2,1)S(1)}, u32[]{:S(2)}, u32[]{:S(2)}) collective-permute-start(bf16[136,256]{1,0:T(8,128)(2,1)S(1)} %add_convert_fusion.1), channel_id=1, source_target_pairs={{0,8},{4,12},{8,0},{12,4},{16,24},{20,28},{24,16},{28,20},{1,9},{5... | collective-permute-start | bytes 208904 | tf_op jit(solution)/shard_map/ppermute | solution.py:248
  61.2 2.9 %collective-permute-done.3 = bf16[136,256]{1,0:T(8,128)(2,1)S(1)} collective-permute-done((bf16[136,256]{1,0:T(8,128)(2,1)S(1)}, bf16[136,256]{1,0:T(8,128)(2,1)S(1)}, u32[]{:S(2)}, u32[]{:S(2)}) %collective-permute-start.3) | collective-permute-done | bytes 69664 | tf_op jit(solution)/shard_map/ppermute | solution.py:248
  64.1 2.3 %collective-permute-done.4 = bf16[136,256]{1,0:T(8,128)(2,1)S(1)} collective-permute-done((bf16[136,256]{1,0:T(8,128)(2,1)S(1)}, bf16[136,256]{1,0:T(8,128)(2,1)S(1)}, u32[]{:S(2)}, u32[]{:S(2)}) %collective-permute-start.4) | collective-permute-done | bytes 69664 | tf_op jit(solution)/shard_map/ppermute | solution.py:248
  67.7 2.7 %collective-permute-start.5 = (bf16[136,256]{1,0:T(8,128)(2,1)S(1)}, bf16[136,256]{1,0:T(8,128)(2,1)S(1)}, u32[]{:S(2)}, u32[]{:S(2)}) collective-permute-start(bf16[136,256]{1,0:T(8,128)(2,1)S(1)} %add_add_fusion), channel_id=1, source_target_pairs={{0,16},{4,20},{8,24},{12,28},{16,0},{20,4},{24,8},{28,12},{1,17},{... | collective-permute-start | bytes 208904 | tf_op jit(solution)/shard_map/ppermute | solution.py:248
  70.4 1.6 %collective-permute-start.7 = (bf16[128,256]{1,0:T(8,128)(2,1)S(1)}, bf16[128,256]{1,0:T(8,128)(2,1)S(1)}, u32[]{:S(2)}, u32[]{:S(2)}) collective-permute-start(bf16[128,256]{1,0:T(8,128)(2,1)S(1)} %get-tuple-element.76), channel_id=1, source_target_pairs={{0,2},{1,3},{2,0},{3,1},{4,6},{5,7},{6,4},{7,5},{8,10},{9,11},{10,... | collective-permute-start | bytes 196616 | tf_op jit(solution)/shard_map/ppermute | solution.py:248
  73.2 1.5 %collective-permute-done.5 = bf16[136,256]{1,0:T(8,128)(2,1)S(1)} collective-permute-done((bf16[136,256]{1,0:T(8,128)(2,1)S(1)}, bf16[136,256]{1,0:T(8,128)(2,1)S(1)}, u32[]{:S(2)}, u32[]{:S(2)}) %collective-permute-start.5) | collective-permute-done | bytes 69664 | tf_op jit(solution)/shard_map/ppermute | solution.py:248
  74.9 2.3 %collective-permute-done.10.refs_1_ = bf16[128,256]{1,0:T(8,128)(2,1)S(1)} collective-permute-done((bf16[128,256]{1,0:T(8,128)(2,1)S(1)}, bf16[128,256]{1,0:T(8,128)(2,1)S(1)}, u32[]{:S(2)}, u32[]{:S(2)}) %collective-permute-start.10) | collective-permute-done | bytes 65568 | tf_op jit(solution)/shard_map/ppermute | solution.py:248
  (29 shorter events, 5.6 us)
Async XLA Ops:
  2.3 13.7 %all-to-all-start = ((s32[8,1,128]{2,1,0:T(1,128)}), s32[8,1,128]{2,1,0:T(1,128)S(1)}, u32[]{:S(2)}, u32[]{:S(2)}) async-start(s32[8,1,128]{2,1,0:T(1,128)} %bitcast.29), calls=%async_computation | async-start | bytes 8192 | tf_op jit(solution)/shard_map/all_to_all | solution.py:263
  26.7 5.3 %copy-start = (bf16[256]{0:T(256)(128)(2,1)S(1)}, bf16[256]{0:T(256)(128)(2,1)}, u32[]{:S(2)}) copy-start(bf16[256]{0:T(256)(128)(2,1)} %param.27) | copy-start | bytes 1540
  28.5 16.3 %all-to-all-start.2 = ((bf16[8,128,256]{2,1,0:T(8,128)(2,1)}), bf16[8,128,256]{2,1,0:T(8,128)(2,1)S(1)}, u32[]{:S(2)}, u32[]{:S(2)}) async-start(bf16[8,128,256]{2,1,0:T(8,128)(2,1)} %bitcast.28), calls=%async_computation.2 | async-start | bytes 1048576 | tf_op jit(solution)/shard_map/all_to_all | solution.py:263
  45.8 1.4 %collective-permute-start = (f32[136,256]{1,0:T(8,128)S(1)}, f32[136,256]{1,0:T(8,128)S(1)}, u32[]{:S(2)}, u32[]{:S(2)}) collective-permute-start(f32[136,256]{1,0:T(8,128)S(1)} %get-tuple-element.59), channel_id=1, source_target_pairs={{0,1},{1,0},{2,3},{3,2},{4,5},{5,4},{6,7},{7,6},{8,9},{9,8},{10,11... | collective-permute-start | bytes 417800 | tf_op jit(solution)/shard_map/ppermute | solution.py:248
  48.5 18.5 %all-to-all-start.3 = ((bf16[8,128,256]{2,1,0:T(8,128)(2,1)}), bf16[8,128,256]{2,1,0:T(8,128)(2,1)S(1)}, u32[]{:S(2)}, u32[]{:S(2)}) async-start(bf16[8,128,256]{2,1,0:T(8,128)(2,1)} %bitcast.27), calls=%async_computation.3 | async-start | bytes 1048576 | tf_op jit(solution)/shard_map/all_to_all | solution.py:263
  52.1 4.3 %collective-permute-start.1 = (bf16[136,256]{1,0:T(8,128)(2,1)S(1)}, bf16[136,256]{1,0:T(8,128)(2,1)S(1)}, u32[]{:S(2)}, u32[]{:S(2)}) collective-permute-start(bf16[136,256]{1,0:T(8,128)(2,1)S(1)} %add.24), channel_id=1, source_target_pairs={{0,2},{1,3},{2,0},{3,1},{4,6},{5,7},{6,4},{7,5},{8,10},{9,11},{10,... | collective-permute-start | bytes 208904 | tf_op jit(solution)/shard_map/ppermute | solution.py:248
  56.4 4.8 %collective-permute-start.2 = (bf16[136,256]{1,0:T(8,128)(2,1)S(1)}, bf16[136,256]{1,0:T(8,128)(2,1)S(1)}, u32[]{:S(2)}, u32[]{:S(2)}) collective-permute-start(bf16[136,256]{1,0:T(8,128)(2,1)S(1)} %add_convert_fusion.1), channel_id=1, source_target_pairs={{0,4},{4,0},{8,12},{12,8},{16,20},{20,16},{24,28},{28,24},{1,5},{5... | collective-permute-start | bytes 208904 | tf_op jit(solution)/shard_map/ppermute | solution.py:248
  58.5 5.6 %collective-permute-start.3 = (bf16[136,256]{1,0:T(8,128)(2,1)S(1)}, bf16[136,256]{1,0:T(8,128)(2,1)S(1)}, u32[]{:S(2)}, u32[]{:S(2)}) collective-permute-start(bf16[136,256]{1,0:T(8,128)(2,1)S(1)} %add_convert_fusion.1), channel_id=1, source_target_pairs={{0,8},{4,12},{8,0},{12,4},{16,24},{20,28},{24,16},{28,20},{1,9},{5... | collective-permute-start | bytes 208904 | tf_op jit(solution)/shard_map/ppermute | solution.py:248
  60.0 6.5 %collective-permute-start.4 = (bf16[136,256]{1,0:T(8,128)(2,1)S(1)}, bf16[136,256]{1,0:T(8,128)(2,1)S(1)}, u32[]{:S(2)}, u32[]{:S(2)}) collective-permute-start(bf16[136,256]{1,0:T(8,128)(2,1)S(1)} %add_convert_fusion.1), channel_id=1, source_target_pairs={{0,12},{4,8},{8,4},{12,0},{16,28},{20,24},{24,20},{28,16},{1,13},{... | collective-permute-start | bytes 208904 | tf_op jit(solution)/shard_map/ppermute | solution.py:248
  67.3 3.1 %collective-permute-start.6 = (bf16[256,256]{1,0:T(8,128)(2,1)S(1)}, bf16[256,256]{1,0:T(8,128)(2,1)S(1)}, u32[]{:S(2)}, u32[]{:S(2)}) collective-permute-start(bf16[256,256]{1,0:T(8,128)(2,1)S(1)} %shard_map.183), channel_id=1, source_target_pairs={{0,1},{1,0},{2,3},{3,2},{4,5},{5,4},{6,7},{7,6},{8,9},{9,8},{10,11... | collective-permute-start | bytes 393224 | tf_op jit(solution)/shard_map/ppermute | solution.py:248
  67.7 7.0 %collective-permute-start.5 = (bf16[136,256]{1,0:T(8,128)(2,1)S(1)}, bf16[136,256]{1,0:T(8,128)(2,1)S(1)}, u32[]{:S(2)}, u32[]{:S(2)}) collective-permute-start(bf16[136,256]{1,0:T(8,128)(2,1)S(1)} %add_add_fusion), channel_id=1, source_target_pairs={{0,16},{4,20},{8,24},{12,28},{16,0},{20,4},{24,8},{28,12},{1,17},{... | collective-permute-start | bytes 208904 | tf_op jit(solution)/shard_map/ppermute | solution.py:248
  70.4 4.3 %collective-permute-start.7 = (bf16[128,256]{1,0:T(8,128)(2,1)S(1)}, bf16[128,256]{1,0:T(8,128)(2,1)S(1)}, u32[]{:S(2)}, u32[]{:S(2)}) collective-permute-start(bf16[128,256]{1,0:T(8,128)(2,1)S(1)} %get-tuple-element.76), channel_id=1, source_target_pairs={{0,2},{1,3},{2,0},{3,1},{4,6},{5,7},{6,4},{7,5},{8,10},{9,11},{10,... | collective-permute-start | bytes 196616 | tf_op jit(solution)/shard_map/ppermute | solution.py:248
  72.2 2.6 %collective-permute-start.9 = (bf16[256,256]{1,0:T(8,128)(2,1)S(1)}, bf16[256,256]{1,0:T(8,128)(2,1)S(1)}, u32[]{:S(2)}, u32[]{:S(2)}) collective-permute-start(bf16[256,256]{1,0:T(8,128)(2,1)S(1)} %shard_map.185), channel_id=1, source_target_pairs={{0,1},{1,0},{2,3},{3,2},{4,5},{5,4},{6,7},{7,6},{8,9},{9,8},{10,11... | collective-permute-start | bytes 393224 | tf_op jit(solution)/shard_map/ppermute | solution.py:248
  72.6 4.6 %collective-permute-start.10 = (bf16[128,256]{1,0:T(8,128)(2,1)S(1)}, bf16[128,256]{1,0:T(8,128)(2,1)S(1)}, u32[]{:S(2)}, u32[]{:S(2)}) collective-permute-start(bf16[128,256]{1,0:T(8,128)(2,1)S(1)} %get-tuple-element.75), channel_id=1, source_target_pairs={{0,2},{1,3},{2,0},{3,1},{4,6},{5,7},{6,4},{7,5},{8,10},{9,11},{10,... | collective-permute-start | bytes 196616 | tf_op jit(solution)/shard_map/ppermute | solution.py:248
  74.7 2.5 %collective-permute-start.8 = (f32[136,256]{1,0:T(8,128)S(1)}, f32[136,256]{1,0:T(8,128)S(1)}, u32[]{:S(2)}, u32[]{:S(2)}) collective-permute-start(f32[136,256]{1,0:T(8,128)S(1)} %convert_add_fusion.1.mine_ref), channel_id=1, source_target_pairs={{0,1},{1,0},{2,3},{3,2},{4,5},{5,4},{6,7},{7,6},{8,9},{9,8},{10,11... | collective-permute-start | bytes 417800 | tf_op jit(solution)/shard_map/ppermute | solution.py:248

commit v4 on v3

--- a/solution.py
+++ b/solution.py
@@ -164,44 +164,36 @@
 
 
 def decode_kernel(
-    rep_ref, ends_ref, gather_ref, target_ref, w1_ref, b1_ref, w2_ref, rows_ref, d_pre_ref, keep_ref, send_ref
+    rep_ref, ends_ref, gather_ref, scatter_ref, target_ref, w1_ref, b1_ref, w2_ref,
+    grads_hbm, weights_ref, grads_ref, sem,
 ):
-    queries = d_pre_ref.shape[0]
     rows = dot(gather_ref[...], ends_ref[...])
-    rows_ref[...] = rows.astype(BF16)
-    z = (rows[:queries] * rows[queries:]).astype(BF16)
-    pre = dot(z, w1_ref[...]) + b1_ref[...]
+    queries = rows.shape[0] // 2
+    head, tail = rows[:queries], rows[queries:]
+    z = (head * tail).astype(BF16)
+    w1 = w1_ref[...]
+    pre = dot(z, w1) + b1_ref[...]
     sig = jax.nn.sigmoid(pre)
     hidden = (pre * sig).astype(BF16).astype(F32)
     w2 = w2_ref[...].astype(F32)
     logit = jnp.sum(hidden * w2, axis=1, keepdims=True)
     dlogit = jax.nn.sigmoid(logit) - target_ref[...]
     d_pre = (dlogit * w2 * (sig * (1.0 + pre * (1.0 - sig)))).astype(BF16)
-    d_pre_ref[...] = d_pre
+    dz = dot(d_pre, w1, ((1,), (1,)))
+    grads = jnp.concatenate([dz * tail, dz * head], axis=0).astype(BF16)
+    copies = store(
+        lambda at, size: dot(scatter_ref[at:at + size, :], grads).astype(BF16), grads_ref, grads_hbm, sem, CHUNKS
+    )
     grad = dot(z, d_pre, ((0,), (0,)))
     half = grad.shape[0] // 2
     odd = (rep_ref[0] & 1) == 1
     low, high = grad[:half], grad[half:]
-    keep_ref[:half] = jnp.where(odd, high, low)
-    send_ref[:half] = jnp.where(odd, low, high)
     bias = jnp.sum(d_pre.astype(F32), axis=0, keepdims=True)
     outer = jnp.sum(hidden * dlogit, axis=0, keepdims=True)
-    first = iota((keep_ref.shape[0] - half, keep_ref.shape[1]), 0)
+    first = iota((weights_ref.shape[0] // 2 - half, grad.shape[1]), 0)
     aux = jnp.where(first == 0, bias, jnp.where(first == 1, outer, 0.0))
-    keep_ref[half:] = aux
-    send_ref[half:] = aux
-
-
-def grads_kernel(rows_ref, d_pre_ref, w1_ref, grads_ref):
-    queries = d_pre_ref.shape[0]
-    dz = dot(d_pre_ref[...], w1_ref[...], ((1,), (1,)))
-    grads_ref[:queries, :] = (dz * rows_ref[queries:, :].astype(F32)).astype(BF16)
-    grads_ref[queries:, :] = (dz * rows_ref[:queries, :].astype(F32)).astype(BF16)
-
-
-def place_kernel(grads_ref, scatter_ref, out_hbm, out_ref, sem):
-    grads = grads_ref[...]
-    wait(store(lambda at, size: dot(scatter_ref[at:at + size, :], grads).astype(BF16), out_ref, out_hbm, sem, CHUNKS))
+    weights_ref[...] = jnp.concatenate([jnp.where(odd, high, low), aux, jnp.where(odd, low, high), aux], axis=0)
+    wait(copies)
 
 
 def final_kernel(rep_ref, mine_ref, other_ref, keep_ref, *refs):
@@ -330,26 +322,21 @@
         scratch=(pltpu.VMEM((1, queries), I32), pltpu.SemaphoreType.DMA((4,))),
     )
     half = width // 2
-    rows, d_pre, keep, send = call(
+    placed, weights = call(
         decode_kernel,
-        [((ends, width), BF16), ((queries, width), BF16), ((half + 8, width), F32), ((half + 8, width), F32)],
-        rep, fetched, gather, target, w1, b1, w2, scalar=True,
-    )
-    weights = keep + swap(send, "rep", 1)
-    (grads,) = call(grads_kernel, [((ends, width), BF16)], rows, d_pre, w1)
-    grads, weights = lax.optimization_barrier((grads, weights))
+        [((slots, width), BF16), ((2 * (half + 8), width), F32)],
+        rep, fetched, gather, scatter, target, w1, b1, w2,
+        scalar=True,
+        hbm_out=(0,),
+        scratch=(pltpu.VMEM((slots, width), BF16), pltpu.SemaphoreType.DMA((CHUNKS,))),
+    )
+    back = exchange(placed.reshape(n_dom, cap, width), "dom").reshape(-1, width)
     step = 2
     while step < n_rep:
         weights = reduce_pairs(weights, "rep", step)
         step *= 2
-    (placed,) = call(
-        place_kernel,
-        [((slots, width), BF16)],
-        grads, scatter,
-        hbm_out=(0,),
-        scratch=(pltpu.VMEM((slots, width), BF16), pltpu.SemaphoreType.DMA((CHUNKS,))),
-    )
-    back = exchange(placed.reshape(n_dom, cap, width), "dom").reshape(-1, width)
+    keep, send = jnp.split(weights, 2, axis=0)
+    weights = keep + swap(send, "rep", 1)
     step = 1
     while 4 * step <= n_dom // 2:
         weights = reduce_fours(weights, "dom", step)

time: 78.5 us -> 76.6 us (0.976)
  waiting for transfers between devices: 28.4 us -> 26.6 us
    ppermute x11, waiting for transfers between devices: 13.4 us -> 12.1 us  [swap(): lax.ppermute(x, axis, [(i, i ^ mask) for i in range(lax.axis_size(axis))])]
    pallas_call x14 -> x12, Pallas kernels: 13.7 us -> 13.7 us  [call(): pl.pallas_call(kernel, out_shape=[(pltpu.HBM if i in far_out else pltpu.V...]
  transfers between devices with their start and end apart: 14 -> 14, of which waited for: 10 -> 9; matrix products, arithmetic and copies ran while one was open for 1% -> 1% of each run, Pallas kernels for 8% -> 7%
where the time goes in v4:
time: 76.6 us; the launch traced here: 76.1 us
  waiting for transfers between devices  26.6 us (35%)
  starting transfers between devices  24.5 us (32%)
  Pallas kernels  13.7 us (18%)
  blocking collectives  9.76 us (13%)
  between operations  0.83 us (1%)
    all_to_all x3, waiting for transfers between devices, exchange(): return lax.all_to_all(x, axis, split_axis=0, concat_axis=0, tiled=True)  14.5 us
    all_to_all x3, starting transfers between devices, exchange(): return lax.all_to_all(x, axis, split_axis=0, concat_axis=0, tiled=True)  14.4 us
    pallas_call x12, Pallas kernels, call(): pl.pallas_call(kernel, out_shape=[(pltpu.HBM if i in far_out else pltpu.V...  13.7 us
    ppermute x11, waiting for transfers between devices, swap(): lax.ppermute(x, axis, [(i, i ^ mask) for i in range(lax.axis_size(axis))])  12.1 us
    ppermute x11, starting transfers between devices, swap(): lax.ppermute(x, axis, [(i, i ^ mask) for i in range(lax.axis_size(axis))])  10.1 us
    all_to_all x1, blocking collectives, exchange(): return lax.all_to_all(x, axis, split_axis=0, concat_axis=0, tiled=True)  9.76 us
  transfers between devices with their start and end apart: 14, of which 9 were waited for; matrix products, arithmetic and copies ran while one was open for 1% of the time, Pallas kernels for 7%

profile of v4, /device:TPU:0, one launch (start us, length us, event | category | flops | bytes accessed | tf_op | source)
XLA Modules:
  0.0 76.1 jit_solution(13116883983667327673)
XLA Ops:
  0.6 1.7 %shard_map.173 = (s32[8,128]{1,0:T(8,128)}, s32[1,512]{1,0:T(1,128)S(1)}) custom-call(s32[2,256]{1,0:T(2,128)} %bitcast.30, s32[2,256]{1,0:T(2,128)} %bitcast.31, s32[8,32]{1,0:T(8,128)} %halo_hbm.2), custom_call_target="tpu_custom_call" | custom-call | tf_op jit(solution)/shard_map/pallas_call | solution.py:229
  2.3 7.3 %all-to-all-start = ((s32[8,1,128]{2,1,0:T(1,128)}), s32[8,1,128]{2,1,0:T(1,128)S(1)}, u32[]{:S(2)}, u32[]{:S(2)}) async-start(s32[8,1,128]{2,1,0:T(1,128)} %bitcast.29), calls=%async_computation | async-start | bytes 8192 | tf_op jit(solution)/shard_map/all_to_all | solution.py:255
  9.6 3.0 %shard_map.174 = (f32[1024,256]{1,0:T(8,128)S(1)}, f32[1024,256]{1,0:T(8,128)S(1)}, bf16[1024,256]{1,0:T(8,128)(2,1)S(1)}, bf16[256,256]{1,0:T(8,128)(2,1)S(1)}, bf16[1024,256]{1,0:T(8,128)(2,1)S(1)}) custom-call(bf16[1024,256]{1,0:T(8,128)(2,1)} %feats_hbm.1, bf16[1024,1024]{1,0:T(8,128)(2,1)} %inner_hbm.1, bf16[256,256]{1,0:T(8,128)(2,1)} %self_hbm.1, ...), custom_call_target="tpu_custom_call" | custom-call | tf_op jit(solution)/shard_map/pallas_call | solution.py:229
  12.6 3.4 %all-to-all-done = s32[8,1,128]{2,1,0:T(1,128)S(1)} async-done(((s32[8,1,128]{2,1,0:T(1,128)}), s32[8,1,128]{2,1,0:T(1,128)S(1)}, u32[]{:S(2)}, u32[]{:S(2)}) %all-to-all-start) | async-done | bytes 4128 | tf_op jit(solution)/shard_map/all_to_all | solution.py:255
  16.0 1.0 %shard_map.175 = (bf16[256,256]{1,0:T(8,128)(2,1)S(1)}, s32[1024,1]{1,0:T(8,128)S(1)}) custom-call(s32[8,128]{1,0:T(8,128)S(1)} %bitcast.25, bf16[1024,256]{1,0:T(8,128)(2,1)S(1)} %get-tuple-element.37.history_ref), custom_call_target="tpu_custom_call" | custom-call | tf_op jit(solution)/shard_map/pallas_call | solution.py:229
  17.0 9.8 %all_to_all.26 = bf16[8,32,256]{2,1,0:T(8,128)(2,1)S(1)} all-to-all(bf16[8,32,256]{2,1,0:T(8,128)(2,1)S(1)} %bitcast.24), channel_id=1, replica_groups=mesh['dom'=8,'rep'=4] {'dom'}, dimensions={0} | all-to-all | bytes 262144 | tf_op jit(solution)/shard_map/all_to_all | solution.py:255
  26.7 1.8 %shard_map.176 = (bf16[1024,256]{1,0:T(8,128)(2,1)}, bf16[1024,256]{1,0:T(8,128)(2,1)}) custom-call(s32[1024,1]{1,0:T(8,128)S(1)} %get-tuple-element.38.ids_ref, f32[1024,256]{1,0:T(8,128)S(1)} %get-tuple-element.39.agg_ref, f32[1024,256]{1,0:T(8,128)S(1)} %get-tuple-element.40.base_ref, bf16[256,256]{1,0:T(8,128)(2,1)S(1)} %bitcast.23, ...), custom_call_target="tpu_custom_call" | custom-call | tf_op jit(solution)/shard_map/pallas_call | solution.py:229
  28.5 3.5 %all-to-all-start.2 = ((bf16[8,128,256]{2,1,0:T(8,128)(2,1)}), bf16[8,128,256]{2,1,0:T(8,128)(2,1)S(1)}, u32[]{:S(2)}, u32[]{:S(2)}) async-start(bf16[8,128,256]{2,1,0:T(8,128)(2,1)} %bitcast.28), calls=%async_computation.2 | async-start | bytes 1048576 | tf_op jit(solution)/shard_map/all_to_all | solution.py:255
  32.6 1.1 %shard_map.177 = (bf16[512,1024]{1,0:T(8,128)(2,1)S(1)}, bf16[1024,512]{1,0:T(8,128)(2,1)S(1)}, f32[256,1]{1,0:T(8,128)S(1)}, bf16[256,256]{1,0:T(8,128)(2,1)S(1...) custom-call(s32[1,512]{1,0:T(1,128)S(1)} %get-tuple-element.46.place_ref, s32[1,256]{1,0:T(1,128)} %bitcast.33, ...), custom_call_target="tpu_custom_call" | custom-call | tf_op jit(solution)/shard_map/pallas_call | solution.py:229
  33.7 11.1 %all-to-all-done.2 = bf16[8,128,256]{2,1,0:T(8,128)(2,1)S(1)} async-done(((bf16[8,128,256]{2,1,0:T(8,128)(2,1)}), bf16[8,128,256]{2,1,0:T(8,128)(2,1)S(1)}, u32[]{:S(2)}, u32[]{:S(2)}) %all-to-all-start.2) | async-done | bytes 524320 | tf_op jit(solution)/shard_map/all_to_all | solution.py:255
  44.8 2.4 %shard_map.178 = (bf16[1024,256]{1,0:T(8,128)(2,1)}, f32[272,256]{1,0:T(8,128)S(1)}) custom-call(s32[1]{0:T(128)} %bitcast.8.rep_ref, bf16[1024,256]{1,0:T(8,128)(2,1)S(1)} %bitcast.22, bf16[512,1024]{1,0:T(8,128)(2,1)S(1)} %get-tuple-element.47.gather_ref, bf16[1024,512]{1,0:T(8,128)(2,1)S(1)} %get-tuple-element.48.scatter_ref, ...), custom_call_target="tpu_custom_call" | custom-call | tf_op jit(solution)/shard_map/pallas_call | solution.py:229
  47.3 1.6 %collective-permute-start = (bf16[272,256]{1,0:T(8,128)(2,1)S(1)}, bf16[272,256]{1,0:T(8,128)(2,1)S(1)}, u32[]{:S(2)}, u32[]{:S(2)}) collective-permute-start(bf16[272,256]{1,0:T(8,128)(2,1)S(1)} %convert_element_type.42), channel_id=1, source_target_pairs={{0,2},{1,3},{2,0},{3,1},{4,6},{5,7},{6,4},{7,5},{8,10},{9,11},{10,... | collective-permute-start | bytes 417800 | tf_op jit(solution)/shard_map/ppermute | solution.py:240
  48.8 3.6 %all-to-all-start.3 = ((bf16[8,128,256]{2,1,0:T(8,128)(2,1)}), bf16[8,128,256]{2,1,0:T(8,128)(2,1)S(1)}, u32[]{:S(2)}, u32[]{:S(2)}) async-start(bf16[8,128,256]{2,1,0:T(8,128)(2,1)} %bitcast.27), calls=%async_computation.3 | async-start | bytes 1048576 | tf_op jit(solution)/shard_map/all_to_all | solution.py:255
  52.6 1.3 %collective-permute-done.1 = f32[136,256]{1,0:T(8,128)S(1)} collective-permute-done((f32[136,256]{1,0:T(8,128)S(1)}, f32[136,256]{1,0:T(8,128)S(1)}, u32[]{:S(2)}, u32[]{:S(2)}) %collective-permute-start.1) | collective-permute-done | bytes 139296 | tf_op jit(solution)/shard_map/ppermute | solution.py:240
  53.9 2.1 %collective-permute-start.2 = (bf16[136,256]{1,0:T(8,128)(2,1)S(1)}, bf16[136,256]{1,0:T(8,128)(2,1)S(1)}, u32[]{:S(2)}, u32[]{:S(2)}) collective-permute-start(bf16[136,256]{1,0:T(8,128)(2,1)S(1)} %fusion), channel_id=1, source_target_pairs={{0,4},{4,0},{8,12},{12,8},{16,20},{20,16},{24,28},{28,24},{1,5},{5... | collective-permute-start | bytes 208904 | tf_op jit(solution)/shard_map/ppermute | solution.py:240
  56.0 1.5 %collective-permute-start.3 = (bf16[136,256]{1,0:T(8,128)(2,1)S(1)}, bf16[136,256]{1,0:T(8,128)(2,1)S(1)}, u32[]{:S(2)}, u32[]{:S(2)}) collective-permute-start(bf16[136,256]{1,0:T(8,128)(2,1)S(1)} %fusion), channel_id=1, source_target_pairs={{0,8},{4,12},{8,0},{12,4},{16,24},{20,28},{24,16},{28,20},{1,9},{5... | collective-permute-start | bytes 208904 | tf_op jit(solution)/shard_map/ppermute | solution.py:240
  58.3 1.8 %collective-permute-done.2 = bf16[136,256]{1,0:T(8,128)(2,1)S(1)} collective-permute-done((bf16[136,256]{1,0:T(8,128)(2,1)S(1)}, bf16[136,256]{1,0:T(8,128)(2,1)S(1)}, u32[]{:S(2)}, u32[]{:S(2)}) %collective-permute-start.2) | collective-permute-done | bytes 69664 | tf_op jit(solution)/shard_map/ppermute | solution.py:240
  60.0 4.9 %collective-permute-done.3 = bf16[136,256]{1,0:T(8,128)(2,1)S(1)} collective-permute-done((bf16[136,256]{1,0:T(8,128)(2,1)S(1)}, bf16[136,256]{1,0:T(8,128)(2,1)S(1)}, u32[]{:S(2)}, u32[]{:S(2)}) %collective-permute-start.3) | collective-permute-done | bytes 69664 | tf_op jit(solution)/shard_map/ppermute | solution.py:240
  65.0 1.1 %collective-permute-done.4 = bf16[136,256]{1,0:T(8,128)(2,1)S(1)} collective-permute-done((bf16[136,256]{1,0:T(8,128)(2,1)S(1)}, bf16[136,256]{1,0:T(8,128)(2,1)S(1)}, u32[]{:S(2)}, u32[]{:S(2)}) %collective-permute-start.4) | collective-permute-done | bytes 69664 | tf_op jit(solution)/shard_map/ppermute | solution.py:240
  66.8 2.4 %collective-permute-start.5 = (bf16[136,256]{1,0:T(8,128)(2,1)S(1)}, bf16[136,256]{1,0:T(8,128)(2,1)S(1)}, u32[]{:S(2)}, u32[]{:S(2)}) collective-permute-start(bf16[136,256]{1,0:T(8,128)(2,1)S(1)} %add_add_fusion), channel_id=1, source_target_pairs={{0,16},{4,20},{8,24},{12,28},{16,0},{20,4},{24,8},{28,12},{1,17},{... | collective-permute-start | bytes 208904 | tf_op jit(solution)/shard_map/ppermute | solution.py:240
  70.6 1.6 %collective-permute-start.10 = (bf16[128,256]{1,0:T(8,128)(2,1)S(1)}, bf16[128,256]{1,0:T(8,128)(2,1)S(1)}, u32[]{:S(2)}, u32[]{:S(2)}) collective-permute-start(bf16[128,256]{1,0:T(8,128)(2,1)S(1)} %get-tuple-element.67), channel_id=1, source_target_pairs={{0,2},{1,3},{2,0},{3,1},{4,6},{5,7},{6,4},{7,5},{8,10},{9,11},{10,... | collective-permute-start | bytes 196616 | tf_op jit(solution)/shard_map/ppermute | solution.py:240
  72.2 1.7 %collective-permute-done.5 = bf16[136,256]{1,0:T(8,128)(2,1)S(1)} collective-permute-done((bf16[136,256]{1,0:T(8,128)(2,1)S(1)}, bf16[136,256]{1,0:T(8,128)(2,1)S(1)}, u32[]{:S(2)}, u32[]{:S(2)}) %collective-permute-start.5) | collective-permute-done | bytes 69664 | tf_op jit(solution)/shard_map/ppermute | solution.py:240
  74.1 1.1 %collective-permute-done.10.refs_1_ = bf16[128,256]{1,0:T(8,128)(2,1)S(1)} collective-permute-done((bf16[128,256]{1,0:T(8,128)(2,1)S(1)}, bf16[128,256]{1,0:T(8,128)(2,1)S(1)}, u32[]{:S(2)}, u32[]{:S(2)}) %collective-permute-start.10) | collective-permute-done | bytes 65568 | tf_op jit(solution)/shard_map/ppermute | solution.py:240
  75.3 0.8 %shard_map.184 = (f32[256,256]{1,0:T(8,128)}, f32[256,256]{1,0:T(8,128)}, f32[1,256]{1,0:T(1,128)}, f32[1,256]{1,0:T(1,128)}) custom-call(s32[1]{0:T(128)} %bitcast.8.rep_ref, f32[136,256]{1,0:T(8,128)S(1)} %convert_add_fusion.2.mine_ref, f32[136,256]{1,0:T(8,128)S(1)} %collective-permute-done.8.other_ref, f32[256,256]{1,0:T(8,128)S(1)} %convert_add_fusion.1.keep_ref, ...), custom_call_target="tpu_custom_call" | custom-call | tf_op jit(solution)/shard_map/pallas_call | solution.py:229
  (29 shorter events, 3.9 us)
Async XLA Ops:
  2.3 13.7 %all-to-all-start = ((s32[8,1,128]{2,1,0:T(1,128)}), s32[8,1,128]{2,1,0:T(1,128)S(1)}, u32[]{:S(2)}, u32[]{:S(2)}) async-start(s32[8,1,128]{2,1,0:T(1,128)} %bitcast.29), calls=%async_computation | async-start | bytes 8192 | tf_op jit(solution)/shard_map/all_to_all | solution.py:255
  26.7 5.3 %copy-start = (bf16[256]{0:T(256)(128)(2,1)S(1)}, bf16[256]{0:T(256)(128)(2,1)}, u32[]{:S(2)}) copy-start(bf16[256]{0:T(256)(128)(2,1)} %param.27) | copy-start | bytes 1540
  28.5 16.3 %all-to-all-start.2 = ((bf16[8,128,256]{2,1,0:T(8,128)(2,1)}), bf16[8,128,256]{2,1,0:T(8,128)(2,1)S(1)}, u32[]{:S(2)}, u32[]{:S(2)}) async-start(bf16[8,128,256]{2,1,0:T(8,128)(2,1)} %bitcast.28), calls=%async_computation.2 | async-start | bytes 1048576 | tf_op jit(solution)/shard_map/all_to_all | solution.py:255
  47.3 5.2 %collective-permute-start = (bf16[272,256]{1,0:T(8,128)(2,1)S(1)}, bf16[272,256]{1,0:T(8,128)(2,1)S(1)}, u32[]{:S(2)}, u32[]{:S(2)}) collective-permute-start(bf16[272,256]{1,0:T(8,128)(2,1)S(1)} %convert_element_type.42), channel_id=1, source_target_pairs={{0,2},{1,3},{2,0},{3,1},{4,6},{5,7},{6,4},{7,5},{8,10},{9,11},{10,... | collective-permute-start | bytes 417800 | tf_op jit(solution)/shard_map/ppermute | solution.py:240
  48.8 17.3 %all-to-all-start.3 = ((bf16[8,128,256]{2,1,0:T(8,128)(2,1)}), bf16[8,128,256]{2,1,0:T(8,128)(2,1)S(1)}, u32[]{:S(2)}, u32[]{:S(2)}) async-start(bf16[8,128,256]{2,1,0:T(8,128)(2,1)} %bitcast.27), calls=%async_computation.3 | async-start | bytes 1048576 | tf_op jit(solution)/shard_map/all_to_all | solution.py:255
  52.5 1.4 %collective-permute-start.1 = (f32[136,256]{1,0:T(8,128)S(1)}, f32[136,256]{1,0:T(8,128)S(1)}, u32[]{:S(2)}, u32[]{:S(2)}) collective-permute-start(f32[136,256]{1,0:T(8,128)S(1)} %split.17), channel_id=1, source_target_pairs={{0,1},{1,0},{2,3},{3,2},{4,5},{5,4},{6,7},{7,6},{8,9},{9,8},{10,11... | collective-permute-start | bytes 417800 | tf_op jit(solution)/shard_map/ppermute | solution.py:240
  53.9 6.1 %collective-permute-start.2 = (bf16[136,256]{1,0:T(8,128)(2,1)S(1)}, bf16[136,256]{1,0:T(8,128)(2,1)S(1)}, u32[]{:S(2)}, u32[]{:S(2)}) collective-permute-start(bf16[136,256]{1,0:T(8,128)(2,1)S(1)} %fusion), channel_id=1, source_target_pairs={{0,4},{4,0},{8,12},{12,8},{16,20},{20,16},{24,28},{28,24},{1,5},{5... | collective-permute-start | bytes 208904 | tf_op jit(solution)/shard_map/ppermute | solution.py:240
  56.0 9.0 %collective-permute-start.3 = (bf16[136,256]{1,0:T(8,128)(2,1)S(1)}, bf16[136,256]{1,0:T(8,128)(2,1)S(1)}, u32[]{:S(2)}, u32[]{:S(2)}) collective-permute-start(bf16[136,256]{1,0:T(8,128)(2,1)S(1)} %fusion), channel_id=1, source_target_pairs={{0,8},{4,12},{8,0},{12,4},{16,24},{20,28},{24,16},{28,20},{1,9},{5... | collective-permute-start | bytes 208904 | tf_op jit(solution)/shard_map/ppermute | solution.py:240
  57.5 8.6 %collective-permute-start.4 = (bf16[136,256]{1,0:T(8,128)(2,1)S(1)}, bf16[136,256]{1,0:T(8,128)(2,1)S(1)}, u32[]{:S(2)}, u32[]{:S(2)}) collective-permute-start(bf16[136,256]{1,0:T(8,128)(2,1)S(1)} %fusion), channel_id=1, source_target_pairs={{0,12},{4,8},{8,4},{12,0},{16,28},{20,24},{24,20},{28,16},{1,13},{... | collective-permute-start | bytes 208904 | tf_op jit(solution)/shard_map/ppermute | solution.py:240
  66.4 2.8 %collective-permute-start.6 = (bf16[256,256]{1,0:T(8,128)(2,1)S(1)}, bf16[256,256]{1,0:T(8,128)(2,1)S(1)}, u32[]{:S(2)}, u32[]{:S(2)}) collective-permute-start(bf16[256,256]{1,0:T(8,128)(2,1)S(1)} %shard_map.181), channel_id=1, source_target_pairs={{0,1},{1,0},{2,3},{3,2},{4,5},{5,4},{6,7},{7,6},{8,9},{9,8},{10,11... | collective-permute-start | bytes 393224 | tf_op jit(solution)/shard_map/ppermute | solution.py:240
  66.8 7.0 %collective-permute-start.5 = (bf16[136,256]{1,0:T(8,128)(2,1)S(1)}, bf16[136,256]{1,0:T(8,128)(2,1)S(1)}, u32[]{:S(2)}, u32[]{:S(2)}) collective-permute-start(bf16[136,256]{1,0:T(8,128)(2,1)S(1)} %add_add_fusion), channel_id=1, source_target_pairs={{0,16},{4,20},{8,24},{12,28},{16,0},{20,4},{24,8},{28,12},{1,17},{... | collective-permute-start | bytes 208904 | tf_op jit(solution)/shard_map/ppermute | solution.py:240
  69.3 4.6 %collective-permute-start.7 = (bf16[128,256]{1,0:T(8,128)(2,1)S(1)}, bf16[128,256]{1,0:T(8,128)(2,1)S(1)}, u32[]{:S(2)}, u32[]{:S(2)}) collective-permute-start(bf16[128,256]{1,0:T(8,128)(2,1)S(1)} %get-tuple-element.68), channel_id=1, source_target_pairs={{0,2},{1,3},{2,0},{3,1},{4,6},{5,7},{6,4},{7,5},{8,10},{9,11},{10,... | collective-permute-start | bytes 196616 | tf_op jit(solution)/shard_map/ppermute | solution.py:240
  70.2 3.8 %collective-permute-start.9 = (bf16[256,256]{1,0:T(8,128)(2,1)S(1)}, bf16[256,256]{1,0:T(8,128)(2,1)S(1)}, u32[]{:S(2)}, u32[]{:S(2)}) collective-permute-start(bf16[256,256]{1,0:T(8,128)(2,1)S(1)} %shard_map.183), channel_id=1, source_target_pairs={{0,1},{1,0},{2,3},{3,2},{4,5},{5,4},{6,7},{7,6},{8,9},{9,8},{10,11... | collective-permute-start | bytes 393224 | tf_op jit(solution)/shard_map/ppermute | solution.py:240
  70.6 4.6 %collective-permute-start.10 = (bf16[128,256]{1,0:T(8,128)(2,1)S(1)}, bf16[128,256]{1,0:T(8,128)(2,1)S(1)}, u32[]{:S(2)}, u32[]{:S(2)}) collective-permute-start(bf16[128,256]{1,0:T(8,128)(2,1)S(1)} %get-tuple-element.67), channel_id=1, source_target_pairs={{0,2},{1,3},{2,0},{3,1},{4,6},{5,7},{6,4},{7,5},{8,10},{9,11},{10,... | collective-permute-start | bytes 196616 | tf_op jit(solution)/shard_map/ppermute | solution.py:240
  73.9 1.4 %collective-permute-start.8 = (f32[136,256]{1,0:T(8,128)S(1)}, f32[136,256]{1,0:T(8,128)S(1)}, u32[]{:S(2)}, u32[]{:S(2)}) collective-permute-start(f32[136,256]{1,0:T(8,128)S(1)} %convert_add_fusion.2.mine_ref), channel_id=1, source_target_pairs={{0,1},{1,0},{2,3},{3,2},{4,5},{5,4},{6,7},{7,6},{8,9},{9,8},{10,11... | collective-permute-start | bytes 417800 | tf_op jit(solution)/shard_map/ppermute | solution.py:240

commit v5 on v4

--- a/solution.py
+++ b/solution.py
@@ -12,6 +12,7 @@
 I32 = jnp.int32
 VMEM_BYTES = 24 * 1024 * 1024
 CHUNKS = 4
+SPARE = 8
 X_PARTS = 2
 
 
@@ -77,7 +78,7 @@
         copy.wait()
 
 
-def request_kernel(cap, owner_hbm, local_hbm, halo_hbm, word_ref, place_ref, owner_ref, local_ref, halo_ref, sem):
+def request_kernel(cap, joint, owner_hbm, local_hbm, halo_hbm, word_ref, place_ref, owner_ref, local_ref, halo_ref, sem):
     wait(loads((owner_hbm, local_hbm, halo_hbm), (owner_ref, local_ref, halo_ref), sem))
     n = word_ref.shape[0]
     owner = jnp.concatenate([owner_ref[0:1, :], owner_ref[1:2, :]], axis=1)
@@ -92,8 +93,9 @@
     wanted = jnp.where(match, local, 0)
     ids = exact_dot(at_slot, wanted, ((1,), (1,)), True).astype(I32)
     word_ref[...] = ids
-    halo = halo_ref.shape[1]
-    word_ref[:, :halo] = ids[:, :halo] + lax.shift_left(halo_ref[...], 16)
+    if joint:
+        halo = halo_ref.shape[1]
+        word_ref[:, :halo] = ids[:, :halo] + lax.shift_left(halo_ref[...], 16)
 
 
 def store(value, buffer, out_ref, sem, chunks):
@@ -150,14 +152,42 @@
     out_ref[...] = dot(ones_where(ids == iota((ids.shape[0], nodes), 1)), history_ref[...]).astype(BF16)
 
 
-def embed_kernel(ids_ref, agg_ref, base_ref, halo_ref, adj_ref, w_ref, embed_hbm, out_hbm, embed_ref, out_ref, embed_sem, out_sem):
-    agg = (agg_ref[...] + dot(adj_ref[...], halo_ref[...])).astype(BF16)
+def halo_and_ids_kernel(asked_ref, wanted_ref, history_ref, out_ref):
+    n, cap = asked_ref.shape
+    ids = as_column(asked_ref[...], cap)
+    rows = dot(ones_where(ids == iota((n * cap, history_ref.shape[0]), 1)), history_ref[...])
+    wanted = wanted_ref[...]
+    spare, half = out_ref.shape[1] - cap, out_ref.shape[2] // 2
+    blank = jnp.zeros((n, half - wanted.shape[1]), I32)
+    parts = [lax.shift_right_logical(wanted, 8), blank, wanted & 255, blank]
+    pairs = jnp.concatenate([part for part in parts if part.shape[1]], axis=1).astype(F32)
+    for i in range(n):
+        tail = jnp.broadcast_to(pairs[i:i + 1], (spare, 2 * half))
+        out_ref[i] = jnp.concatenate([rows[i * cap:(i + 1) * cap], tail], axis=0).astype(BF16)
+
+
+def embed_kernel(
+    cap, agg_ref, base_ref, halo_ref, adj_ref, w_ref, ids_ref,
+    embed_hbm, out_hbm, word_ref, embed_ref, out_ref, embed_sem, out_sem,
+):
+    if cap:
+        n, rows, width = halo_ref.shape
+        chunks = [halo_ref[i].astype(F32) for i in range(n)]
+        halo = jnp.concatenate([chunk[:rows - SPARE] for chunk in chunks], axis=0).astype(BF16)
+        pairs = jnp.concatenate([chunk[rows - SPARE:rows - SPARE + 1] for chunk in chunks], axis=0)
+        half = width // 2
+        word = (pairs[:, :cap] * 256.0 + pairs[:, half:half + cap]).astype(I32)
+        word_ref[...] = word
+        ids = as_column(word, cap)
+    else:
+        halo, ids = halo_ref[...], ids_ref[...]
+        word_ref[...] = jnp.zeros(word_ref.shape, I32)
+    agg = (agg_ref[...] + dot(adj_ref[...], halo)).astype(BF16)
     embed = jnp.maximum(base_ref[...] + dot(agg, w_ref[...]), 0.0).astype(BF16)
     copies = store(lambda at, size: embed[at:at + size], embed_ref, embed_hbm, embed_sem, 1)
 
     def fetched(at, size):
-        mask = ones_where(ids_ref[at:at + size, :] == iota((size, embed.shape[0]), 1))
-        return dot(mask, embed).astype(BF16)
+        return dot(ones_where(ids[at:at + size, :] == iota((size, embed.shape[0]), 1)), embed).astype(BF16)
 
     copies += store(fetched, out_ref, out_hbm, out_sem, CHUNKS)
     wait(copies)
@@ -269,18 +299,22 @@
     rep = lax.axis_index("rep").astype(I32).reshape(1)
 
     ends = 2 * queries
+    ride = cap_halo % 16 == 0 and cap <= width // 2
+    if ride:
+        asked = exchange(halo_rows, "dom")
     word, place = call(
-        functools.partial(request_kernel, cap),
+        functools.partial(request_kernel, cap, not ride),
         [((n_dom, cap), I32), ((1, ends), I32)],
         edge_owner.T, edge_rows.T, halo_rows,
-        far_out=(0,),
+        far_out=() if ride else (0,),
         hbm_in=(0, 1, 2),
         scratch=(
             pltpu.VMEM((2, queries), I32), pltpu.VMEM((2, queries), I32), pltpu.VMEM(halo_rows.shape, I32),
             pltpu.SemaphoreType.DMA((3,)),
         ),
     )
-    word = exchange(word, "dom")
+    if not ride:
+        word = exchange(word, "dom")
     agg, base, adj_halo, w_nbr, history = call(
         inner_kernel,
         [
@@ -294,22 +328,30 @@
             pltpu.VMEM((1, width), F32), pltpu.SemaphoreType.DMA((7,)),
         ),
     )
-    halo, ids = call(
-        functools.partial(halo_kernel, cap_halo, cap),
-        [((n_dom * cap_halo, width), BF16), ((slots, 1), I32)],
-        word, history,
-    )
-    halo = exchange(halo.reshape(n_dom, cap_halo, width), "dom").reshape(-1, width)
-    embed, fetched = call(
-        embed_kernel,
-        [((nodes, width), BF16), ((slots, width), BF16)],
-        ids, agg, base, halo, adj_halo, w_nbr,
+    if ride:
+        (halo,) = call(
+            halo_and_ids_kernel, [((n_dom, cap_halo + SPARE, width), BF16)], asked, word, history
+        )
+        halo = exchange(halo, "dom")
+        ids = jnp.zeros((8, 128), I32)
+    else:
+        halo, ids = call(
+            functools.partial(halo_kernel, cap_halo, cap),
+            [((n_dom * cap_halo, width), BF16), ((slots, 1), I32)],
+            word, history,
+        )
+        halo = exchange(halo.reshape(n_dom, cap_halo, width), "dom").reshape(-1, width)
+    embed, fetched, got = call(
+        functools.partial(embed_kernel, cap if ride else 0),
+        [((nodes, width), BF16), ((slots, width), BF16), ((n_dom, cap), I32)],
+        agg, base, halo, adj_halo, w_nbr, ids,
         hbm_out=(0, 1),
         scratch=(
             pltpu.VMEM((nodes, width), BF16), pltpu.VMEM((slots, width), BF16),
             pltpu.SemaphoreType.DMA((1,)), pltpu.SemaphoreType.DMA((CHUNKS,)),
         ),
     )
+    word = got if ride else word
     fetched = exchange(fetched.reshape(n_dom, cap, width), "dom").reshape(-1, width)
     gather, scatter, target, w1, b1, w2 = call(
         edge_mask_kernel,

time: 76.6 us -> 75.9 us (level)
  blocking collectives: 9.76 us -> 11.1 us
  waiting for transfers between devices: 26.6 us -> 25.5 us
  Pallas kernels: 13.7 us -> 12.8 us
    all_to_all x1, blocking collectives: 9.76 us -> 11.1 us  [exchange(): return lax.all_to_all(x, axis, split_axis=0, concat_axis=0, tiled=True)]
    all_to_all x3, waiting for transfers between devices: 14.5 us -> 13.4 us  [exchange(): return lax.all_to_all(x, axis, split_axis=0, concat_axis=0, tiled=True)]
    pallas_call x12, Pallas kernels: 13.7 us -> 12.8 us  [call(): pl.pallas_call(kernel, out_shape=[(pltpu.HBM if i in far_out else pltpu.V...]
  transfers between devices with their start and end apart: 14 -> 14, of which waited for: 9 -> 9; matrix products, arithmetic and copies ran while one was open for 1% -> 1% of each run, Pallas kernels for 7% -> 9%
where the time goes in v5:
time: 75.9 us; the launch traced here: 75.5 us
  waiting for transfers between devices  25.5 us (34%)
  starting transfers between devices  24.5 us (32%)
  Pallas kernels  12.8 us (17%)
  blocking collectives  11.1 us (15%)
  between operations  0.83 us (1%)
    all_to_all x3, starting transfers between devices, exchange(): return lax.all_to_all(x, axis, split_axis=0, concat_axis=0, tiled=True)  14.4 us
    all_to_all x3, waiting for transfers between devices, exchange(): return lax.all_to_all(x, axis, split_axis=0, concat_axis=0, tiled=True)  13.4 us
    pallas_call x12, Pallas kernels, call(): pl.pallas_call(kernel, out_shape=[(pltpu.HBM if i in far_out else pltpu.V...  12.8 us
    ppermute x11, waiting for transfers between devices, swap(): lax.ppermute(x, axis, [(i, i ^ mask) for i in range(lax.axis_size(axis))])  12.1 us
    all_to_all x1, blocking collectives, exchange(): return lax.all_to_all(x, axis, split_axis=0, concat_axis=0, tiled=True)  11.1 us
    ppermute x11, starting transfers between devices, swap(): lax.ppermute(x, axis, [(i, i ^ mask) for i in range(lax.axis_size(axis))])  10.1 us
  transfers between devices with their start and end apart: 14, of which 9 were waited for; matrix products, arithmetic and copies ran while one was open for 1% of the time, Pallas kernels for 9%

profile of v5, /device:TPU:0, one launch (start us, length us, event | category | flops | bytes accessed | tf_op | source)
XLA Modules:
  0.0 75.5 jit_solution(15400454084083190842)
XLA Ops:
  0.6 7.3 %all-to-all-start = ((s32[8,1,32]{2,1,0:T(1,128)}), s32[8,1,32]{2,1,0:T(1,128)S(1)}, u32[]{:S(2)}, u32[]{:S(2)}) async-start(s32[8,1,32]{2,1,0:T(1,128)} %bitcast.22), calls=%async_computation | async-start | bytes 8192 | tf_op jit(solution)/shard_map/all_to_all | solution.py:285
  7.9 1.1 %shard_map.174 = (s32[8,128]{1,0:T(8,128)S(1)}, s32[1,512]{1,0:T(1,128)S(1)}) custom-call(s32[2,256]{1,0:T(2,128)} %bitcast.23, s32[2,256]{1,0:T(2,128)} %bitcast.24, s32[8,32]{1,0:T(8,128)} %halo_hbm.3), custom_call_target="tpu_custom_call" | custom-call | tf_op jit(solution)/shard_map/pallas_call | solution.py:259
  9.0 3.0 %shard_map.173 = (f32[1024,256]{1,0:T(8,128)S(1)}, f32[1024,256]{1,0:T(8,128)S(1)}, bf16[1024,256]{1,0:T(8,128)(2,1)S(1)}, bf16[256,256]{1,0:T(8,128)(2,1)S(1)}, bf16[1024,256]{1,0:T(8,128)(2,1)S(1)}) custom-call(bf16[1024,256]{1,0:T(8,128)(2,1)} %feats_hbm.1, bf16[1024,1024]{1,0:T(8,128)(2,1)} %inner_hbm.1, bf16[256,256]{1,0:T(8,128)(2,1)} %self_hbm.1, ...), custom_call_target="tpu_custom_call" | custom-call | tf_op jit(solution)/shard_map/pallas_call | solution.py:259
  12.0 2.3 %all-to-all-done = s32[8,1,32]{2,1,0:T(1,128)S(1)} async-done(((s32[8,1,32]{2,1,0:T(1,128)}), s32[8,1,32]{2,1,0:T(1,128)S(1)}, u32[]{:S(2)}, u32[]{:S(2)}) %all-to-all-start) | async-done | bytes 1056 | tf_op jit(solution)/shard_map/all_to_all | solution.py:285
  14.9 11.1 %all_to_all.26.halo_ref = bf16[8,40,256]{2,1,0:T(8,128)(2,1)S(1)} all-to-all(bf16[8,40,256]{2,1,0:T(8,128)(2,1)S(1)} %shard_map.175), channel_id=1, replica_groups=mesh['dom'=8,'rep'=4] {'dom'}, dimensions={0} | all-to-all | bytes 327680 | tf_op jit(solution)/shard_map/all_to_all | solution.py:285
  26.0 1.9 %shard_map.176 = (bf16[1024,256]{1,0:T(8,128)(2,1)}, bf16[1024,256]{1,0:T(8,128)(2,1)}, s32[8,128]{1,0:T(8,128)S(1)}) custom-call(f32[1024,256]{1,0:T(8,128)S(1)} %get-tuple-element.35.agg_ref, f32[1024,256]{1,0:T(8,128)S(1)} %get-tuple-element.36.base_ref, bf16[8,40,256]{2,1,0:T(8,128)(2,1)S(1)} %all_to_all.26.halo_ref, ...), custom_call_target="tpu_custom_call" | custom-call | tf_op jit(solution)/shard_map/pallas_call | solution.py:259
  27.9 3.5 %all-to-all-start.2 = ((bf16[8,128,256]{2,1,0:T(8,128)(2,1)}), bf16[8,128,256]{2,1,0:T(8,128)(2,1)S(1)}, u32[]{:S(2)}, u32[]{:S(2)}) async-start(bf16[8,128,256]{2,1,0:T(8,128)(2,1)} %bitcast.21), calls=%async_computation.2 | async-start | bytes 1048576 | tf_op jit(solution)/shard_map/all_to_all | solution.py:285
  32.0 1.1 %shard_map.177 = (bf16[512,1024]{1,0:T(8,128)(2,1)S(1)}, bf16[1024,512]{1,0:T(8,128)(2,1)S(1)}, f32[256,1]{1,0:T(8,128)S(1)}, bf16[256,256]{1,0:T(8,128)(2,1)S(1...) custom-call(s32[1,512]{1,0:T(1,128)S(1)} %get-tuple-element.43.place_ref, s32[1,256]{1,0:T(1,128)} %bitcast.26, ...), custom_call_target="tpu_custom_call" | custom-call | tf_op jit(solution)/shard_map/pallas_call | solution.py:259
  33.1 11.1 %all-to-all-done.2 = bf16[8,128,256]{2,1,0:T(8,128)(2,1)S(1)} async-done(((bf16[8,128,256]{2,1,0:T(8,128)(2,1)}), bf16[8,128,256]{2,1,0:T(8,128)(2,1)S(1)}, u32[]{:S(2)}, u32[]{:S(2)}) %all-to-all-start.2) | async-done | bytes 524320 | tf_op jit(solution)/shard_map/all_to_all | solution.py:285
  44.2 2.4 %shard_map.178 = (bf16[1024,256]{1,0:T(8,128)(2,1)}, f32[272,256]{1,0:T(8,128)S(1)}) custom-call(s32[1]{0:T(128)} %bitcast.5.rep_ref, bf16[1024,256]{1,0:T(8,128)(2,1)S(1)} %bitcast.18, bf16[512,1024]{1,0:T(8,128)(2,1)S(1)} %get-tuple-element.44.gather_ref, bf16[1024,512]{1,0:T(8,128)(2,1)S(1)} %get-tuple-element.45.scatter_ref, ...), custom_call_target="tpu_custom_call" | custom-call | tf_op jit(solution)/shard_map/pallas_call | solution.py:259
  46.6 1.5 %collective-permute-start = (bf16[272,256]{1,0:T(8,128)(2,1)S(1)}, bf16[272,256]{1,0:T(8,128)(2,1)S(1)}, u32[]{:S(2)}, u32[]{:S(2)}) collective-permute-start(bf16[272,256]{1,0:T(8,128)(2,1)S(1)} %convert_element_type.42), channel_id=1, source_target_pairs={{0,2},{1,3},{2,0},{3,1},{4,6},{5,7},{6,4},{7,5},{8,10},{9,11},{10,... | collective-permute-start | bytes 417800 | tf_op jit(solution)/shard_map/ppermute | solution.py:270
  48.2 3.6 %all-to-all-start.3 = ((bf16[8,128,256]{2,1,0:T(8,128)(2,1)}), bf16[8,128,256]{2,1,0:T(8,128)(2,1)S(1)}, u32[]{:S(2)}, u32[]{:S(2)}) async-start(bf16[8,128,256]{2,1,0:T(8,128)(2,1)} %bitcast.20), calls=%async_computation.3 | async-start | bytes 1048576 | tf_op jit(solution)/shard_map/all_to_all | solution.py:285
  51.9 1.3 %collective-permute-done.1 = f32[136,256]{1,0:T(8,128)S(1)} collective-permute-done((f32[136,256]{1,0:T(8,128)S(1)}, f32[136,256]{1,0:T(8,128)S(1)}, u32[]{:S(2)}, u32[]{:S(2)}) %collective-permute-start.1) | collective-permute-done | bytes 139296 | tf_op jit(solution)/shard_map/ppermute | solution.py:270
  53.3 2.1 %collective-permute-start.2 = (bf16[136,256]{1,0:T(8,128)(2,1)S(1)}, bf16[136,256]{1,0:T(8,128)(2,1)S(1)}, u32[]{:S(2)}, u32[]{:S(2)}) collective-permute-start(bf16[136,256]{1,0:T(8,128)(2,1)S(1)} %fusion), channel_id=1, source_target_pairs={{0,4},{4,0},{8,12},{12,8},{16,20},{20,16},{24,28},{28,24},{1,5},{5... | collective-permute-start | bytes 208904 | tf_op jit(solution)/shard_map/ppermute | solution.py:270
  55.4 1.5 %collective-permute-start.3 = (bf16[136,256]{1,0:T(8,128)(2,1)S(1)}, bf16[136,256]{1,0:T(8,128)(2,1)S(1)}, u32[]{:S(2)}, u32[]{:S(2)}) collective-permute-start(bf16[136,256]{1,0:T(8,128)(2,1)S(1)} %fusion), channel_id=1, source_target_pairs={{0,8},{4,12},{8,0},{12,4},{16,24},{20,28},{24,16},{28,20},{1,9},{5... | collective-permute-start | bytes 208904 | tf_op jit(solution)/shard_map/ppermute | solution.py:270
  56.9 0.7 shard_map.179
  57.7 1.7 %collective-permute-done.2 = bf16[136,256]{1,0:T(8,128)(2,1)S(1)} collective-permute-done((bf16[136,256]{1,0:T(8,128)(2,1)S(1)}, bf16[136,256]{1,0:T(8,128)(2,1)S(1)}, u32[]{:S(2)}, u32[]{:S(2)}) %collective-permute-start.2) | collective-permute-done | bytes 69664 | tf_op jit(solution)/shard_map/ppermute | solution.py:270
  59.4 5.0 %collective-permute-done.3 = bf16[136,256]{1,0:T(8,128)(2,1)S(1)} collective-permute-done((bf16[136,256]{1,0:T(8,128)(2,1)S(1)}, bf16[136,256]{1,0:T(8,128)(2,1)S(1)}, u32[]{:S(2)}, u32[]{:S(2)}) %collective-permute-start.3) | collective-permute-done | bytes 69664 | tf_op jit(solution)/shard_map/ppermute | solution.py:270
  64.3 1.1 %collective-permute-done.4 = bf16[136,256]{1,0:T(8,128)(2,1)S(1)} collective-permute-done((bf16[136,256]{1,0:T(8,128)(2,1)S(1)}, bf16[136,256]{1,0:T(8,128)(2,1)S(1)}, u32[]{:S(2)}, u32[]{:S(2)}) %collective-permute-start.4) | collective-permute-done | bytes 69664 | tf_op jit(solution)/shard_map/ppermute | solution.py:270
  66.2 2.4 %collective-permute-start.5 = (bf16[136,256]{1,0:T(8,128)(2,1)S(1)}, bf16[136,256]{1,0:T(8,128)(2,1)S(1)}, u32[]{:S(2)}, u32[]{:S(2)}) collective-permute-start(bf16[136,256]{1,0:T(8,128)(2,1)S(1)} %add_add_fusion), channel_id=1, source_target_pairs={{0,16},{4,20},{8,24},{12,28},{16,0},{20,4},{24,8},{28,12},{1,17},{... | collective-permute-start | bytes 208904 | tf_op jit(solution)/shard_map/ppermute | solution.py:270
  70.0 1.5 %collective-permute-start.10 = (bf16[128,256]{1,0:T(8,128)(2,1)S(1)}, bf16[128,256]{1,0:T(8,128)(2,1)S(1)}, u32[]{:S(2)}, u32[]{:S(2)}) collective-permute-start(bf16[128,256]{1,0:T(8,128)(2,1)S(1)} %get-tuple-element.65), channel_id=1, source_target_pairs={{0,2},{1,3},{2,0},{3,1},{4,6},{5,7},{6,4},{7,5},{8,10},{9,11},{10,... | collective-permute-start | bytes 196616 | tf_op jit(solution)/shard_map/ppermute | solution.py:270
  71.5 1.7 %collective-permute-done.5 = bf16[136,256]{1,0:T(8,128)(2,1)S(1)} collective-permute-done((bf16[136,256]{1,0:T(8,128)(2,1)S(1)}, bf16[136,256]{1,0:T(8,128)(2,1)S(1)}, u32[]{:S(2)}, u32[]{:S(2)}) %collective-permute-start.5) | collective-permute-done | bytes 69664 | tf_op jit(solution)/shard_map/ppermute | solution.py:270
  73.4 1.1 %collective-permute-done.10.refs_1_ = bf16[128,256]{1,0:T(8,128)(2,1)S(1)} collective-permute-done((bf16[128,256]{1,0:T(8,128)(2,1)S(1)}, bf16[128,256]{1,0:T(8,128)(2,1)S(1)}, u32[]{:S(2)}, u32[]{:S(2)}) %collective-permute-start.10) | collective-permute-done | bytes 65568 | tf_op jit(solution)/shard_map/ppermute | solution.py:270
  74.7 0.8 %shard_map.184 = (f32[256,256]{1,0:T(8,128)}, f32[256,256]{1,0:T(8,128)}, f32[1,256]{1,0:T(1,128)}, f32[1,256]{1,0:T(1,128)}) custom-call(s32[1]{0:T(128)} %bitcast.5.rep_ref, f32[136,256]{1,0:T(8,128)S(1)} %convert_add_fusion.2.mine_ref, f32[136,256]{1,0:T(8,128)S(1)} %collective-permute-done.8.other_ref, f32[256,256]{1,0:T(8,128)S(1)} %convert_add_fusion.1.keep_ref, ...), custom_call_target="tpu_custom_call" | custom-call | tf_op jit(solution)/shard_map/pallas_call | solution.py:259
  (30 shorter events, 3.7 us)
Async XLA Ops:
  0.6 13.7 %all-to-all-start = ((s32[8,1,32]{2,1,0:T(1,128)}), s32[8,1,32]{2,1,0:T(1,128)S(1)}, u32[]{:S(2)}, u32[]{:S(2)}) async-start(s32[8,1,32]{2,1,0:T(1,128)} %bitcast.22), calls=%async_computation | async-start | bytes 8192 | tf_op jit(solution)/shard_map/all_to_all | solution.py:285
  14.9 16.6 %copy-start = (bf16[256]{0:T(256)(128)(2,1)S(1)}, bf16[256]{0:T(256)(128)(2,1)}, u32[]{:S(2)}) copy-start(bf16[256]{0:T(256)(128)(2,1)} %param.27) | copy-start | bytes 1540
  27.9 16.3 %all-to-all-start.2 = ((bf16[8,128,256]{2,1,0:T(8,128)(2,1)}), bf16[8,128,256]{2,1,0:T(8,128)(2,1)S(1)}, u32[]{:S(2)}, u32[]{:S(2)}) async-start(bf16[8,128,256]{2,1,0:T(8,128)(2,1)} %bitcast.21), calls=%async_computation.2 | async-start | bytes 1048576 | tf_op jit(solution)/shard_map/all_to_all | solution.py:285
  46.6 5.2 %collective-permute-start = (bf16[272,256]{1,0:T(8,128)(2,1)S(1)}, bf16[272,256]{1,0:T(8,128)(2,1)S(1)}, u32[]{:S(2)}, u32[]{:S(2)}) collective-permute-start(bf16[272,256]{1,0:T(8,128)(2,1)S(1)} %convert_element_type.42), channel_id=1, source_target_pairs={{0,2},{1,3},{2,0},{3,1},{4,6},{5,7},{6,4},{7,5},{8,10},{9,11},{10,... | collective-permute-start | bytes 417800 | tf_op jit(solution)/shard_map/ppermute | solution.py:270
  48.2 17.3 %all-to-all-start.3 = ((bf16[8,128,256]{2,1,0:T(8,128)(2,1)}), bf16[8,128,256]{2,1,0:T(8,128)(2,1)S(1)}, u32[]{:S(2)}, u32[]{:S(2)}) async-start(bf16[8,128,256]{2,1,0:T(8,128)(2,1)} %bitcast.20), calls=%async_computation.3 | async-start | bytes 1048576 | tf_op jit(solution)/shard_map/all_to_all | solution.py:285
  51.9 1.4 %collective-permute-start.1 = (f32[136,256]{1,0:T(8,128)S(1)}, f32[136,256]{1,0:T(8,128)S(1)}, u32[]{:S(2)}, u32[]{:S(2)}) collective-permute-start(f32[136,256]{1,0:T(8,128)S(1)} %split.17), channel_id=1, source_target_pairs={{0,1},{1,0},{2,3},{3,2},{4,5},{5,4},{6,7},{7,6},{8,9},{9,8},{10,11... | collective-permute-start | bytes 417800 | tf_op jit(solution)/shard_map/ppermute | solution.py:270
  53.3 6.1 %collective-permute-start.2 = (bf16[136,256]{1,0:T(8,128)(2,1)S(1)}, bf16[136,256]{1,0:T(8,128)(2,1)S(1)}, u32[]{:S(2)}, u32[]{:S(2)}) collective-permute-start(bf16[136,256]{1,0:T(8,128)(2,1)S(1)} %fusion), channel_id=1, source_target_pairs={{0,4},{4,0},{8,12},{12,8},{16,20},{20,16},{24,28},{28,24},{1,5},{5... | collective-permute-start | bytes 208904 | tf_op jit(solution)/shard_map/ppermute | solution.py:270
  55.4 9.0 %collective-permute-start.3 = (bf16[136,256]{1,0:T(8,128)(2,1)S(1)}, bf16[136,256]{1,0:T(8,128)(2,1)S(1)}, u32[]{:S(2)}, u32[]{:S(2)}) collective-permute-start(bf16[136,256]{1,0:T(8,128)(2,1)S(1)} %fusion), channel_id=1, source_target_pairs={{0,8},{4,12},{8,0},{12,4},{16,24},{20,28},{24,16},{28,20},{1,9},{5... | collective-permute-start | bytes 208904 | tf_op jit(solution)/shard_map/ppermute | solution.py:270
  56.9 8.6 %collective-permute-start.4 = (bf16[136,256]{1,0:T(8,128)(2,1)S(1)}, bf16[136,256]{1,0:T(8,128)(2,1)S(1)}, u32[]{:S(2)}, u32[]{:S(2)}) collective-permute-start(bf16[136,256]{1,0:T(8,128)(2,1)S(1)} %fusion), channel_id=1, source_target_pairs={{0,12},{4,8},{8,4},{12,0},{16,28},{20,24},{24,20},{28,16},{1,13},{... | collective-permute-start | bytes 208904 | tf_op jit(solution)/shard_map/ppermute | solution.py:270
  65.8 2.8 %collective-permute-start.6 = (bf16[256,256]{1,0:T(8,128)(2,1)S(1)}, bf16[256,256]{1,0:T(8,128)(2,1)S(1)}, u32[]{:S(2)}, u32[]{:S(2)}) collective-permute-start(bf16[256,256]{1,0:T(8,128)(2,1)S(1)} %shard_map.181), channel_id=1, source_target_pairs={{0,1},{1,0},{2,3},{3,2},{4,5},{5,4},{6,7},{7,6},{8,9},{9,8},{10,11... | collective-permute-start | bytes 393224 | tf_op jit(solution)/shard_map/ppermute | solution.py:270
  66.2 7.0 %collective-permute-start.5 = (bf16[136,256]{1,0:T(8,128)(2,1)S(1)}, bf16[136,256]{1,0:T(8,128)(2,1)S(1)}, u32[]{:S(2)}, u32[]{:S(2)}) collective-permute-start(bf16[136,256]{1,0:T(8,128)(2,1)S(1)} %add_add_fusion), channel_id=1, source_target_pairs={{0,16},{4,20},{8,24},{12,28},{16,0},{20,4},{24,8},{28,12},{1,17},{... | collective-permute-start | bytes 208904 | tf_op jit(solution)/shard_map/ppermute | solution.py:270
  68.7 4.6 %collective-permute-start.7 = (bf16[128,256]{1,0:T(8,128)(2,1)S(1)}, bf16[128,256]{1,0:T(8,128)(2,1)S(1)}, u32[]{:S(2)}, u32[]{:S(2)}) collective-permute-start(bf16[128,256]{1,0:T(8,128)(2,1)S(1)} %get-tuple-element.66), channel_id=1, source_target_pairs={{0,2},{1,3},{2,0},{3,1},{4,6},{5,7},{6,4},{7,5},{8,10},{9,11},{10,... | collective-permute-start | bytes 196616 | tf_op jit(solution)/shard_map/ppermute | solution.py:270
  69.6 3.8 %collective-permute-start.9 = (bf16[256,256]{1,0:T(8,128)(2,1)S(1)}, bf16[256,256]{1,0:T(8,128)(2,1)S(1)}, u32[]{:S(2)}, u32[]{:S(2)}) collective-permute-start(bf16[256,256]{1,0:T(8,128)(2,1)S(1)} %shard_map.183), channel_id=1, source_target_pairs={{0,1},{1,0},{2,3},{3,2},{4,5},{5,4},{6,7},{7,6},{8,9},{9,8},{10,11... | collective-permute-start | bytes 393224 | tf_op jit(solution)/shard_map/ppermute | solution.py:270
  70.0 4.6 %collective-permute-start.10 = (bf16[128,256]{1,0:T(8,128)(2,1)S(1)}, bf16[128,256]{1,0:T(8,128)(2,1)S(1)}, u32[]{:S(2)}, u32[]{:S(2)}) collective-permute-start(bf16[128,256]{1,0:T(8,128)(2,1)S(1)} %get-tuple-element.65), channel_id=1, source_target_pairs={{0,2},{1,3},{2,0},{3,1},{4,6},{5,7},{6,4},{7,5},{8,10},{9,11},{10,... | collective-permute-start | bytes 196616 | tf_op jit(solution)/shard_map/ppermute | solution.py:270
  73.3 1.4 %collective-permute-start.8 = (f32[136,256]{1,0:T(8,128)S(1)}, f32[136,256]{1,0:T(8,128)S(1)}, u32[]{:S(2)}, u32[]{:S(2)}) collective-permute-start(f32[136,256]{1,0:T(8,128)S(1)} %convert_add_fusion.2.mine_ref), channel_id=1, source_target_pairs={{0,1},{1,0},{2,3},{3,2},{4,5},{5,4},{6,7},{7,6},{8,9},{9,8},{10,11... | collective-permute-start | bytes 417800 | tf_op jit(solution)/shard_map/ppermute | solution.py:270

commit v6 on v5

--- a/solution.py
+++ b/solution.py
@@ -244,8 +244,10 @@
     outer_ref[...] = low[half + 1:half + 2]
 
 
-def scatter_kernel(mask_ref, grads_ref, out_ref):
-    out_ref[...] = dot(mask_ref[...], grads_ref[...]).astype(out_ref.dtype)
+def scatter_kernel(grads_ref, *refs):
+    count = len(refs) // 2
+    for mask_ref, out_ref in zip(refs[:count], refs[count:]):
+        out_ref[...] = dot(mask_ref[...], grads_ref[...]).astype(out_ref.dtype)
 
 
 def call(kernel, outs, *args, scalar=False, hbm_in=(), hbm_out=(), far_out=(), scratch=()):
@@ -270,15 +272,19 @@
     return lax.ppermute(x, axis, [(i, i ^ mask) for i in range(lax.axis_size(axis))])
 
 
+def rounded(x):
+    return lax.reduce_precision(x, exponent_bits=8, mantissa_bits=7)
+
+
 def reduce_pairs(x, axis, mask):
-    mine = x.astype(BF16)
-    return mine.astype(F32) + swap(mine, axis, mask).astype(F32)
+    mine = rounded(x)
+    return mine + swap(mine.astype(BF16), axis, mask).astype(F32)
 
 
 def reduce_fours(x, axis, mask):
-    mine = x.astype(BF16)
-    first, second, third = (swap(mine, axis, mask * k).astype(F32) for k in (1, 2, 3))
-    return (mine.astype(F32) + first) + (second + third)
+    mine = rounded(x)
+    first, second, third = (swap(mine.astype(BF16), axis, mask * k).astype(F32) for k in (1, 2, 3))
+    return (mine + first) + (second + third)
 
 
 def exchange(x, axis):
@@ -366,48 +372,54 @@
     half = width // 2
     placed, weights = call(
         decode_kernel,
-        [((slots, width), BF16), ((2 * (half + 8), width), F32)],
+        [((slots, width), BF16), ((2 * (half + 16), width), F32)],
         rep, fetched, gather, scatter, target, w1, b1, w2,
         scalar=True,
         hbm_out=(0,),
         scratch=(pltpu.VMEM((slots, width), BF16), pltpu.SemaphoreType.DMA((CHUNKS,))),
     )
     back = exchange(placed.reshape(n_dom, cap, width), "dom").reshape(-1, width)
-    step = 2
+    keep, send = jnp.split(rounded(weights), 2, axis=0)
+    weights = keep + swap(send.astype(BF16), "rep", 1).astype(F32)
+    if n_rep > 2:
+        second, third = swap(keep.astype(BF16), "rep", 2), swap(send.astype(BF16), "rep", 3)
+        weights = weights + (second.astype(F32) + third.astype(F32))
+    step = 4
     while step < n_rep:
         weights = reduce_pairs(weights, "rep", step)
         step *= 2
-    keep, send = jnp.split(weights, 2, axis=0)
-    weights = keep + swap(send, "rep", 1)
     step = 1
     while 4 * step <= n_dom // 2:
-        weights = reduce_fours(weights, "dom", step)
+        mine = rounded(weights)
+        parts = [swap(mine.astype(BF16), "dom", step * k) for k in (1, 2, 3)]
+        back, *parts[:2] = lax.optimization_barrier((back, *parts[:2]))
+        first, second, third = (part.astype(F32) for part in parts)
+        weights = (mine + first) + (second + third)
         step *= 4
-
-    back, weights = lax.optimization_barrier((back, weights))
     size = nodes // n_rep
     masks = call(
         functools.partial(sum_mask_kernel, cap), [((size, slots), BF16)] * n_rep, rep, word, scalar=True
     )
 
-    def block_sum(j, dtype):
-        (out,) = call(scatter_kernel, [((size, width), dtype)], masks[j], back)
-        return out
-
-    sums = {}
-    for j in reversed(range(0, n_rep, 2)):
-        send = block_sum(j + 1, BF16)
-        sums[j] = block_sum(j, F32) + swap(send, "rep", 1).astype(F32)
+    block = {}
+    for group in (range(n_rep - 1, 0, -2), range(n_rep - 2, -1, -2)):
+        outs = call(
+            scatter_kernel,
+            [((size, width), BF16 if j % 2 else F32) for j in group],
+            back, *(masks[j] for j in group),
+        )
+        block.update(zip(group, outs))
+    sums = {j: block[j] + swap(block[j + 1], "rep", 1).astype(F32) for j in reversed(range(0, n_rep, 2))}
     rep_step, away = 2, []
     while rep_step < n_rep:
         for j in range(0, n_rep, 2 * rep_step):
             parts = jnp.split(sums[j + rep_step].astype(BF16), X_PARTS, axis=0)
             away = [swap(part, "rep", rep_step) for part in parts]
             if step < n_dom:
-                mine = weights.astype(BF16)
-                others = swap(mine, "dom", step)
+                mine = rounded(weights)
+                others = swap(mine.astype(BF16), "dom", step)
                 others, away[0] = lax.optimization_barrier((others, away[0]))
-                weights = mine.astype(F32) + others.astype(F32)
+                weights = mine + others.astype(F32)
                 step *= 2
             if 2 * rep_step < n_rep:
                 sums[j] = sums[j] + jnp.concatenate(away, axis=0).astype(F32)

time: 75.9 us -> 75.7 us (level)
    pallas_call x12 -> x10, Pallas kernels: 12.8 us -> 12.5 us  [call(): pl.pallas_call(kernel, out_shape=[(pltpu.HBM if i in far_out else pltpu.V...]
    ppermute x11 -> x12, starting transfers between devices: 10.1 us -> 10.1 us  [swap(): lax.ppermute(x, axis, [(i, i ^ mask) for i in range(lax.axis_size(axis))])]
    ppermute x11 -> x12, waiting for transfers between devices: 12.1 us -> 12.1 us  [swap(): lax.ppermute(x, axis, [(i, i ^ mask) for i in range(lax.axis_size(axis))])]
  transfers between devices with their start and end apart: 14 -> 15, of which waited for: 9 -> 10; matrix products, arithmetic and copies ran while one was open for 1% -> 1% of each run, Pallas kernels for 9% -> 9%
where the time goes in v6:
time: 75.7 us; the launch traced here: 75.3 us
  waiting for transfers between devices  25.5 us (34%)
  starting transfers between devices  24.6 us (32%)
  Pallas kernels  12.5 us (17%)
  blocking collectives  11.1 us (15%)
  between operations  0.82 us (1%)
    all_to_all x3, starting transfers between devices, exchange(): return lax.all_to_all(x, axis, split_axis=0, concat_axis=0, tiled=True)  14.4 us
    all_to_all x3, waiting for transfers between devices, exchange(): return lax.all_to_all(x, axis, split_axis=0, concat_axis=0, tiled=True)  13.4 us
    pallas_call x10, Pallas kernels, call(): pl.pallas_call(kernel, out_shape=[(pltpu.HBM if i in far_out else pltpu.V...  12.5 us
    ppermute x12, waiting for transfers between devices, swap(): lax.ppermute(x, axis, [(i, i ^ mask) for i in range(lax.axis_size(axis))])  12.1 us
    all_to_all x1, blocking collectives, exchange(): return lax.all_to_all(x, axis, split_axis=0, concat_axis=0, tiled=True)  11.1 us
    ppermute x12, starting transfers between devices, swap(): lax.ppermute(x, axis, [(i, i ^ mask) for i in range(lax.axis_size(axis))])  10.1 us
  transfers between devices with their start and end apart: 15, of which 10 were waited for; matrix products, arithmetic and copies ran while one was open for 1% of the time, Pallas kernels for 9%

profile of v6, /device:TPU:0, one launch (start us, length us, event | category | flops | bytes accessed | tf_op | source)
XLA Modules:
  0.0 75.3 jit_solution(13361318767902663304)
XLA Ops:
  0.6 7.3 %all-to-all-start = ((s32[8,1,32]{2,1,0:T(1,128)}), s32[8,1,32]{2,1,0:T(1,128)S(1)}, u32[]{:S(2)}, u32[]{:S(2)}) async-start(s32[8,1,32]{2,1,0:T(1,128)} %bitcast.20), calls=%async_computation | async-start | bytes 8192 | tf_op jit(solution)/shard_map/all_to_all | solution.py:291
  7.9 1.1 %shard_map.174 = (s32[8,128]{1,0:T(8,128)S(1)}, s32[1,512]{1,0:T(1,128)S(1)}) custom-call(s32[2,256]{1,0:T(2,128)} %bitcast.21, s32[2,256]{1,0:T(2,128)} %bitcast.22, s32[8,32]{1,0:T(8,128)} %halo_hbm.3), custom_call_target="tpu_custom_call" | custom-call | tf_op jit(solution)/shard_map/pallas_call | solution.py:261
  9.0 3.0 %shard_map.173 = (f32[1024,256]{1,0:T(8,128)S(1)}, f32[1024,256]{1,0:T(8,128)S(1)}, bf16[1024,256]{1,0:T(8,128)(2,1)S(1)}, bf16[256,256]{1,0:T(8,128)(2,1)S(1)}, bf16[1024,256]{1,0:T(8,128)(2,1)S(1)}) custom-call(bf16[1024,256]{1,0:T(8,128)(2,1)} %feats_hbm.1, bf16[1024,1024]{1,0:T(8,128)(2,1)} %inner_hbm.1, bf16[256,256]{1,0:T(8,128)(2,1)} %self_hbm.1, ...), custom_call_target="tpu_custom_call" | custom-call | tf_op jit(solution)/shard_map/pallas_call | solution.py:261
  12.0 2.3 %all-to-all-done = s32[8,1,32]{2,1,0:T(1,128)S(1)} async-done(((s32[8,1,32]{2,1,0:T(1,128)}), s32[8,1,32]{2,1,0:T(1,128)S(1)}, u32[]{:S(2)}, u32[]{:S(2)}) %all-to-all-start) | async-done | bytes 1056 | tf_op jit(solution)/shard_map/all_to_all | solution.py:291
  14.9 11.1 %all_to_all.26.halo_ref = bf16[8,40,256]{2,1,0:T(8,128)(2,1)S(1)} all-to-all(bf16[8,40,256]{2,1,0:T(8,128)(2,1)S(1)} %shard_map.175), channel_id=1, replica_groups=mesh['dom'=8,'rep'=4] {'dom'}, dimensions={0} | all-to-all | bytes 327680 | tf_op jit(solution)/shard_map/all_to_all | solution.py:291
  26.0 1.9 %shard_map.176 = (bf16[1024,256]{1,0:T(8,128)(2,1)}, bf16[1024,256]{1,0:T(8,128)(2,1)}, s32[8,128]{1,0:T(8,128)S(1)}) custom-call(f32[1024,256]{1,0:T(8,128)S(1)} %get-tuple-element.40.agg_ref, f32[1024,256]{1,0:T(8,128)S(1)} %get-tuple-element.41.base_ref, bf16[8,40,256]{2,1,0:T(8,128)(2,1)S(1)} %all_to_all.26.halo_ref, ...), custom_call_target="tpu_custom_call" | custom-call | tf_op jit(solution)/shard_map/pallas_call | solution.py:261
  27.9 3.5 %all-to-all-start.2 = ((bf16[8,128,256]{2,1,0:T(8,128)(2,1)}), bf16[8,128,256]{2,1,0:T(8,128)(2,1)S(1)}, u32[]{:S(2)}, u32[]{:S(2)}) async-start(bf16[8,128,256]{2,1,0:T(8,128)(2,1)} %bitcast.19), calls=%async_computation.2 | async-start | bytes 1048576 | tf_op jit(solution)/shard_map/all_to_all | solution.py:291
  31.4 0.6 reshape.45.w2_hbm
  32.0 1.1 %shard_map.177 = (bf16[512,1024]{1,0:T(8,128)(2,1)S(1)}, bf16[1024,512]{1,0:T(8,128)(2,1)S(1)}, f32[256,1]{1,0:T(8,128)S(1)}, bf16[256,256]{1,0:T(8,128)(2,1)S(1...) custom-call(s32[1,512]{1,0:T(1,128)S(1)} %get-tuple-element.48.place_ref, s32[1,256]{1,0:T(1,128)} %bitcast.24, ...), custom_call_target="tpu_custom_call" | custom-call | tf_op jit(solution)/shard_map/pallas_call | solution.py:261
  33.1 11.1 %all-to-all-done.2 = bf16[8,128,256]{2,1,0:T(8,128)(2,1)S(1)} async-done(((bf16[8,128,256]{2,1,0:T(8,128)(2,1)}), bf16[8,128,256]{2,1,0:T(8,128)(2,1)S(1)}, u32[]{:S(2)}, u32[]{:S(2)}) %all-to-all-start.2) | async-done | bytes 524320 | tf_op jit(solution)/shard_map/all_to_all | solution.py:291
  44.2 2.5 %shard_map.178 = (bf16[1024,256]{1,0:T(8,128)(2,1)}, f32[288,256]{1,0:T(8,128)S(1)}) custom-call(s32[1]{0:T(128)} %bitcast.5.rep_ref, bf16[1024,256]{1,0:T(8,128)(2,1)S(1)} %bitcast.16, bf16[512,1024]{1,0:T(8,128)(2,1)S(1)} %get-tuple-element.49.gather_ref, bf16[1024,512]{1,0:T(8,128)(2,1)S(1)} %get-tuple-element.50.scatter_ref, ...), custom_call_target="tpu_custom_call" | custom-call | tf_op jit(solution)/shard_map/pallas_call | solution.py:261
  46.6 3.6 %all-to-all-start.3 = ((bf16[8,128,256]{2,1,0:T(8,128)(2,1)}), bf16[8,128,256]{2,1,0:T(8,128)(2,1)S(1)}, u32[]{:S(2)}, u32[]{:S(2)}) async-start(bf16[8,128,256]{2,1,0:T(8,128)(2,1)} %bitcast.18), calls=%async_computation.3 | async-start | bytes 1048576 | tf_op jit(solution)/shard_map/all_to_all | solution.py:291
  50.4 1.6 %collective-permute-start.2 = (bf16[144,256]{1,0:T(8,128)(2,1)S(1)}, bf16[144,256]{1,0:T(8,128)(2,1)S(1)}, u32[]{:S(2)}, u32[]{:S(2)}) collective-permute-start(bf16[144,256]{1,0:T(8,128)(2,1)S(1)} %get-tuple-element.78), channel_id=1, source_target_pairs={{0,3},{1,2},{2,1},{3,0},{4,7},{5,6},{6,5},{7,4},{8,11},{9,10},{10,... | collective-permute-start | bytes 221192 | tf_op jit(solution)/shard_map/ppermute | solution.py:272
  52.5 2.1 %collective-permute-done.2 = bf16[144,256]{1,0:T(8,128)(2,1)S(1)} collective-permute-done((bf16[144,256]{1,0:T(8,128)(2,1)S(1)}, bf16[144,256]{1,0:T(8,128)(2,1)S(1)}, u32[]{:S(2)}, u32[]{:S(2)}) %collective-permute-start.2) | collective-permute-done | bytes 73760 | tf_op jit(solution)/shard_map/ppermute | solution.py:272
  54.6 2.0 %collective-permute-done.1 = bf16[144,256]{1,0:T(8,128)(2,1)S(1)} collective-permute-done((bf16[144,256]{1,0:T(8,128)(2,1)S(1)}, bf16[144,256]{1,0:T(8,128)(2,1)S(1)}, u32[]{:S(2)}, u32[]{:S(2)}) %collective-permute-start.1) | collective-permute-done | bytes 73760 | tf_op jit(solution)/shard_map/ppermute | solution.py:272
  56.6 2.1 %collective-permute-start.3 = (bf16[144,256]{1,0:T(8,128)(2,1)S(1)}, bf16[144,256]{1,0:T(8,128)(2,1)S(1)}, u32[]{:S(2)}, u32[]{:S(2)}) collective-permute-start(bf16[144,256]{1,0:T(8,128)(2,1)S(1)} %get-tuple-element.75), channel_id=1, source_target_pairs={{0,4},{4,0},{8,12},{12,8},{16,20},{20,16},{24,28},{28,24},{1,5},{5... | collective-permute-start | bytes 221192 | tf_op jit(solution)/shard_map/ppermute | solution.py:272
  58.7 1.5 %collective-permute-start.4 = (bf16[144,256]{1,0:T(8,128)(2,1)S(1)}, bf16[144,256]{1,0:T(8,128)(2,1)S(1)}, u32[]{:S(2)}, u32[]{:S(2)}) collective-permute-start(bf16[144,256]{1,0:T(8,128)(2,1)S(1)} %get-tuple-element.75), channel_id=1, source_target_pairs={{0,8},{4,12},{8,0},{12,4},{16,24},{20,28},{24,16},{28,20},{1,9},{5... | collective-permute-start | bytes 221192 | tf_op jit(solution)/shard_map/ppermute | solution.py:272
  60.3 0.7 shard_map.179
  61.1 3.8 %collective-permute-done.4 = bf16[144,256]{1,0:T(8,128)(2,1)S(1)} collective-permute-done((bf16[144,256]{1,0:T(8,128)(2,1)S(1)}, bf16[144,256]{1,0:T(8,128)(2,1)S(1)}, u32[]{:S(2)}, u32[]{:S(2)}) %collective-permute-start.4) | collective-permute-done | bytes 73760 | tf_op jit(solution)/shard_map/ppermute | solution.py:272
  65.9 2.1 %collective-permute-start.6 = (bf16[144,256]{1,0:T(8,128)(2,1)S(1)}, bf16[144,256]{1,0:T(8,128)(2,1)S(1)}, u32[]{:S(2)}, u32[]{:S(2)}) collective-permute-start(bf16[144,256]{1,0:T(8,128)(2,1)S(1)} %fusion), channel_id=1, source_target_pairs={{0,16},{4,20},{8,24},{12,28},{16,0},{20,4},{24,8},{28,12},{1,17},{... | collective-permute-start | bytes 221192 | tf_op jit(solution)/shard_map/ppermute | solution.py:272
  68.4 1.6 %collective-permute-start.8 = (bf16[128,256]{1,0:T(8,128)(2,1)S(1)}, bf16[128,256]{1,0:T(8,128)(2,1)S(1)}, u32[]{:S(2)}, u32[]{:S(2)}) collective-permute-start(bf16[128,256]{1,0:T(8,128)(2,1)S(1)} %get-tuple-element.80), channel_id=1, source_target_pairs={{0,2},{1,3},{2,0},{3,1},{4,6},{5,7},{6,4},{7,5},{8,10},{9,11},{10,... | collective-permute-start | bytes 196616 | tf_op jit(solution)/shard_map/ppermute | solution.py:272
  70.5 1.8 %collective-permute-done.6 = bf16[144,256]{1,0:T(8,128)(2,1)S(1)} collective-permute-done((bf16[144,256]{1,0:T(8,128)(2,1)S(1)}, bf16[144,256]{1,0:T(8,128)(2,1)S(1)}, u32[]{:S(2)}, u32[]{:S(2)}) %collective-permute-start.6) | collective-permute-done | bytes 73760 | tf_op jit(solution)/shard_map/ppermute | solution.py:272
  72.9 1.5 %collective-permute-done.11.refs_1_ = bf16[128,256]{1,0:T(8,128)(2,1)S(1)} collective-permute-done((bf16[128,256]{1,0:T(8,128)(2,1)S(1)}, bf16[128,256]{1,0:T(8,128)(2,1)S(1)}, u32[]{:S(2)}, u32[]{:S(2)}) %collective-permute-start.11) | collective-permute-done | bytes 65568 | tf_op jit(solution)/shard_map/ppermute | solution.py:272
  74.5 0.8 %shard_map.182 = (f32[256,256]{1,0:T(8,128)}, f32[256,256]{1,0:T(8,128)}, f32[1,256]{1,0:T(1,128)}, f32[1,256]{1,0:T(1,128)}) custom-call(s32[1]{0:T(128)} %bitcast.5.rep_ref, f32[144,256]{1,0:T(8,128)S(1)} %convert_add_fusion.1.mine_ref, f32[144,256]{1,0:T(8,128)S(1)} %collective-permute-done.9.other_ref, f32[256,256]{1,0:T(8,128)S(1)} %convert_add_fusion.keep_ref, ...), custom_call_target="tpu_custom_call" | custom-call | tf_op jit(solution)/shard_map/pallas_call | solution.py:261
  (29 shorter events, 3.9 us)
Async XLA Ops:
  0.6 13.7 %all-to-all-start = ((s32[8,1,32]{2,1,0:T(1,128)}), s32[8,1,32]{2,1,0:T(1,128)S(1)}, u32[]{:S(2)}, u32[]{:S(2)}) async-start(s32[8,1,32]{2,1,0:T(1,128)} %bitcast.20), calls=%async_computation | async-start | bytes 8192 | tf_op jit(solution)/shard_map/all_to_all | solution.py:291
  14.9 16.6 %copy-start = (bf16[256]{0:T(256)(128)(2,1)S(1)}, bf16[256]{0:T(256)(128)(2,1)}, u32[]{:S(2)}) copy-start(bf16[256]{0:T(256)(128)(2,1)} %param.27) | copy-start | bytes 1540
  27.9 16.3 %all-to-all-start.2 = ((bf16[8,128,256]{2,1,0:T(8,128)(2,1)}), bf16[8,128,256]{2,1,0:T(8,128)(2,1)S(1)}, u32[]{:S(2)}, u32[]{:S(2)}) async-start(bf16[8,128,256]{2,1,0:T(8,128)(2,1)} %bitcast.19), calls=%async_computation.2 | async-start | bytes 1048576 | tf_op jit(solution)/shard_map/all_to_all | solution.py:291
  46.6 18.3 %all-to-all-start.3 = ((bf16[8,128,256]{2,1,0:T(8,128)(2,1)}), bf16[8,128,256]{2,1,0:T(8,128)(2,1)S(1)}, u32[]{:S(2)}, u32[]{:S(2)}) async-start(bf16[8,128,256]{2,1,0:T(8,128)(2,1)} %bitcast.18), calls=%async_computation.3 | async-start | bytes 1048576 | tf_op jit(solution)/shard_map/all_to_all | solution.py:291
  50.3 2.2 %collective-permute-start = (bf16[144,256]{1,0:T(8,128)(2,1)S(1)}, bf16[144,256]{1,0:T(8,128)(2,1)S(1)}, u32[]{:S(2)}, u32[]{:S(2)}) collective-permute-start(bf16[144,256]{1,0:T(8,128)(2,1)S(1)} %get-tuple-element.78), channel_id=1, source_target_pairs={{0,1},{1,0},{2,3},{3,2},{4,5},{5,4},{6,7},{7,6},{8,9},{9,8},{10,11... | collective-permute-start | bytes 221192 | tf_op jit(solution)/shard_map/ppermute | solution.py:272
  50.4 4.2 %collective-permute-start.2 = (bf16[144,256]{1,0:T(8,128)(2,1)S(1)}, bf16[144,256]{1,0:T(8,128)(2,1)S(1)}, u32[]{:S(2)}, u32[]{:S(2)}) collective-permute-start(bf16[144,256]{1,0:T(8,128)(2,1)S(1)} %get-tuple-element.78), channel_id=1, source_target_pairs={{0,3},{1,2},{2,1},{3,0},{4,7},{5,6},{6,5},{7,4},{8,11},{9,10},{10,... | collective-permute-start | bytes 221192 | tf_op jit(solution)/shard_map/ppermute | solution.py:272
  52.0 4.6 %collective-permute-start.1 = (bf16[144,256]{1,0:T(8,128)(2,1)S(1)}, bf16[144,256]{1,0:T(8,128)(2,1)S(1)}, u32[]{:S(2)}, u32[]{:S(2)}) collective-permute-start(bf16[144,256]{1,0:T(8,128)(2,1)S(1)} %get-tuple-element.77), channel_id=1, source_target_pairs={{0,2},{1,3},{2,0},{3,1},{4,6},{5,7},{6,4},{7,5},{8,10},{9,11},{10,... | collective-permute-start | bytes 221192 | tf_op jit(solution)/shard_map/ppermute | solution.py:272
  56.6 4.4 %collective-permute-start.3 = (bf16[144,256]{1,0:T(8,128)(2,1)S(1)}, bf16[144,256]{1,0:T(8,128)(2,1)S(1)}, u32[]{:S(2)}, u32[]{:S(2)}) collective-permute-start(bf16[144,256]{1,0:T(8,128)(2,1)S(1)} %get-tuple-element.75), channel_id=1, source_target_pairs={{0,4},{4,0},{8,12},{12,8},{16,20},{20,16},{24,28},{28,24},{1,5},{5... | collective-permute-start | bytes 221192 | tf_op jit(solution)/shard_map/ppermute | solution.py:272
  58.7 6.2 %collective-permute-start.4 = (bf16[144,256]{1,0:T(8,128)(2,1)S(1)}, bf16[144,256]{1,0:T(8,128)(2,1)S(1)}, u32[]{:S(2)}, u32[]{:S(2)}) collective-permute-start(bf16[144,256]{1,0:T(8,128)(2,1)S(1)} %get-tuple-element.75), channel_id=1, source_target_pairs={{0,8},{4,12},{8,0},{12,4},{16,24},{20,28},{24,16},{28,20},{1,9},{5... | collective-permute-start | bytes 221192 | tf_op jit(solution)/shard_map/ppermute | solution.py:272
  60.2 5.6 %collective-permute-start.5 = (bf16[144,256]{1,0:T(8,128)(2,1)S(1)}, bf16[144,256]{1,0:T(8,128)(2,1)S(1)}, u32[]{:S(2)}, u32[]{:S(2)}) collective-permute-start(bf16[144,256]{1,0:T(8,128)(2,1)S(1)} %get-tuple-element.75), channel_id=1, source_target_pairs={{0,12},{4,8},{8,4},{12,0},{16,28},{20,24},{24,20},{28,16},{1,13},{... | collective-permute-start | bytes 221192 | tf_op jit(solution)/shard_map/ppermute | solution.py:272
  65.3 3.0 %collective-permute-start.7 = (bf16[256,256]{1,0:T(8,128)(2,1)S(1)}, bf16[256,256]{1,0:T(8,128)(2,1)S(1)}, u32[]{:S(2)}, u32[]{:S(2)}) collective-permute-start(bf16[256,256]{1,0:T(8,128)(2,1)S(1)} %get-tuple-element.66), channel_id=1, source_target_pairs={{0,1},{1,0},{2,3},{3,2},{4,5},{5,4},{6,7},{7,6},{8,9},{9,8},{10,11... | collective-permute-start | bytes 393224 | tf_op jit(solution)/shard_map/ppermute | solution.py:272
  65.9 6.5 %collective-permute-start.6 = (bf16[144,256]{1,0:T(8,128)(2,1)S(1)}, bf16[144,256]{1,0:T(8,128)(2,1)S(1)}, u32[]{:S(2)}, u32[]{:S(2)}) collective-permute-start(bf16[144,256]{1,0:T(8,128)(2,1)S(1)} %fusion), channel_id=1, source_target_pairs={{0,16},{4,20},{8,24},{12,28},{16,0},{20,4},{24,8},{28,12},{1,17},{... | collective-permute-start | bytes 221192 | tf_op jit(solution)/shard_map/ppermute | solution.py:272
  68.4 4.3 %collective-permute-start.8 = (bf16[128,256]{1,0:T(8,128)(2,1)S(1)}, bf16[128,256]{1,0:T(8,128)(2,1)S(1)}, u32[]{:S(2)}, u32[]{:S(2)}) collective-permute-start(bf16[128,256]{1,0:T(8,128)(2,1)S(1)} %get-tuple-element.80), channel_id=1, source_target_pairs={{0,2},{1,3},{2,0},{3,1},{4,6},{5,7},{6,4},{7,5},{8,10},{9,11},{10,... | collective-permute-start | bytes 196616 | tf_op jit(solution)/shard_map/ppermute | solution.py:272
  70.0 2.9 %collective-permute-start.10 = (bf16[256,256]{1,0:T(8,128)(2,1)S(1)}, bf16[256,256]{1,0:T(8,128)(2,1)S(1)}, u32[]{:S(2)}, u32[]{:S(2)}) collective-permute-start(bf16[256,256]{1,0:T(8,128)(2,1)S(1)} %get-tuple-element.69), channel_id=1, source_target_pairs={{0,1},{1,0},{2,3},{3,2},{4,5},{5,4},{6,7},{7,6},{8,9},{9,8},{10,11... | collective-permute-start | bytes 393224 | tf_op jit(solution)/shard_map/ppermute | solution.py:272
  70.0 4.5 %collective-permute-start.11 = (bf16[128,256]{1,0:T(8,128)(2,1)S(1)}, bf16[128,256]{1,0:T(8,128)(2,1)S(1)}, u32[]{:S(2)}, u32[]{:S(2)}) collective-permute-start(bf16[128,256]{1,0:T(8,128)(2,1)S(1)} %get-tuple-element.79), channel_id=1, source_target_pairs={{0,2},{1,3},{2,0},{3,1},{4,6},{5,7},{6,4},{7,5},{8,10},{9,11},{10,... | collective-permute-start | bytes 196616 | tf_op jit(solution)/shard_map/ppermute | solution.py:272
  72.8 1.7 %collective-permute-start.9 = (f32[144,256]{1,0:T(8,128)S(1)}, f32[144,256]{1,0:T(8,128)S(1)}, u32[]{:S(2)}, u32[]{:S(2)}) collective-permute-start(f32[144,256]{1,0:T(8,128)S(1)} %convert_add_fusion.1.mine_ref), channel_id=1, source_target_pairs={{0,1},{1,0},{2,3},{3,2},{4,5},{5,4},{6,7},{7,6},{8,9},{9,8},{10,11... | collective-permute-start | bytes 442376 | tf_op jit(solution)/shard_map/ppermute | solution.py:272

commit v7 on v6

--- a/solution.py
+++ b/solution.py
@@ -236,7 +236,7 @@
         sums_ref[...] = keep_ref[...]
     half = grad_ref.shape[0] // 2
     odd = (rep_ref[0] & 1) == 1
-    mine, other = mine_ref[...], other_ref[...]
+    mine, other = mine_ref[...].astype(F32), other_ref[...].astype(F32)
     low = jnp.where(odd, other, mine)
     grad_ref[:half] = low[:half]
     grad_ref[half:] = jnp.where(odd, mine, other)[:half]
@@ -428,6 +428,7 @@
         weights = reduce_pairs(weights, "dom", step)
         step *= 2
 
+    weights = rounded(weights).astype(BF16)
     others = swap(weights, "rep", 1)
     grad_embed, grad_dec1, grad_bias1, grad_dec2 = call(
         final_kernel,

time: 75.7 us -> 75.7 us (level)
  no operation moved by 1% of the time
where the time goes in v7:
time: 75.7 us; the launch traced here: 75.3 us
  waiting for transfers between devices  25.5 us (34%)
  starting transfers between devices  24.6 us (32%)
  Pallas kernels  12.5 us (17%)
  blocking collectives  11.1 us (15%)
  between operations  0.82 us (1%)
    all_to_all x3, starting transfers between devices, exchange(): return lax.all_to_all(x, axis, split_axis=0, concat_axis=0, tiled=True)  14.4 us
    all_to_all x3, waiting for transfers between devices, exchange(): return lax.all_to_all(x, axis, split_axis=0, concat_axis=0, tiled=True)  13.4 us
    pallas_call x10, Pallas kernels, call(): pl.pallas_call(kernel, out_shape=[(pltpu.HBM if i in far_out else pltpu.V...  12.5 us
    ppermute x12, waiting for transfers between devices, swap(): lax.ppermute(x, axis, [(i, i ^ mask) for i in range(lax.axis_size(axis))])  12.1 us
    all_to_all x1, blocking collectives, exchange(): return lax.all_to_all(x, axis, split_axis=0, concat_axis=0, tiled=True)  11.1 us
    ppermute x12, starting transfers between devices, swap(): lax.ppermute(x, axis, [(i, i ^ mask) for i in range(lax.axis_size(axis))])  10.1 us
  transfers between devices with their start and end apart: 15, of which 10 were waited for; matrix products, arithmetic and copies ran while one was open for 1% of the time, Pallas kernels for 9%

profile of v7, /device:TPU:0, one launch (start us, length us, event | category | flops | bytes accessed | tf_op | source)
XLA Modules:
  0.0 75.3 jit_solution(10286835895897131924)
XLA Ops:
  0.6 7.3 %all-to-all-start = ((s32[8,1,32]{2,1,0:T(1,128)}), s32[8,1,32]{2,1,0:T(1,128)S(1)}, u32[]{:S(2)}, u32[]{:S(2)}) async-start(s32[8,1,32]{2,1,0:T(1,128)} %bitcast.20), calls=%async_computation | async-start | bytes 8192 | tf_op jit(solution)/shard_map/all_to_all | solution.py:291
  7.9 1.1 %shard_map.174 = (s32[8,128]{1,0:T(8,128)S(1)}, s32[1,512]{1,0:T(1,128)S(1)}) custom-call(s32[2,256]{1,0:T(2,128)} %bitcast.21, s32[2,256]{1,0:T(2,128)} %bitcast.22, s32[8,32]{1,0:T(8,128)} %halo_hbm.3), custom_call_target="tpu_custom_call" | custom-call | tf_op jit(solution)/shard_map/pallas_call | solution.py:261
  9.0 3.0 %shard_map.173 = (f32[1024,256]{1,0:T(8,128)S(1)}, f32[1024,256]{1,0:T(8,128)S(1)}, bf16[1024,256]{1,0:T(8,128)(2,1)S(1)}, bf16[256,256]{1,0:T(8,128)(2,1)S(1)}, bf16[1024,256]{1,0:T(8,128)(2,1)S(1)}) custom-call(bf16[1024,256]{1,0:T(8,128)(2,1)} %feats_hbm.1, bf16[1024,1024]{1,0:T(8,128)(2,1)} %inner_hbm.1, bf16[256,256]{1,0:T(8,128)(2,1)} %self_hbm.1, ...), custom_call_target="tpu_custom_call" | custom-call | tf_op jit(solution)/shard_map/pallas_call | solution.py:261
  12.0 2.3 %all-to-all-done = s32[8,1,32]{2,1,0:T(1,128)S(1)} async-done(((s32[8,1,32]{2,1,0:T(1,128)}), s32[8,1,32]{2,1,0:T(1,128)S(1)}, u32[]{:S(2)}, u32[]{:S(2)}) %all-to-all-start) | async-done | bytes 1056 | tf_op jit(solution)/shard_map/all_to_all | solution.py:291
  14.9 11.1 %all_to_all.26.halo_ref = bf16[8,40,256]{2,1,0:T(8,128)(2,1)S(1)} all-to-all(bf16[8,40,256]{2,1,0:T(8,128)(2,1)S(1)} %shard_map.175), channel_id=1, replica_groups=mesh['dom'=8,'rep'=4] {'dom'}, dimensions={0} | all-to-all | bytes 327680 | tf_op jit(solution)/shard_map/all_to_all | solution.py:291
  26.0 1.9 %shard_map.176 = (bf16[1024,256]{1,0:T(8,128)(2,1)}, bf16[1024,256]{1,0:T(8,128)(2,1)}, s32[8,128]{1,0:T(8,128)S(1)}) custom-call(f32[1024,256]{1,0:T(8,128)S(1)} %get-tuple-element.40.agg_ref, f32[1024,256]{1,0:T(8,128)S(1)} %get-tuple-element.41.base_ref, bf16[8,40,256]{2,1,0:T(8,128)(2,1)S(1)} %all_to_all.26.halo_ref, ...), custom_call_target="tpu_custom_call" | custom-call | tf_op jit(solution)/shard_map/pallas_call | solution.py:261
  27.9 3.5 %all-to-all-start.2 = ((bf16[8,128,256]{2,1,0:T(8,128)(2,1)}), bf16[8,128,256]{2,1,0:T(8,128)(2,1)S(1)}, u32[]{:S(2)}, u32[]{:S(2)}) async-start(bf16[8,128,256]{2,1,0:T(8,128)(2,1)} %bitcast.19), calls=%async_computation.2 | async-start | bytes 1048576 | tf_op jit(solution)/shard_map/all_to_all | solution.py:291
  31.4 0.6 reshape.45.w2_hbm
  32.0 1.1 %shard_map.177 = (bf16[512,1024]{1,0:T(8,128)(2,1)S(1)}, bf16[1024,512]{1,0:T(8,128)(2,1)S(1)}, f32[256,1]{1,0:T(8,128)S(1)}, bf16[256,256]{1,0:T(8,128)(2,1)S(1...) custom-call(s32[1,512]{1,0:T(1,128)S(1)} %get-tuple-element.48.place_ref, s32[1,256]{1,0:T(1,128)} %bitcast.24, ...), custom_call_target="tpu_custom_call" | custom-call | tf_op jit(solution)/shard_map/pallas_call | solution.py:261
  33.1 11.1 %all-to-all-done.2 = bf16[8,128,256]{2,1,0:T(8,128)(2,1)S(1)} async-done(((bf16[8,128,256]{2,1,0:T(8,128)(2,1)}), bf16[8,128,256]{2,1,0:T(8,128)(2,1)S(1)}, u32[]{:S(2)}, u32[]{:S(2)}) %all-to-all-start.2) | async-done | bytes 524320 | tf_op jit(solution)/shard_map/all_to_all | solution.py:291
  44.2 2.5 %shard_map.178 = (bf16[1024,256]{1,0:T(8,128)(2,1)}, f32[288,256]{1,0:T(8,128)S(1)}) custom-call(s32[1]{0:T(128)} %bitcast.5.rep_ref, bf16[1024,256]{1,0:T(8,128)(2,1)S(1)} %bitcast.16, bf16[512,1024]{1,0:T(8,128)(2,1)S(1)} %get-tuple-element.49.gather_ref, bf16[1024,512]{1,0:T(8,128)(2,1)S(1)} %get-tuple-element.50.scatter_ref, ...), custom_call_target="tpu_custom_call" | custom-call | tf_op jit(solution)/shard_map/pallas_call | solution.py:261
  46.6 3.6 %all-to-all-start.3 = ((bf16[8,128,256]{2,1,0:T(8,128)(2,1)}), bf16[8,128,256]{2,1,0:T(8,128)(2,1)S(1)}, u32[]{:S(2)}, u32[]{:S(2)}) async-start(bf16[8,128,256]{2,1,0:T(8,128)(2,1)} %bitcast.18), calls=%async_computation.3 | async-start | bytes 1048576 | tf_op jit(solution)/shard_map/all_to_all | solution.py:291
  50.4 1.6 %collective-permute-start.2 = (bf16[144,256]{1,0:T(8,128)(2,1)S(1)}, bf16[144,256]{1,0:T(8,128)(2,1)S(1)}, u32[]{:S(2)}, u32[]{:S(2)}) collective-permute-start(bf16[144,256]{1,0:T(8,128)(2,1)S(1)} %get-tuple-element.78), channel_id=1, source_target_pairs={{0,3},{1,2},{2,1},{3,0},{4,7},{5,6},{6,5},{7,4},{8,11},{9,10},{10,... | collective-permute-start | bytes 221192 | tf_op jit(solution)/shard_map/ppermute | solution.py:272
  52.5 2.1 %collective-permute-done.2 = bf16[144,256]{1,0:T(8,128)(2,1)S(1)} collective-permute-done((bf16[144,256]{1,0:T(8,128)(2,1)S(1)}, bf16[144,256]{1,0:T(8,128)(2,1)S(1)}, u32[]{:S(2)}, u32[]{:S(2)}) %collective-permute-start.2) | collective-permute-done | bytes 73760 | tf_op jit(solution)/shard_map/ppermute | solution.py:272
  54.6 2.0 %collective-permute-done.1 = bf16[144,256]{1,0:T(8,128)(2,1)S(1)} collective-permute-done((bf16[144,256]{1,0:T(8,128)(2,1)S(1)}, bf16[144,256]{1,0:T(8,128)(2,1)S(1)}, u32[]{:S(2)}, u32[]{:S(2)}) %collective-permute-start.1) | collective-permute-done | bytes 73760 | tf_op jit(solution)/shard_map/ppermute | solution.py:272
  56.6 2.1 %collective-permute-start.3 = (bf16[144,256]{1,0:T(8,128)(2,1)S(1)}, bf16[144,256]{1,0:T(8,128)(2,1)S(1)}, u32[]{:S(2)}, u32[]{:S(2)}) collective-permute-start(bf16[144,256]{1,0:T(8,128)(2,1)S(1)} %get-tuple-element.75), channel_id=1, source_target_pairs={{0,4},{4,0},{8,12},{12,8},{16,20},{20,16},{24,28},{28,24},{1,5},{5... | collective-permute-start | bytes 221192 | tf_op jit(solution)/shard_map/ppermute | solution.py:272
  58.7 1.5 %collective-permute-start.4 = (bf16[144,256]{1,0:T(8,128)(2,1)S(1)}, bf16[144,256]{1,0:T(8,128)(2,1)S(1)}, u32[]{:S(2)}, u32[]{:S(2)}) collective-permute-start(bf16[144,256]{1,0:T(8,128)(2,1)S(1)} %get-tuple-element.75), channel_id=1, source_target_pairs={{0,8},{4,12},{8,0},{12,4},{16,24},{20,28},{24,16},{28,20},{1,9},{5... | collective-permute-start | bytes 221192 | tf_op jit(solution)/shard_map/ppermute | solution.py:272
  60.3 0.7 shard_map.179
  61.1 3.8 %collective-permute-done.4 = bf16[144,256]{1,0:T(8,128)(2,1)S(1)} collective-permute-done((bf16[144,256]{1,0:T(8,128)(2,1)S(1)}, bf16[144,256]{1,0:T(8,128)(2,1)S(1)}, u32[]{:S(2)}, u32[]{:S(2)}) %collective-permute-start.4) | collective-permute-done | bytes 73760 | tf_op jit(solution)/shard_map/ppermute | solution.py:272
  65.9 2.1 %collective-permute-start.6 = (bf16[144,256]{1,0:T(8,128)(2,1)S(1)}, bf16[144,256]{1,0:T(8,128)(2,1)S(1)}, u32[]{:S(2)}, u32[]{:S(2)}) collective-permute-start(bf16[144,256]{1,0:T(8,128)(2,1)S(1)} %fusion), channel_id=1, source_target_pairs={{0,16},{4,20},{8,24},{12,28},{16,0},{20,4},{24,8},{28,12},{1,17},{... | collective-permute-start | bytes 221192 | tf_op jit(solution)/shard_map/ppermute | solution.py:272
  68.4 1.6 %collective-permute-start.8 = (bf16[128,256]{1,0:T(8,128)(2,1)S(1)}, bf16[128,256]{1,0:T(8,128)(2,1)S(1)}, u32[]{:S(2)}, u32[]{:S(2)}) collective-permute-start(bf16[128,256]{1,0:T(8,128)(2,1)S(1)} %get-tuple-element.80), channel_id=1, source_target_pairs={{0,2},{1,3},{2,0},{3,1},{4,6},{5,7},{6,4},{7,5},{8,10},{9,11},{10,... | collective-permute-start | bytes 196616 | tf_op jit(solution)/shard_map/ppermute | solution.py:272
  70.5 1.8 %collective-permute-done.6 = bf16[144,256]{1,0:T(8,128)(2,1)S(1)} collective-permute-done((bf16[144,256]{1,0:T(8,128)(2,1)S(1)}, bf16[144,256]{1,0:T(8,128)(2,1)S(1)}, u32[]{:S(2)}, u32[]{:S(2)}) %collective-permute-start.6) | collective-permute-done | bytes 73760 | tf_op jit(solution)/shard_map/ppermute | solution.py:272
  72.9 1.5 %collective-permute-done.11.refs_1_ = bf16[128,256]{1,0:T(8,128)(2,1)S(1)} collective-permute-done((bf16[128,256]{1,0:T(8,128)(2,1)S(1)}, bf16[128,256]{1,0:T(8,128)(2,1)S(1)}, u32[]{:S(2)}, u32[]{:S(2)}) %collective-permute-start.11) | collective-permute-done | bytes 65568 | tf_op jit(solution)/shard_map/ppermute | solution.py:272
  74.5 0.8 %shard_map.182 = (f32[256,256]{1,0:T(8,128)}, f32[256,256]{1,0:T(8,128)}, f32[1,256]{1,0:T(1,128)}, f32[1,256]{1,0:T(1,128)}) custom-call(s32[1]{0:T(128)} %bitcast.5.rep_ref, bf16[144,256]{1,0:T(8,128)(2,1)S(1)} %reduce-precision_convert_fusion.mine_ref, bf16[144,256]{1,0:T(8,128)(2,1)S(1)} %collective-permute-done.9.other_ref, ...), custom_call_target="tpu_custom_call" | custom-call | tf_op jit(solution)/shard_map/pallas_call | solution.py:261
  (29 shorter events, 3.9 us)
Async XLA Ops:
  0.6 13.7 %all-to-all-start = ((s32[8,1,32]{2,1,0:T(1,128)}), s32[8,1,32]{2,1,0:T(1,128)S(1)}, u32[]{:S(2)}, u32[]{:S(2)}) async-start(s32[8,1,32]{2,1,0:T(1,128)} %bitcast.20), calls=%async_computation | async-start | bytes 8192 | tf_op jit(solution)/shard_map/all_to_all | solution.py:291
  14.9 16.6 %copy-start = (bf16[256]{0:T(256)(128)(2,1)S(1)}, bf16[256]{0:T(256)(128)(2,1)}, u32[]{:S(2)}) copy-start(bf16[256]{0:T(256)(128)(2,1)} %param.27) | copy-start | bytes 1540
  27.9 16.3 %all-to-all-start.2 = ((bf16[8,128,256]{2,1,0:T(8,128)(2,1)}), bf16[8,128,256]{2,1,0:T(8,128)(2,1)S(1)}, u32[]{:S(2)}, u32[]{:S(2)}) async-start(bf16[8,128,256]{2,1,0:T(8,128)(2,1)} %bitcast.19), calls=%async_computation.2 | async-start | bytes 1048576 | tf_op jit(solution)/shard_map/all_to_all | solution.py:291
  46.6 18.3 %all-to-all-start.3 = ((bf16[8,128,256]{2,1,0:T(8,128)(2,1)}), bf16[8,128,256]{2,1,0:T(8,128)(2,1)S(1)}, u32[]{:S(2)}, u32[]{:S(2)}) async-start(bf16[8,128,256]{2,1,0:T(8,128)(2,1)} %bitcast.18), calls=%async_computation.3 | async-start | bytes 1048576 | tf_op jit(solution)/shard_map/all_to_all | solution.py:291
  50.3 2.2 %collective-permute-start = (bf16[144,256]{1,0:T(8,128)(2,1)S(1)}, bf16[144,256]{1,0:T(8,128)(2,1)S(1)}, u32[]{:S(2)}, u32[]{:S(2)}) collective-permute-start(bf16[144,256]{1,0:T(8,128)(2,1)S(1)} %get-tuple-element.78), channel_id=1, source_target_pairs={{0,1},{1,0},{2,3},{3,2},{4,5},{5,4},{6,7},{7,6},{8,9},{9,8},{10,11... | collective-permute-start | bytes 221192 | tf_op jit(solution)/shard_map/ppermute | solution.py:272
  50.4 4.2 %collective-permute-start.2 = (bf16[144,256]{1,0:T(8,128)(2,1)S(1)}, bf16[144,256]{1,0:T(8,128)(2,1)S(1)}, u32[]{:S(2)}, u32[]{:S(2)}) collective-permute-start(bf16[144,256]{1,0:T(8,128)(2,1)S(1)} %get-tuple-element.78), channel_id=1, source_target_pairs={{0,3},{1,2},{2,1},{3,0},{4,7},{5,6},{6,5},{7,4},{8,11},{9,10},{10,... | collective-permute-start | bytes 221192 | tf_op jit(solution)/shard_map/ppermute | solution.py:272
  52.0 4.6 %collective-permute-start.1 = (bf16[144,256]{1,0:T(8,128)(2,1)S(1)}, bf16[144,256]{1,0:T(8,128)(2,1)S(1)}, u32[]{:S(2)}, u32[]{:S(2)}) collective-permute-start(bf16[144,256]{1,0:T(8,128)(2,1)S(1)} %get-tuple-element.77), channel_id=1, source_target_pairs={{0,2},{1,3},{2,0},{3,1},{4,6},{5,7},{6,4},{7,5},{8,10},{9,11},{10,... | collective-permute-start | bytes 221192 | tf_op jit(solution)/shard_map/ppermute | solution.py:272
  56.6 4.4 %collective-permute-start.3 = (bf16[144,256]{1,0:T(8,128)(2,1)S(1)}, bf16[144,256]{1,0:T(8,128)(2,1)S(1)}, u32[]{:S(2)}, u32[]{:S(2)}) collective-permute-start(bf16[144,256]{1,0:T(8,128)(2,1)S(1)} %get-tuple-element.75), channel_id=1, source_target_pairs={{0,4},{4,0},{8,12},{12,8},{16,20},{20,16},{24,28},{28,24},{1,5},{5... | collective-permute-start | bytes 221192 | tf_op jit(solution)/shard_map/ppermute | solution.py:272
  58.7 6.2 %collective-permute-start.4 = (bf16[144,256]{1,0:T(8,128)(2,1)S(1)}, bf16[144,256]{1,0:T(8,128)(2,1)S(1)}, u32[]{:S(2)}, u32[]{:S(2)}) collective-permute-start(bf16[144,256]{1,0:T(8,128)(2,1)S(1)} %get-tuple-element.75), channel_id=1, source_target_pairs={{0,8},{4,12},{8,0},{12,4},{16,24},{20,28},{24,16},{28,20},{1,9},{5... | collective-permute-start | bytes 221192 | tf_op jit(solution)/shard_map/ppermute | solution.py:272
  60.2 5.6 %collective-permute-start.5 = (bf16[144,256]{1,0:T(8,128)(2,1)S(1)}, bf16[144,256]{1,0:T(8,128)(2,1)S(1)}, u32[]{:S(2)}, u32[]{:S(2)}) collective-permute-start(bf16[144,256]{1,0:T(8,128)(2,1)S(1)} %get-tuple-element.75), channel_id=1, source_target_pairs={{0,12},{4,8},{8,4},{12,0},{16,28},{20,24},{24,20},{28,16},{1,13},{... | collective-permute-start | bytes 221192 | tf_op jit(solution)/shard_map/ppermute | solution.py:272
  65.3 3.0 %collective-permute-start.7 = (bf16[256,256]{1,0:T(8,128)(2,1)S(1)}, bf16[256,256]{1,0:T(8,128)(2,1)S(1)}, u32[]{:S(2)}, u32[]{:S(2)}) collective-permute-start(bf16[256,256]{1,0:T(8,128)(2,1)S(1)} %get-tuple-element.66), channel_id=1, source_target_pairs={{0,1},{1,0},{2,3},{3,2},{4,5},{5,4},{6,7},{7,6},{8,9},{9,8},{10,11... | collective-permute-start | bytes 393224 | tf_op jit(solution)/shard_map/ppermute | solution.py:272
  65.9 6.5 %collective-permute-start.6 = (bf16[144,256]{1,0:T(8,128)(2,1)S(1)}, bf16[144,256]{1,0:T(8,128)(2,1)S(1)}, u32[]{:S(2)}, u32[]{:S(2)}) collective-permute-start(bf16[144,256]{1,0:T(8,128)(2,1)S(1)} %fusion), channel_id=1, source_target_pairs={{0,16},{4,20},{8,24},{12,28},{16,0},{20,4},{24,8},{28,12},{1,17},{... | collective-permute-start | bytes 221192 | tf_op jit(solution)/shard_map/ppermute | solution.py:272
  68.4 4.3 %collective-permute-start.8 = (bf16[128,256]{1,0:T(8,128)(2,1)S(1)}, bf16[128,256]{1,0:T(8,128)(2,1)S(1)}, u32[]{:S(2)}, u32[]{:S(2)}) collective-permute-start(bf16[128,256]{1,0:T(8,128)(2,1)S(1)} %get-tuple-element.80), channel_id=1, source_target_pairs={{0,2},{1,3},{2,0},{3,1},{4,6},{5,7},{6,4},{7,5},{8,10},{9,11},{10,... | collective-permute-start | bytes 196616 | tf_op jit(solution)/shard_map/ppermute | solution.py:272
  70.0 2.9 %collective-permute-start.10 = (bf16[256,256]{1,0:T(8,128)(2,1)S(1)}, bf16[256,256]{1,0:T(8,128)(2,1)S(1)}, u32[]{:S(2)}, u32[]{:S(2)}) collective-permute-start(bf16[256,256]{1,0:T(8,128)(2,1)S(1)} %get-tuple-element.69), channel_id=1, source_target_pairs={{0,1},{1,0},{2,3},{3,2},{4,5},{5,4},{6,7},{7,6},{8,9},{9,8},{10,11... | collective-permute-start | bytes 393224 | tf_op jit(solution)/shard_map/ppermute | solution.py:272
  70.0 4.5 %collective-permute-start.11 = (bf16[128,256]{1,0:T(8,128)(2,1)S(1)}, bf16[128,256]{1,0:T(8,128)(2,1)S(1)}, u32[]{:S(2)}, u32[]{:S(2)}) collective-permute-start(bf16[128,256]{1,0:T(8,128)(2,1)S(1)} %get-tuple-element.79), channel_id=1, source_target_pairs={{0,2},{1,3},{2,0},{3,1},{4,6},{5,7},{6,4},{7,5},{8,10},{9,11},{10,... | collective-permute-start | bytes 196616 | tf_op jit(solution)/shard_map/ppermute | solution.py:272
  72.8 1.7 %collective-permute-start.9 = (bf16[144,256]{1,0:T(8,128)(2,1)S(1)}, bf16[144,256]{1,0:T(8,128)(2,1)S(1)}, u32[]{:S(2)}, u32[]{:S(2)}) collective-permute-start(bf16[144,256]{1,0:T(8,128)(2,1)S(1)} %reduce-precision_convert_fusion.mine_ref), channel_id=1, source_target_pairs={{0,1},{1,0},{2,3},{3,2},{4,5},{5,4},{6,7},{7,6},{8,9},{9,8},{10,11... | collective-permute-start | bytes 221192 | tf_op jit(solution)/shard_map/ppermute | solution.py:272
